TPU v7x, 128 devices: a whole 4x4x4 slice. The times are simulated.
128 devices in a mesh: sub: 4 (over y_lo, core), lat: 32 (over y_hi, z, x).
Axes of the slice: x: 4, y: 4 (y_hi: 2, y_lo: 2; y = y_hi * 2 + y_lo), z: 4, core: 2. Of those that a mesh axis runs over, the one named last changes fastest.
Arguments:
- noise: float32 [2, 2, 4, 3, 64, 8, 128], P(None, None, None, None, 'lat', 'sub'), may hold values from -16 to 16
- colours: int32 [2, 64, 8, 128], P(None, 'lat', 'sub'), may hold values from 0 to 15
- probe_rows: int32 [4], replicated, may hold values from 0 to 15
- links: bfloat16 [2, 4, 2, 3, 3, 64, 8, 128], P(None, None, None, None, None, 'lat'), may hold values from -2.5 to 2.5
- clover_even: bfloat16 [2, 2, 6, 6, 64, 8, 128], P(None, None, None, None, 'lat'), may hold values from -0.125 to 2, as said below
- clover_odd_inverse: bfloat16 [2, 2, 6, 6, 64, 8, 128], P(None, None, None, None, 'lat'), may hold values from -0.125 to 2, as said below
Outputs:
- loops: float32 [2, 2, 4, 64, 8, 128], P(None, None, None, 'lat', 'sub')
Inputs may be any that keep to these rules, and one draw needn't show every extreme that they name: `clover_even`: each 6 x 6 block is Hermitian, with a real diagonal of 1.2 to 2.0. `clover_odd_inverse`: each 6 x 6 block is Hermitian, with a real diagonal of 1.2 to 2.0.
All inputs are finite; a program needn't handle non-finite values.
Results may differ from a plain program's by a relative error of at most 0.0003.
Values sent between devices are 32-bit elements; how exact they have to be, the bound alone decides.
No kernel may reach another device: no remote copies, remote signals or barrier semaphores. Data moves between devices by JAX's collectives and lax.ppermute only.
A program may use at most 448 MiB of HBM per device.

v0:
```python
import functools

import jax
import jax.numpy as jnp
from jax import lax
from jax.experimental import pallas as pl
from jax.experimental.pallas import tpu as pltpu
from jax.sharding import PartitionSpec as P

KAPPA = 0.135
F32 = jnp.float32

TURN = (
    ((1, 1), (0, 1)),
    ((1, 0), (0, 2)),
    ((0, 1), (1, 3)),
    ((0, 0), (1, 0)),
)
PAIRS = tuple((i, j) for i in range(6) for j in range(i + 1, 6))


def plus(x, y, power):
    power = power % 4
    if power == 0:
        return (x[0] + y[0], x[1] + y[1])
    if power == 1:
        return (x[0] - y[1], x[1] + y[0])
    if power == 2:
        return (x[0] - y[0], x[1] - y[1])
    return (x[0] + y[1], x[1] - y[0])


def mul(x, y):
    return (x[0] * y[0] - x[1] * y[1], x[0] * y[1] + x[1] * y[0])


def mul_conj(x, y):
    return (x[0] * y[0] + x[1] * y[1], x[0] * y[1] - x[1] * y[0])


def project(spinor, hop_dir, sign):
    if hop_dir == 3:
        extra = 0 if sign > 0 else 2
    else:
        extra = 2 if sign > 0 else 0
    return [
        [
            plus(spinor[s][a], spinor[2 + TURN[hop_dir][s][0]][a], TURN[hop_dir][s][1] + extra)
            for a in range(3)
        ]
        for s in range(2)
    ]


def expand_onto(total, half, hop_dir, sign):
    extra = 0 if sign > 0 else 2
    for s in range(2):
        source, power = TURN[hop_dir][s]
        for a in range(3):
            total[s][a] = half[s][a] if total[s][a] is None else plus(total[s][a], half[s][a], 0)
            if total[2 + s][a] is None:
                zero = jnp.zeros_like(half[source][a][0])
                total[2 + s][a] = plus((zero, zero), half[source][a], power + extra)
            else:
                total[2 + s][a] = plus(total[2 + s][a], half[source][a], power + extra)
    return total


def link_at(links, parity, hop_dir, time):
    return [
        [
            (
                links[parity, hop_dir, 0, i, j, time].astype(F32),
                links[parity, hop_dir, 1, i, j, time].astype(F32),
            )
            for j in range(3)
        ]
        for i in range(3)
    ]


def link_mul(link, half):
    out = []
    for s in range(2):
        row = []
        for i in range(3):
            total = mul(link[i][0], half[s][0])
            for j in (1, 2):
                total = plus(total, mul(link[i][j], half[s][j]), 0)
            row.append(total)
        out.append(row)
    return out


def link_mul_adj(link, half):
    out = []
    for s in range(2):
        row = []
        for i in range(3):
            total = mul_conj(link[0][i], half[s][0])
            for j in (1, 2):
                total = plus(total, mul_conj(link[j][i], half[s][j]), 0)
            row.append(total)
        out.append(row)
    return out


def shift_x(half, time, parity, offset):
    shape = (8, 128)
    depth = lax.broadcasted_iota(jnp.int32, shape, 0)
    lane = lax.broadcasted_iota(jnp.int32, shape, 1)
    row = (depth + lane // 4 + (time + parity)) % 2
    wanted = 1 if offset > 0 else 0
    moved = (lane // 4) * 4 + (lane + offset) % 4
    index = jnp.where(row == wanted, moved, lane)
    pick = lambda v: jnp.take_along_axis(v, index, axis=1, mode="promise_in_bounds")
    return [[(pick(v[0]), pick(v[1])) for v in r] for r in half]


def shift(half, hop_dir, time, parity, offset):
    if hop_dir == 0:
        return shift_x(half, time, parity, offset)
    if hop_dir == 1:
        pick = lambda v: pltpu.roll(v, (-4 * offset) % 128, 1)
    else:
        pick = lambda v: pltpu.roll(v, (-offset) % 8, 0)
    return [[(pick(v[0]), pick(v[1])) for v in r] for r in half]


def load_spinor(ref, *lead):
    return [
        [(ref[(*lead, s * 3 + a)], ref[(*lead, 12 + s * 3 + a)]) for a in range(3)]
        for s in range(4)
    ]


def store_spinor(ref, spinor, *lead):
    for s in range(4):
        for a in range(3):
            ref[(*lead, s * 3 + a)] = spinor[s][a][0]
            ref[(*lead, 12 + s * 3 + a)] = spinor[s][a][1]


def load_half(ref, base=0):
    return [
        [(ref[base + s * 3 + a], ref[base + 6 + s * 3 + a]) for a in range(3)] for s in range(2)
    ]


def store_half(ref, half, base, factor):
    for s in range(2):
        for a in range(3):
            ref[base + s * 3 + a] = half[s][a][0] * factor
            ref[base + 6 + s * 3 + a] = half[s][a][1] * factor


def scaled_half(half, factor):
    return [[(v[0] * factor, v[1] * factor) for v in r] for r in half]


def add_half(x, y):
    return [[plus(x[s][a], y[s][a], 0) for a in range(3)] for s in range(2)]


def hop_at(field, links, time, parity, dagger, high=None, low=None):
    forward, backward = (1, -1) if dagger else (-1, 1)
    total = [[None] * 3 for _ in range(4)]
    own = load_spinor(field, time)
    for hop_dir in range(3):
        half = shift(project(own, hop_dir, forward), hop_dir, time, parity, 1)
        half = link_mul(link_at(links, parity, hop_dir, time), half)
        expand_onto(total, half, hop_dir, forward)
        half = link_mul_adj(
            link_at(links, 1 - parity, hop_dir, time), project(own, hop_dir, backward)
        )
        expand_onto(total, shift(half, hop_dir, time, parity, -1), hop_dir, backward)
    if time == 0:
        half = project(load_spinor(field, 1), 3, forward)
        expand_onto(total, link_mul(link_at(links, parity, 3, 0), half), 3, forward)
        if low is not None:
            expand_onto(total, low, 3, backward)
    else:
        half = project(load_spinor(field, 0), 3, backward)
        expand_onto(total, link_mul_adj(link_at(links, 1 - parity, 3, 0), half), 3, backward)
        if high is not None:
            expand_onto(total, link_mul(link_at(links, parity, 3, 1), high), 3, forward)
    return total


def block_at(clover, chiral, time):
    diagonal = [clover[chiral, 0, i, i, time].astype(F32) for i in range(6)]
    upper = {
        (i, j): (
            clover[chiral, 0, i, j, time].astype(F32),
            clover[chiral, 1, i, j, time].astype(F32),
        )
        for i, j in PAIRS
    }
    return diagonal, upper


def block_packed(ref):
    diagonal = [ref[i] for i in range(6)]
    upper = {pair: (ref[6 + 2 * n], ref[7 + 2 * n]) for n, pair in enumerate(PAIRS)}
    return diagonal, upper


def block_mul(block, half):
    diagonal, upper = block
    flat = half[0] + half[1]
    out = [(diagonal[i] * flat[i][0], diagonal[i] * flat[i][1]) for i in range(6)]
    for i, j in PAIRS:
        out[i] = plus(out[i], mul(upper[i, j], flat[j]), 0)
        out[j] = plus(out[j], mul_conj(upper[i, j], flat[i]), 0)
    return [out[:3], out[3:]]


def clover_at(clover, spinor, time):
    return block_mul(block_at(clover, 0, time), spinor[:2]) + block_mul(
        block_at(clover, 1, time), spinor[2:]
    )


def edge_signs():
    position = lax.axis_index("lat")
    last = lax.axis_size("lat") - 1
    at_first = jnp.where(position == 0, -1.0, 1.0).astype(F32)
    at_last = jnp.where(position == last, -1.0, 1.0).astype(F32)
    return at_first, at_last


def begin_schur(vector, links, odd_inverse, dagger, partial, high, low):
    forward, backward = (1, -1) if dagger else (-1, 1)
    at_first, at_last = edge_signs()
    for time in range(2):
        store_spinor(
            partial, clover_at(odd_inverse, hop_at(vector, links, time, 1, dagger), time), time
        )
    store_half(high, project(load_spinor(vector, 0), 3, forward), 0, at_first)
    store_half(high, project(load_spinor(partial, 0), 3, forward), 12, at_first)
    half = link_mul_adj(link_at(links, 0, 3, 1), project(load_spinor(vector, 1), 3, backward))
    store_half(low, half, 0, at_last)
    half = link_mul_adj(link_at(links, 1, 3, 1), project(load_spinor(partial, 1), 3, backward))
    store_half(low, half, 12, at_last)


def end_schur(
    vector, partial, sent_high, sent_low, got_high, got_low, around_high, around_low,
    links, even, odd_inverse, dagger, odd_field, result,
):
    forward, backward = (1, -1) if dagger else (-1, 1)
    at_first, at_last = edge_signs()
    for time in range(2):
        if time == 0:
            half, sign = load_half(got_low), backward
        else:
            half = link_mul(link_at(links, 1, 3, 1), load_half(got_high))
            sign = forward
        own = load_spinor(partial, time)
        top = block_mul(block_at(odd_inverse, 0, time), half)
        bottom = block_mul(block_at(odd_inverse, 1, time), half)
        whole = [[plus(own[s][a], top[s][a], 0) for a in range(3)] for s in range(2)] + [
            [plus(own[2 + s][a], bottom[s][a], 0 if sign > 0 else 2) for a in range(3)]
            for s in range(2)
        ]
        store_spinor(odd_field, whole, time)
    back = block_mul(block_packed(around_high), load_half(sent_low))
    high = add_half(load_half(got_high, 12), scaled_half(back, at_last))
    back = block_mul(block_packed(around_low), load_half(sent_high))
    low = add_half(load_half(got_low, 12), scaled_half(back, at_first))
    for time in range(2):
        returned = hop_at(odd_field, links, time, 0, dagger, high, low)
        direct = clover_at(even, load_spinor(vector, time), time)
        factor = KAPPA * KAPPA
        store_spinor(
            result,
            [
                [
                    (
                        direct[s][a][0] - factor * returned[s][a][0],
                        direct[s][a][1] - factor * returned[s][a][1],
                    )
                    for a in range(3)
                ]
                for s in range(4)
            ],
            time,
        )


def around_kernel(links, odd_inverse, high, low):
    blocks = []
    for time in range(2):
        diagonal0, upper0 = block_at(odd_inverse, 0, time)
        diagonal1, upper1 = block_at(odd_inverse, 1, time)
        blocks.append(
            (
                [x - y for x, y in zip(diagonal0, diagonal1)],
                {pair: plus(upper0[pair], upper1[pair], 2) for pair in PAIRS},
            )
        )
    diagonal, upper = blocks[0]
    for i in range(6):
        high[i] = diagonal[i]
    for n, pair in enumerate(PAIRS):
        high[6 + 2 * n], high[7 + 2 * n] = upper[pair]
    diagonal, upper = blocks[1]

    def entry(i, j):
        if i == j:
            return (diagonal[i], jnp.zeros_like(diagonal[i]))
        if i < j:
            return upper[i, j]
        value = upper[j, i]
        return (value[0], -value[1])

    link = link_at(links, 1, 3, 1)
    for s0, s1 in ((0, 0), (0, 1), (1, 1)):
        right = [[None] * 3 for _ in range(3)]
        for a in range(3):
            for b in range(3):
                total = mul(entry(s0 * 3 + a, s1 * 3), link[0][b])
                for c in (1, 2):
                    total = plus(total, mul(entry(s0 * 3 + a, s1 * 3 + c), link[c][b]), 0)
                right[a][b] = total
        for a in range(3):
            for b in range(3):
                if s0 == s1 and a > b:
                    continue
                total = mul_conj(link[0][a], right[0][b])
                for c in (1, 2):
                    total = plus(total, mul_conj(link[c][a], right[c][b]), 0)
                i, j = s0 * 3 + a, s1 * 3 + b
                if i == j:
                    low[i] = total[0]
                else:
                    n = PAIRS.index((i, j))
                    low[6 + 2 * n], low[7 + 2 * n] = total


def vector_index():
    upper = lax.axis_index("lat") // (lax.axis_size("lat") // 2)
    return jnp.bitwise_xor(lax.axis_index("sub"), 2 * upper)


def start_kernel(probe_rows, gathered, links, odd_inverse, probes, turned, rhs, high, low, raw):
    for q in range(4):
        raw[:, :, 2 * q : 2 * q + 2, :] = gathered[q]
    probe_row = probe_rows[vector_index()]
    at_first, at_last = edge_signs()
    for parity in range(2):
        for time in range(2):
            masked = jnp.bitwise_and(raw[48 + parity, time].astype(jnp.int32), probe_row)
            masked = jnp.bitwise_xor(masked, jnp.right_shift(masked, 2))
            masked = jnp.bitwise_xor(masked, jnp.right_shift(masked, 1))
            sign = (1 - 2 * jnp.bitwise_and(masked, 1)).astype(F32)
            for n in range(24):
                probes[parity, time, n] = raw[parity * 24 + n, time] * sign
    for time in range(2):
        store_spinor(turned, clover_at(odd_inverse, load_spinor(probes, 1, time), time), time)
    for time in range(2):
        total = hop_at(turned, links, time, 0, False)
        own = load_spinor(probes, 0, time)
        store_spinor(
            rhs,
            [
                [
                    (own[s][a][0] + KAPPA * total[s][a][0], own[s][a][1] + KAPPA * total[s][a][1])
                    for a in range(3)
                ]
                for s in range(4)
            ],
            time,
        )
    store_half(high, project(load_spinor(turned, 0), 3, -1), 0, at_first)
    half = link_mul_adj(link_at(links, 1, 3, 1), project(load_spinor(turned, 1), 3, 1))
    store_half(low, half, 0, at_last)


def rhs_kernel(partial, got_high, got_low, links, odd_inverse, rhs, odd, high, low):
    half = scaled_half(load_half(got_low), KAPPA)
    store_spinor(rhs, expand_onto(load_spinor(partial, 0), half, 3, 1), 0)
    half = scaled_half(link_mul(link_at(links, 0, 3, 1), load_half(got_high)), KAPPA)
    store_spinor(rhs, expand_onto(load_spinor(partial, 1), half, 3, -1), 1)
    begin_schur(rhs, links, odd_inverse, True, odd, high, low)


def step_kernel(
    dagger,
    vector, partial, sent_high, sent_low, got_high, got_low, around_high, around_low,
    links, even, odd_inverse,
    result, odd_field, odd, high, low,
):
    end_schur(
        vector, partial, sent_high, sent_low, got_high, got_low, around_high, around_low,
        links, even, odd_inverse, dagger, odd_field, result,
    )
    begin_schur(result, links, odd_inverse, not dagger, odd, high, low)


def column_sum(left, right):
    total = None
    for time in range(2):
        for n in range(24):
            term = left(time, n) * right(time, n)
            total = term if total is None else total + term
    return jnp.sum(total, axis=0, keepdims=True)


def last_kernel(
    vector, partial, sent_high, sent_low, got_high, got_low, around_high, around_low,
    links, even, odd_inverse, first, image,
    odd_field, sums, result,
):
    end_schur(
        vector, partial, sent_high, sent_low, got_high, got_low, around_high, around_low,
        links, even, odd_inverse, False, odd_field, result,
    )
    first_at = lambda time, n: first[time, n]
    image_at = lambda time, n: image[time, n]
    vector_at = lambda time, n: vector[time, n]
    norm = column_sum(first_at, first_at)
    image_norm = column_sum(image_at, image_at)
    norm_all = jnp.sum(norm, axis=1, keepdims=True)
    about = jnp.sum(image_norm, axis=1, keepdims=True) / jnp.where(norm_all > 0, norm_all, 1.0)
    about = jnp.broadcast_to(about, (1, 128))
    about_full = jnp.broadcast_to(about, (8, 128))
    rest_at = lambda time, n: vector[time, n] - about_full * first[time, n]
    image_rest_at = lambda time, n: result[time, n] - about_full * image[time, n]
    rows = [
        norm,
        column_sum(first_at, vector_at),
        about,
        column_sum(rest_at, rest_at),
        column_sum(rest_at, first_at),
        column_sum(image_rest_at, image_rest_at),
        column_sum(image_rest_at, image_at),
        image_norm,
    ]
    block = jnp.concatenate(rows, axis=0)
    for n in range(sums.shape[0]):
        sums[n] = block


def trace_kernel(sums, probes, turned, first, first_odd, second, second_odd, out):
    whole = lambda x: jnp.sum(jnp.sum(x, axis=0, keepdims=True), axis=1, keepdims=True)
    row = [sums[:, n, :] for n in range(8)]
    norm, crossed, about, rest, rest_first, image_rest, image_cross, image_norm = row
    norm_all = whole(norm)
    inverse = whole(crossed) / norm_all
    alpha = norm_all / whole(crossed)
    off = about - inverse
    norm_next = alpha * alpha * whole(rest + 2.0 * off * rest_first + off * off * norm)
    beta = norm_next / norm_all
    off = about - (1.0 + beta) / alpha
    curved = alpha * alpha * whole(
        image_rest + 2.0 * off * image_cross + off * off * image_norm
    )
    alpha_next = norm_next / curved
    alpha = jnp.broadcast_to(alpha, (8, 128))
    alpha_next = jnp.broadcast_to(alpha_next, (8, 128))
    beta = jnp.broadcast_to(beta, (8, 128))
    for time in range(2):
        for parity in range(2):
            values = []
            for n in range(24):
                if parity == 0:
                    base, other = first[time, n], second[time, n]
                else:
                    base, other = first_odd[time, n], second_odd[time, n]
                search = (base - alpha * other) + beta * base
                value = alpha * base + alpha_next * search
                if parity == 1:
                    value = turned[time, n] + KAPPA * value
                values.append(value)
            right = [
                [(values[s * 3 + a], values[12 + s * 3 + a]) for a in range(3)] for s in range(4)
            ]
            left = load_spinor(probes, parity, time)

            def dot(s, r):
                total = mul_conj(left[s][0], right[r][0])
                for a in (1, 2):
                    total = plus(total, mul_conj(left[s][a], right[r][a]), 0)
                return total

            up = [[dot(s, 2 + r) for r in range(2)] for s in range(2)]
            down = [[dot(2 + s, r) for r in range(2)] for s in range(2)]
            x_sum = plus(plus(down[0][1], down[1][0], 0), plus(up[0][1], up[1][0], 0), 2)
            y_sum = plus(plus(down[0][1], down[1][0], 2), plus(up[0][1], up[1][0], 2), 2)
            z_sum = plus(plus(down[0][0], down[1][1], 2), plus(up[0][0], up[1][1], 2), 2)
            t_sum = plus(plus(down[0][0], down[1][1], 0), plus(up[0][0], up[1][1], 0), 0)
            columns = ((-x_sum[1], x_sum[0]), y_sum, (-z_sum[1], z_sum[0]), t_sum)
            for hop_dir in range(4):
                for part in range(2):
                    value = columns[hop_dir][part]
                    for q in range(4):
                        out[q, parity * 8 + part * 4 + hop_dir, time] = value[2 * q : 2 * q + 2]


VMEM = pl.BlockSpec(memory_space=pltpu.VMEM)
SMEM = pl.BlockSpec(memory_space=pltpu.SMEM)


def call(kernel, name, shapes, scalars, arrays, scratch=()):
    return pl.pallas_call(
        kernel,
        out_shape=tuple(jax.ShapeDtypeStruct(s, F32) for s in shapes),
        in_specs=[SMEM] * len(scalars) + [VMEM] * len(arrays),
        out_specs=tuple(VMEM for _ in shapes),
        scratch_shapes=[pltpu.VMEM(s, F32) for s in scratch],
        compiler_params=pltpu.CompilerParams(vmem_limit_bytes=24 * 1024 * 1024),
        name=name,
    )(*scalars, *arrays)


FIELD = (2, 24, 8, 128)
EDGE = (24, 8, 128)


def to_neighbour(array, by):
    length, subs = lax.axis_size("lat"), lax.axis_size("sub")
    flip = lambda place: 2 * (place // (length // 2))
    pairs = []
    for place in range(length):
        target = (place + by) % length
        for vector in range(subs):
            pairs.append(
                (
                    (vector ^ flip(place)) * length + place,
                    (vector ^ flip(target)) * length + target,
                )
            )
    return lax.ppermute(array, ("sub", "lat"), pairs)


def exchange(high, low):
    return to_neighbour(high, -1), to_neighbour(low, 1)


def shards(noise, colours, probe_rows, links, clover_even, clover_odd_inverse):
    own = jnp.concatenate(
        [noise.reshape((48,) + noise.shape[4:]), colours.astype(F32)], axis=0
    )
    gathered = lax.all_gather(own, "sub")
    around = call(
        around_kernel, "around", ((36, 8, 128),) * 2, (), (links, clover_odd_inverse)
    )
    around = exchange(*around)
    probes, turned, partial, high, low = call(
        start_kernel,
        "start",
        ((2,) + FIELD, FIELD, FIELD, (12, 8, 128), (12, 8, 128)),
        (probe_rows,),
        (gathered, links, clover_odd_inverse),
        ((50, 2, 8, 128),),
    )
    got = exchange(high, low)
    vector, odd, high, low = call(
        rhs_kernel, "rhs", (FIELD, FIELD, EDGE, EDGE), (), (partial, *got, links, clover_odd_inverse)
    )
    kept = []
    for step in range(3):
        got = exchange(high, low)
        result, odd_field, odd, high, low = call(
            functools.partial(step_kernel, step % 2 == 0),
            "step%d" % step,
            (FIELD, FIELD, FIELD, EDGE, EDGE),
            (),
            (vector, odd, high, low, *got, *around, links, clover_even, clover_odd_inverse),
        )
        kept.append((result, odd_field))
        vector = result
    first, image, second = kept[0][0], kept[1][0], kept[2][0]
    first_odd = kept[1][1]
    got = exchange(high, low)
    second_odd, sums = call(
        last_kernel,
        "last",
        (FIELD, (lax.axis_size("lat"), 8, 128)),
        (),
        (
            second, odd, high, low, *got, *around, links, clover_even, clover_odd_inverse,
            first, image,
        ),
        (FIELD,),
    )
    return probes, turned, first, first_odd, second, second_odd, sums


def gather_sums(sums):
    length, subs = lax.axis_size("lat"), lax.axis_size("sub")
    groups = [
        [(vector ^ (2 * (place // (length // 2)))) * length + place for place in range(length)]
        for vector in range(subs)
    ]
    return lax.all_to_all(
        sums, ("sub", "lat"), 0, 0, tiled=True, axis_index_groups=groups
    )


def whole(noise, colours, probe_rows, links, clover_even, clover_odd_inverse):
    probes, turned, first, first_odd, second, second_odd, sums = shards(
        noise, colours, probe_rows, links, clover_even, clover_odd_inverse
    )
    sums = gather_sums(sums)
    (traces,) = call(
        trace_kernel,
        "trace",
        ((4, 16, 2, 2, 128),),
        (),
        (sums, probes, turned, first, first_odd, second, second_odd),
    )
    traces = lax.all_to_all(traces, "sub", 0, 0, tiled=True)
    return jnp.sum(traces, axis=0).reshape(2, 2, 4, 2, 2, 128)


def solution(mesh):
    placed = (
        P(None, None, None, None, "lat", "sub", None),
        P(None, "lat", "sub", None),
        P(),
        P(None, None, None, None, None, "lat", None, None),
        P(None, None, None, None, "lat", None, None),
        P(None, None, None, None, "lat", None, None),
    )
    return jax.shard_map(
        whole,
        mesh=mesh,
        in_specs=placed,
        out_specs=P(None, None, None, "lat", "sub", None),
        check_vma=False,
    )
```

profile of v0, /device:TPU:1, one launch (start us, length us, event | category | flops | bytes accessed | tf_op | source)
XLA Modules:
  0.0 103.6 jit_solution(6372259017102838132)
XLA Ops:
  0.0 0.0 copy-start
  0.0 0.8 convert_element_type.3
  0.8 0.9 pad_maximum_fusion
  1.7 8.0 %all-gather = f32[200,2,2,128]{3,2,1,0:T(2,128)S(1)} all-gather(f32[50,2,2,128]{3,2,1,0:T(2,128)S(1)} %pad_maximum_fusion), channel_id=2, replica_groups=mesh['sub'=4,'lat'=32] {'sub'}, dimensions={0}, use_global_device_ids=true | all-gather | bytes 512000 | tf_op jit(solution)/shard_map/all_gather | solution.py:545
  9.7 0.0 copy-start.4
  9.7 0.0 copy-done
  9.7 0.7 copy-done.4
  10.3 0.0 copy-start.1
  10.3 1.1 %copy-done.1 = bf16[2,2,6,6,2,8,128]{6,5,4,3,2,1,0:T(8,128)(2,1)S(1)} copy-done((bf16[2,2,6,6,2,8,128]{6,5,4,3,2,1,0:T(8,128)(2,1)S(1)}, bf16[2,2,6,6,2,8,128]{6,5,4,3,2,1,0:T(8,128)(2,1)}, u32[]{:S(2)}) %copy-start.1) | copy-done | bytes 589848
  11.4 1.2 %start.1 = (f32[2,2,24,8,128]{4,3,2,1,0:T(8,128)S(1)}, f32[2,24,8,128]{3,2,1,0:T(8,128)S(1)}, f32[2,24,8,128]{3,2,1,0:T(8,128)S(1)}, f32[12,8,128]{2,1,0:T(8,128)S(1)}, f32[12,8,128]{2,1,0:T(8,128)S(1)}) custom-call(s32[4]{0:T(128)S(1)} %copy-done.4, f32[4,50,2,2,128]{4,3,2,1,0:T(2,128)S(1)} %bitcast.3, bf16[2,4,2,3,3,2,8,128]{7,6,5,4,3,2,1,0:T(8,128)(2,1)S(1)} %copy-done, ...), custom_call_target="tpu_custom_call" | custom-call | tf_op jit(solution)/shard_map/start/pallas_call | solution.py:506
  12.6 8.0 %collective-permute-start = (f32[12,8,128]{2,1,0:T(8,128)S(1)}, f32[12,8,128]{2,1,0:T(8,128)S(1)}, u32[]{:S(2)}, u32[]{:S(2)}) collective-permute-start(f32[12,8,128]{2,1,0:T(8,128)S(1)} %get-tuple-element.32), channel_id=1, source_target_pairs={{0,95},{32,127},{64,31},{96,63},{1,0},{33,32},{65,64},{97,96},{2,1... | collective-permute-start | bytes 147464 | tf_op jit(solution)/shard_map/ppermute | solution.py:534
  20.7 0.0 collective-permute-start.1
  20.7 0.2 around.1
  20.9 7.0 %collective-permute-start.4 = (f32[36,8,128]{2,1,0:T(8,128)S(1)}, f32[36,8,128]{2,1,0:T(8,128)S(1)}, u32[]{:S(2)}, u32[]{:S(2)}) collective-permute-start(f32[36,8,128]{2,1,0:T(8,128)S(1)} %get-tuple-element.38), channel_id=1, source_target_pairs={{0,95},{32,127},{64,31},{96,63},{1,0},{33,32},{65,64},{97,96},{2,1... | collective-permute-start | bytes 442376 | tf_op jit(solution)/shard_map/ppermute | solution.py:534
  27.8 0.0 collective-permute-start.5
  27.8 0.0 collective-permute-done.got_high
  27.8 1.2 %collective-permute-done.1.got_low = f32[12,8,128]{2,1,0:T(8,128)S(1)} collective-permute-done((f32[12,8,128]{2,1,0:T(8,128)S(1)}, f32[12,8,128]{2,1,0:T(8,128)S(1)}, u32[]{:S(2)}, u32[]{:S(2)}) %collective-permute-start.1) | collective-permute-done | bytes 49184 | tf_op jit(solution)/shard_map/ppermute | solution.py:534
  29.1 0.0 copy-start.2
  29.1 0.0 copy-start.3
  29.1 0.7 rhs.1
  29.7 5.7 %collective-permute-start.2 = (f32[24,8,128]{2,1,0:T(8,128)S(1)}, f32[24,8,128]{2,1,0:T(8,128)S(1)}, u32[]{:S(2)}, u32[]{:S(2)}) collective-permute-start(f32[24,8,128]{2,1,0:T(8,128)S(1)} %get-tuple-element.36.sent_high), channel_id=1, source_target_pairs={{0,95},{32,127},{64,31},{96,63},{1,0},{33,32},{65,64},{97,96},{2,1... | collective-permute-start | bytes 294920 | tf_op jit(solution)/shard_map/ppermute | solution.py:534
  35.5 0.0 collective-permute-start.3
  35.5 0.0 collective-permute-done.4.around_high
  35.5 2.1 %collective-permute-done.5.around_low = f32[36,8,128]{2,1,0:T(8,128)S(1)} collective-permute-done((f32[36,8,128]{2,1,0:T(8,128)S(1)}, f32[36,8,128]{2,1,0:T(8,128)S(1)}, u32[]{:S(2)}, u32[]{:S(2)}) %collective-permute-start.5) | collective-permute-done | bytes 147488 | tf_op jit(solution)/shard_map/ppermute | solution.py:534
  37.6 0.0 collective-permute-done.2.got_high
  37.6 6.8 %collective-permute-done.3.got_low = f32[24,8,128]{2,1,0:T(8,128)S(1)} collective-permute-done((f32[24,8,128]{2,1,0:T(8,128)S(1)}, f32[24,8,128]{2,1,0:T(8,128)S(1)}, u32[]{:S(2)}, u32[]{:S(2)}) %collective-permute-start.3) | collective-permute-done | bytes 98336 | tf_op jit(solution)/shard_map/ppermute | solution.py:534
  44.4 0.0 copy-done.2
  44.4 0.0 copy-done.3
  44.4 1.9 %step0.1 = (f32[2,24,8,128]{3,2,1,0:T(8,128)S(1)}, f32[2,24,8,128]{3,2,1,0:T(8,128)}, f32[2,24,8,128]{3,2,1,0:T(8,128)S(1)}, f32[24,8,128]{2,1,0:T(8,128)S(1)}, f32[24,8,128]{2,1,0:T(8,128)S(1)}) custom-call(f32[2,24,8,128]{3,2,1,0:T(8,128)S(1)} %get-tuple-element.34.vector, f32[2,24,8,128]{3,2,1,0:T(8,128)S(1)} %get-tuple-element.35.partial, ...), custom_call_target="tpu_custom_call" | custom-call | tf_op jit(solution)/shard_map/step0/pallas_call | solution.py:506
  46.3 0.0 collective-permute-start.6
  46.3 1.5 %collective-permute-start.7 = (f32[24,8,128]{2,1,0:T(8,128)S(1)}, f32[24,8,128]{2,1,0:T(8,128)S(1)}, u32[]{:S(2)}, u32[]{:S(2)}) collective-permute-start(f32[24,8,128]{2,1,0:T(8,128)S(1)} %get-tuple-element.43.sent_low), channel_id=1, source_target_pairs={{0,1},{32,33},{64,65},{96,97},{1,2},{33,34},{65,66},{97,98},{2,3},... | collective-permute-start | bytes 294920 | tf_op jit(solution)/shard_map/ppermute | solution.py:534
  47.8 2.0 %collective-permute-done.6.got_high = f32[24,8,128]{2,1,0:T(8,128)S(1)} collective-permute-done((f32[24,8,128]{2,1,0:T(8,128)S(1)}, f32[24,8,128]{2,1,0:T(8,128)S(1)}, u32[]{:S(2)}, u32[]{:S(2)}) %collective-permute-start.6) | collective-permute-done | bytes 98336 | tf_op jit(solution)/shard_map/ppermute | solution.py:534
  49.8 5.4 %collective-permute-done.7.got_low = f32[24,8,128]{2,1,0:T(8,128)S(1)} collective-permute-done((f32[24,8,128]{2,1,0:T(8,128)S(1)}, f32[24,8,128]{2,1,0:T(8,128)S(1)}, u32[]{:S(2)}, u32[]{:S(2)}) %collective-permute-start.7) | collective-permute-done | bytes 98336 | tf_op jit(solution)/shard_map/ppermute | solution.py:534
  55.2 1.5 %step1.1 = (f32[2,24,8,128]{3,2,1,0:T(8,128)S(1)}, f32[2,24,8,128]{3,2,1,0:T(8,128)S(1)}, f32[2,24,8,128]{3,2,1,0:T(8,128)S(1)}, f32[24,8,128]{2,1,0:T(8,128)S(1)}, f32[24,8,128]{2,1,0:T(8,128)S(1)}) custom-call(f32[2,24,8,128]{3,2,1,0:T(8,128)S(1)} %get-tuple-element.40.vector.first, f32[2,24,8,128]{3,2,1,0:T(8,128)S(1)} %get-tuple-element.41.partial, ...), custom_call_target="tpu_custom_call" | custom-call | tf_op jit(solution)/shard_map/step1/pallas_call | solution.py:506
  56.7 0.1 collective-permute-start.8
  56.8 1.5 %collective-permute-start.9 = (f32[24,8,128]{2,1,0:T(8,128)S(1)}, f32[24,8,128]{2,1,0:T(8,128)S(1)}, u32[]{:S(2)}, u32[]{:S(2)}) collective-permute-start(f32[24,8,128]{2,1,0:T(8,128)S(1)} %get-tuple-element.47.sent_low), channel_id=1, source_target_pairs={{0,1},{32,33},{64,65},{96,97},{1,2},{33,34},{65,66},{97,98},{2,3},... | collective-permute-start | bytes 294920 | tf_op jit(solution)/shard_map/ppermute | solution.py:534
  58.2 2.0 %collective-permute-done.8.got_high = f32[24,8,128]{2,1,0:T(8,128)S(1)} collective-permute-done((f32[24,8,128]{2,1,0:T(8,128)S(1)}, f32[24,8,128]{2,1,0:T(8,128)S(1)}, u32[]{:S(2)}, u32[]{:S(2)}) %collective-permute-start.8) | collective-permute-done | bytes 98336 | tf_op jit(solution)/shard_map/ppermute | solution.py:534
  60.2 5.5 %collective-permute-done.9.got_low = f32[24,8,128]{2,1,0:T(8,128)S(1)} collective-permute-done((f32[24,8,128]{2,1,0:T(8,128)S(1)}, f32[24,8,128]{2,1,0:T(8,128)S(1)}, u32[]{:S(2)}, u32[]{:S(2)}) %collective-permute-start.9) | collective-permute-done | bytes 98336 | tf_op jit(solution)/shard_map/ppermute | solution.py:534
  65.7 1.9 %step2.1 = (f32[2,24,8,128]{3,2,1,0:T(8,128)S(1)}, f32[2,24,8,128]{3,2,1,0:T(8,128)}, f32[2,24,8,128]{3,2,1,0:T(8,128)S(1)}, f32[24,8,128]{2,1,0:T(8,128)S(1)}, f32[24,8,128]{2,1,0:T(8,128)S(1)}) custom-call(f32[2,24,8,128]{3,2,1,0:T(8,128)S(1)} %get-tuple-element.44.vector.image, f32[2,24,8,128]{3,2,1,0:T(8,128)S(1)} %get-tuple-element.45.partial, ...), custom_call_target="tpu_custom_call" | custom-call | tf_op jit(solution)/shard_map/step2/pallas_call | solution.py:506
  67.7 0.0 collective-permute-start.10
  67.7 1.5 %collective-permute-start.11 = (f32[24,8,128]{2,1,0:T(8,128)S(1)}, f32[24,8,128]{2,1,0:T(8,128)S(1)}, u32[]{:S(2)}, u32[]{:S(2)}) collective-permute-start(f32[24,8,128]{2,1,0:T(8,128)S(1)} %get-tuple-element.51.sent_low), channel_id=1, source_target_pairs={{0,1},{32,33},{64,65},{96,97},{1,2},{33,34},{65,66},{97,98},{2,3},... | collective-permute-start | bytes 294920 | tf_op jit(solution)/shard_map/ppermute | solution.py:534
  69.1 2.0 %collective-permute-done.10.got_high = f32[24,8,128]{2,1,0:T(8,128)S(1)} collective-permute-done((f32[24,8,128]{2,1,0:T(8,128)S(1)}, f32[24,8,128]{2,1,0:T(8,128)S(1)}, u32[]{:S(2)}, u32[]{:S(2)}) %collective-permute-start.10) | collective-permute-done | bytes 98336 | tf_op jit(solution)/shard_map/ppermute | solution.py:534
  71.2 5.4 %collective-permute-done.11.got_low = f32[24,8,128]{2,1,0:T(8,128)S(1)} collective-permute-done((f32[24,8,128]{2,1,0:T(8,128)S(1)}, f32[24,8,128]{2,1,0:T(8,128)S(1)}, u32[]{:S(2)}, u32[]{:S(2)}) %collective-permute-start.11) | collective-permute-done | bytes 98336 | tf_op jit(solution)/shard_map/ppermute | solution.py:534
  76.6 1.0 last.1
  77.6 11.5 %all_to_all.10.sums = f32[32,8,128]{2,1,0:T(8,128)S(1)} all-to-all(f32[32,8,128]{2,1,0:T(8,128)S(1)} %get-tuple-element.52), channel_id=1, replica_groups={{0,1,2,3,4,5,6,7,8,9,10,11,12,13,14,15,80,81,82,83,84,85,86,87,88,89,90..., dimensions={0} | all-to-all | bytes 262144 | tf_op jit(solution)/shard_map/all_to_all | solution.py:597
  89.1 0.5 trace.1
  89.6 13.3 %all_to_all.11 = f32[4,16,2,2,128]{4,3,2,1,0:T(2,128)S(1)} all-to-all(f32[4,16,2,2,128]{4,3,2,1,0:T(2,128)S(1)} %trace.1), channel_id=1, replica_groups=mesh['sub'=4,'lat'=32] {'sub'}, dimensions={0} | all-to-all | bytes 262144 | tf_op jit(solution)/shard_map/all_to_all | solution.py:614
  102.9 0.7 reduce_sum.9
Async XLA Ops:
  0.0 9.7 %copy-start = (bf16[2,4,2,3,3,2,8,128]{7,6,5,4,3,2,1,0:T(8,128)(2,1)S(1)}, bf16[2,4,2,3,3,2,8,128]{7,6,5,4,3,2,1,0:T(8,128)(2,1)}, u32[]{:S(2)}) copy-start(bf16[2,4,2,3,3,2,8,128]{7,6,5,4,3,2,1,0:T(8,128)(2,1)} %links.13) | copy-start | bytes 1769476
  9.7 0.7 copy-start.4
  10.3 1.1 %copy-start.1 = (bf16[2,2,6,6,2,8,128]{6,5,4,3,2,1,0:T(8,128)(2,1)S(1)}, bf16[2,2,6,6,2,8,128]{6,5,4,3,2,1,0:T(8,128)(2,1)}, u32[]{:S(2)}) copy-start(bf16[2,2,6,6,2,8,128]{6,5,4,3,2,1,0:T(8,128)(2,1)} %odd_inverse.13) | copy-start | bytes 1769476
  12.6 15.2 %collective-permute-start = (f32[12,8,128]{2,1,0:T(8,128)S(1)}, f32[12,8,128]{2,1,0:T(8,128)S(1)}, u32[]{:S(2)}, u32[]{:S(2)}) collective-permute-start(f32[12,8,128]{2,1,0:T(8,128)S(1)} %get-tuple-element.32), channel_id=1, source_target_pairs={{0,95},{32,127},{64,31},{96,63},{1,0},{33,32},{65,64},{97,96},{2,1... | collective-permute-start | bytes 147464 | tf_op jit(solution)/shard_map/ppermute | solution.py:534
  20.7 8.4 %collective-permute-start.1 = (f32[12,8,128]{2,1,0:T(8,128)S(1)}, f32[12,8,128]{2,1,0:T(8,128)S(1)}, u32[]{:S(2)}, u32[]{:S(2)}) collective-permute-start(f32[12,8,128]{2,1,0:T(8,128)S(1)} %get-tuple-element.33), channel_id=1, source_target_pairs={{0,1},{32,33},{64,65},{96,97},{1,2},{33,34},{65,66},{97,98},{2,3},... | collective-permute-start | bytes 147464 | tf_op jit(solution)/shard_map/ppermute | solution.py:534
  20.9 14.6 %collective-permute-start.4 = (f32[36,8,128]{2,1,0:T(8,128)S(1)}, f32[36,8,128]{2,1,0:T(8,128)S(1)}, u32[]{:S(2)}, u32[]{:S(2)}) collective-permute-start(f32[36,8,128]{2,1,0:T(8,128)S(1)} %get-tuple-element.38), channel_id=1, source_target_pairs={{0,95},{32,127},{64,31},{96,63},{1,0},{33,32},{65,64},{97,96},{2,1... | collective-permute-start | bytes 442376 | tf_op jit(solution)/shard_map/ppermute | solution.py:534
  27.8 9.8 %collective-permute-start.5 = (f32[36,8,128]{2,1,0:T(8,128)S(1)}, f32[36,8,128]{2,1,0:T(8,128)S(1)}, u32[]{:S(2)}, u32[]{:S(2)}) collective-permute-start(f32[36,8,128]{2,1,0:T(8,128)S(1)} %get-tuple-element.39), channel_id=1, source_target_pairs={{0,1},{32,33},{64,65},{96,97},{1,2},{33,34},{65,66},{97,98},{2,3},... | collective-permute-start | bytes 442376 | tf_op jit(solution)/shard_map/ppermute | solution.py:534
  29.1 15.3 %copy-start.2 = (bf16[2,2,6,6,2,8,128]{6,5,4,3,2,1,0:T(8,128)(2,1)S(1)}, bf16[2,2,6,6,2,8,128]{6,5,4,3,2,1,0:T(8,128)(2,1)}, u32[]{:S(2)}) copy-start(bf16[2,2,6,6,2,8,128]{6,5,4,3,2,1,0:T(8,128)(2,1)} %odd_inverse.13) | copy-start | bytes 1769476
  29.1 15.3 %copy-start.3 = (bf16[2,2,6,6,2,8,128]{6,5,4,3,2,1,0:T(8,128)(2,1)S(1)}, bf16[2,2,6,6,2,8,128]{6,5,4,3,2,1,0:T(8,128)(2,1)}, u32[]{:S(2)}) copy-start(bf16[2,2,6,6,2,8,128]{6,5,4,3,2,1,0:T(8,128)(2,1)} %even.7) | copy-start | bytes 1769476
  29.7 7.9 %collective-permute-start.2 = (f32[24,8,128]{2,1,0:T(8,128)S(1)}, f32[24,8,128]{2,1,0:T(8,128)S(1)}, u32[]{:S(2)}, u32[]{:S(2)}) collective-permute-start(f32[24,8,128]{2,1,0:T(8,128)S(1)} %get-tuple-element.36.sent_high), channel_id=1, source_target_pairs={{0,95},{32,127},{64,31},{96,63},{1,0},{33,32},{65,64},{97,96},{2,1... | collective-permute-start | bytes 294920 | tf_op jit(solution)/shard_map/ppermute | solution.py:534
  35.5 8.9 %collective-permute-start.3 = (f32[24,8,128]{2,1,0:T(8,128)S(1)}, f32[24,8,128]{2,1,0:T(8,128)S(1)}, u32[]{:S(2)}, u32[]{:S(2)}) collective-permute-start(f32[24,8,128]{2,1,0:T(8,128)S(1)} %get-tuple-element.37.sent_low), channel_id=1, source_target_pairs={{0,1},{32,33},{64,65},{96,97},{1,2},{33,34},{65,66},{97,98},{2,3},... | collective-permute-start | bytes 294920 | tf_op jit(solution)/shard_map/ppermute | solution.py:534
  46.3 3.5 %collective-permute-start.6 = (f32[24,8,128]{2,1,0:T(8,128)S(1)}, f32[24,8,128]{2,1,0:T(8,128)S(1)}, u32[]{:S(2)}, u32[]{:S(2)}) collective-permute-start(f32[24,8,128]{2,1,0:T(8,128)S(1)} %get-tuple-element.42.sent_high), channel_id=1, source_target_pairs={{0,95},{32,127},{64,31},{96,63},{1,0},{33,32},{65,64},{97,96},{2,1... | collective-permute-start | bytes 294920 | tf_op jit(solution)/shard_map/ppermute | solution.py:534
  46.3 8.9 %collective-permute-start.7 = (f32[24,8,128]{2,1,0:T(8,128)S(1)}, f32[24,8,128]{2,1,0:T(8,128)S(1)}, u32[]{:S(2)}, u32[]{:S(2)}) collective-permute-start(f32[24,8,128]{2,1,0:T(8,128)S(1)} %get-tuple-element.43.sent_low), channel_id=1, source_target_pairs={{0,1},{32,33},{64,65},{96,97},{1,2},{33,34},{65,66},{97,98},{2,3},... | collective-permute-start | bytes 294920 | tf_op jit(solution)/shard_map/ppermute | solution.py:534
  56.7 3.5 %collective-permute-start.8 = (f32[24,8,128]{2,1,0:T(8,128)S(1)}, f32[24,8,128]{2,1,0:T(8,128)S(1)}, u32[]{:S(2)}, u32[]{:S(2)}) collective-permute-start(f32[24,8,128]{2,1,0:T(8,128)S(1)} %get-tuple-element.46.sent_high), channel_id=1, source_target_pairs={{0,95},{32,127},{64,31},{96,63},{1,0},{33,32},{65,64},{97,96},{2,1... | collective-permute-start | bytes 294920 | tf_op jit(solution)/shard_map/ppermute | solution.py:534
  56.8 9.0 %collective-permute-start.9 = (f32[24,8,128]{2,1,0:T(8,128)S(1)}, f32[24,8,128]{2,1,0:T(8,128)S(1)}, u32[]{:S(2)}, u32[]{:S(2)}) collective-permute-start(f32[24,8,128]{2,1,0:T(8,128)S(1)} %get-tuple-element.47.sent_low), channel_id=1, source_target_pairs={{0,1},{32,33},{64,65},{96,97},{1,2},{33,34},{65,66},{97,98},{2,3},... | collective-permute-start | bytes 294920 | tf_op jit(solution)/shard_map/ppermute | solution.py:534
  67.7 3.5 %collective-permute-start.10 = (f32[24,8,128]{2,1,0:T(8,128)S(1)}, f32[24,8,128]{2,1,0:T(8,128)S(1)}, u32[]{:S(2)}, u32[]{:S(2)}) collective-permute-start(f32[24,8,128]{2,1,0:T(8,128)S(1)} %get-tuple-element.50.sent_high), channel_id=1, source_target_pairs={{0,95},{32,127},{64,31},{96,63},{1,0},{33,32},{65,64},{97,96},{2,1... | collective-permute-start | bytes 294920 | tf_op jit(solution)/shard_map/ppermute | solution.py:534
  67.7 8.9 %collective-permute-start.11 = (f32[24,8,128]{2,1,0:T(8,128)S(1)}, f32[24,8,128]{2,1,0:T(8,128)S(1)}, u32[]{:S(2)}, u32[]{:S(2)}) collective-permute-start(f32[24,8,128]{2,1,0:T(8,128)S(1)} %get-tuple-element.51.sent_low), channel_id=1, source_target_pairs={{0,1},{32,33},{64,65},{96,97},{1,2},{33,34},{65,66},{97,98},{2,3},... | collective-permute-start | bytes 294920 | tf_op jit(solution)/shard_map/ppermute | solution.py:534
where the time goes:
time: 104 us
  blocking collectives  32.8 us (32%)
  waiting for transfers between devices  32.5 us (31%)
  starting transfers between devices  25.2 us (24%)
  Pallas kernels  8.96 us (9%)
  other arithmetic  2.35 us (2%)
  local copies, waits for them, and re-layouts  1.73 us (2%)
    ppermute x12, waiting for transfers between devices, to_neighbour(): return lax.ppermute(array, ('sub', 'lat'), pairs)  32.5 us
    ppermute x12, starting transfers between devices, to_neighbour(): return lax.ppermute(array, ('sub', 'lat'), pairs)  25.2 us
    all_to_all x1, blocking collectives, whole(): traces = lax.all_to_all(traces, 'sub', 0, 0, tiled=True)  13.3 us
    all_to_all x1, blocking collectives, gather_sums(): lax.all_to_all(sums, ('sub', 'lat'), 0, 0, tiled=True, axis_index_groups=...  11.5 us
    pallas_call x8, Pallas kernels, call(): pl.pallas_call(kernel, out_shape=tuple((jax.ShapeDtypeStruct(s, F32) for...  8.96 us
    all_gather x1, blocking collectives, shards(): gathered = lax.all_gather(own, 'sub')  7.97 us
  transfers between devices with their start and end apart: 12, of which 9 were waited for; matrix products, arithmetic and copies ran while one was open for 0% of the time, Pallas kernels for 1%

commit v1 on v0

--- a/solution.py
+++ b/solution.py
@@ -141,17 +141,39 @@
             ref[(*lead, 12 + s * 3 + a)] = spinor[s][a][1]
 
 
-def load_half(ref, base=0):
+class Swapped:
+
+    def __init__(self, far, near):
+        self.far, self.near = far, near
+        self.odd = lax.rem(lax.axis_index("lat"), 2) == 1
+
+    def high(self, n):
+        return lax.select(self.odd, self.far[n], self.near[n])
+
+    def low(self, n):
+        return lax.select(self.odd, self.near[n], self.far[n])
+
+    def put(self, n, for_earlier, for_later):
+        self.far[n] = lax.select(self.odd, for_later, for_earlier)
+        self.near[n] = lax.select(self.odd, for_earlier, for_later)
+
+
+def load_half(row, base=0):
     return [
-        [(ref[base + s * 3 + a], ref[base + 6 + s * 3 + a]) for a in range(3)] for s in range(2)
+        [(row(base + s * 3 + a), row(base + 6 + s * 3 + a)) for a in range(3)] for s in range(2)
     ]
 
 
-def store_half(ref, half, base, factor):
+def store_halves(edges, for_earlier, for_later, base):
+    at_first, at_last = edge_signs()
     for s in range(2):
         for a in range(3):
-            ref[base + s * 3 + a] = half[s][a][0] * factor
-            ref[base + 6 + s * 3 + a] = half[s][a][1] * factor
+            for part in range(2):
+                edges.put(
+                    base + part * 6 + s * 3 + a,
+                    for_earlier[s][a][part] * at_first,
+                    for_later[s][a][part] * at_last,
+                )
 
 
 def scaled_half(half, factor):
@@ -199,9 +221,9 @@
     return diagonal, upper
 
 
-def block_packed(ref):
-    diagonal = [ref[i] for i in range(6)]
-    upper = {pair: (ref[6 + 2 * n], ref[7 + 2 * n]) for n, pair in enumerate(PAIRS)}
+def block_packed(row):
+    diagonal = [row(i) for i in range(6)]
+    upper = {pair: (row(6 + 2 * n), row(7 + 2 * n)) for n, pair in enumerate(PAIRS)}
     return diagonal, upper
 
 
@@ -229,32 +251,28 @@
     return at_first, at_last
 
 
-def begin_schur(vector, links, odd_inverse, dagger, partial, high, low):
+def begin_schur(vector, links, odd_inverse, dagger, partial, sent):
     forward, backward = (1, -1) if dagger else (-1, 1)
-    at_first, at_last = edge_signs()
     for time in range(2):
         store_spinor(
             partial, clover_at(odd_inverse, hop_at(vector, links, time, 1, dagger), time), time
         )
-    store_half(high, project(load_spinor(vector, 0), 3, forward), 0, at_first)
-    store_half(high, project(load_spinor(partial, 0), 3, forward), 12, at_first)
-    half = link_mul_adj(link_at(links, 0, 3, 1), project(load_spinor(vector, 1), 3, backward))
-    store_half(low, half, 0, at_last)
-    half = link_mul_adj(link_at(links, 1, 3, 1), project(load_spinor(partial, 1), 3, backward))
-    store_half(low, half, 12, at_last)
+    for base, field, parity in ((0, vector, 0), (12, partial, 1)):
+        earlier = project(load_spinor(field, 0), 3, forward)
+        later = project(load_spinor(field, 1), 3, backward)
+        store_halves(sent, earlier, link_mul_adj(link_at(links, parity, 3, 1), later), base)
 
 
 def end_schur(
-    vector, partial, sent_high, sent_low, got_high, got_low, around_high, around_low,
-    links, even, odd_inverse, dagger, odd_field, result,
+    vector, partial, sent, got, around, links, even, odd_inverse, dagger, odd_field, result
 ):
     forward, backward = (1, -1) if dagger else (-1, 1)
     at_first, at_last = edge_signs()
     for time in range(2):
         if time == 0:
-            half, sign = load_half(got_low), backward
+            half, sign = load_half(got.low), backward
         else:
-            half = link_mul(link_at(links, 1, 3, 1), load_half(got_high))
+            half = link_mul(link_at(links, 1, 3, 1), load_half(got.high))
             sign = forward
         own = load_spinor(partial, time)
         top = block_mul(block_at(odd_inverse, 0, time), half)
@@ -264,10 +282,10 @@
             for s in range(2)
         ]
         store_spinor(odd_field, whole, time)
-    back = block_mul(block_packed(around_high), load_half(sent_low))
-    high = add_half(load_half(got_high, 12), scaled_half(back, at_last))
-    back = block_mul(block_packed(around_low), load_half(sent_high))
-    low = add_half(load_half(got_low, 12), scaled_half(back, at_first))
+    back = block_mul(block_packed(around.high), load_half(sent.high))
+    high = add_half(load_half(got.high, 12), scaled_half(back, at_last))
+    back = block_mul(block_packed(around.low), load_half(sent.low))
+    low = add_half(load_half(got.low, 12), scaled_half(back, at_first))
     for time in range(2):
         returned = hop_at(odd_field, links, time, 0, dagger, high, low)
         direct = clover_at(even, load_spinor(vector, time), time)
@@ -288,7 +306,7 @@
         )
 
 
-def around_kernel(links, odd_inverse, high, low):
+def around_kernel(links, odd_inverse, _, far, near):
     blocks = []
     for time in range(2):
         diagonal0, upper0 = block_at(odd_inverse, 0, time)
@@ -300,10 +318,8 @@
             )
         )
     diagonal, upper = blocks[0]
-    for i in range(6):
-        high[i] = diagonal[i]
-    for n, pair in enumerate(PAIRS):
-        high[6 + 2 * n], high[7 + 2 * n] = upper[pair]
+    earlier = diagonal + [part for pair in PAIRS for part in upper[pair]]
+    later = [None] * 36
     diagonal, upper = blocks[1]
 
     def entry(i, j):
@@ -332,22 +348,24 @@
                     total = plus(total, mul_conj(link[c][a], right[c][b]), 0)
                 i, j = s0 * 3 + a, s1 * 3 + b
                 if i == j:
-                    low[i] = total[0]
+                    later[i] = total[0]
                 else:
                     n = PAIRS.index((i, j))
-                    low[6 + 2 * n], low[7 + 2 * n] = total
-
-
-def vector_index():
-    upper = lax.axis_index("lat") // (lax.axis_size("lat") // 2)
-    return jnp.bitwise_xor(lax.axis_index("sub"), 2 * upper)
-
-
-def start_kernel(probe_rows, gathered, links, odd_inverse, probes, turned, rhs, high, low, raw):
+                    later[6 + 2 * n], later[7 + 2 * n] = total
+    edges = Swapped(far, near)
+    for n in range(36):
+        edges.put(n, earlier[n], later[n])
+
+
+def pack_kernel(noise, colours, out):
+    out[:48] = noise[...]
+    out[48:] = colours[...].astype(F32)
+
+
+def start_kernel(probe_rows, gathered, links, odd_inverse, probes, turned, rhs, far, near, raw):
     for q in range(4):
         raw[:, :, 2 * q : 2 * q + 2, :] = gathered[q]
-    probe_row = probe_rows[vector_index()]
-    at_first, at_last = edge_signs()
+    probe_row = probe_rows[lax.axis_index("sub")]
     for parity in range(2):
         for time in range(2):
             masked = jnp.bitwise_and(raw[48 + parity, time].astype(jnp.int32), probe_row)
@@ -372,30 +390,30 @@
             ],
             time,
         )
-    store_half(high, project(load_spinor(turned, 0), 3, -1), 0, at_first)
     half = link_mul_adj(link_at(links, 1, 3, 1), project(load_spinor(turned, 1), 3, 1))
-    store_half(low, half, 0, at_last)
-
-
-def rhs_kernel(partial, got_high, got_low, links, odd_inverse, rhs, odd, high, low):
-    half = scaled_half(load_half(got_low), KAPPA)
+    store_halves(Swapped(far, near), project(load_spinor(turned, 0), 3, -1), half, 0)
+
+
+def rhs_kernel(partial, got_far, got_near, links, odd_inverse, rhs, odd, far, near):
+    got = Swapped(got_far, got_near)
+    half = scaled_half(load_half(got.low), KAPPA)
     store_spinor(rhs, expand_onto(load_spinor(partial, 0), half, 3, 1), 0)
-    half = scaled_half(link_mul(link_at(links, 0, 3, 1), load_half(got_high)), KAPPA)
+    half = scaled_half(link_mul(link_at(links, 0, 3, 1), load_half(got.high)), KAPPA)
     store_spinor(rhs, expand_onto(load_spinor(partial, 1), half, 3, -1), 1)
-    begin_schur(rhs, links, odd_inverse, True, odd, high, low)
+    begin_schur(rhs, links, odd_inverse, True, odd, Swapped(far, near))
 
 
 def step_kernel(
     dagger,
-    vector, partial, sent_high, sent_low, got_high, got_low, around_high, around_low,
+    vector, partial, sent_far, sent_near, got_far, got_near, around_far, around_near,
     links, even, odd_inverse,
-    result, odd_field, odd, high, low,
+    result, odd, far, near, odd_field,
 ):
     end_schur(
-        vector, partial, sent_high, sent_low, got_high, got_low, around_high, around_low,
-        links, even, odd_inverse, dagger, odd_field, result,
-    )
-    begin_schur(result, links, odd_inverse, not dagger, odd, high, low)
+        vector, partial, Swapped(sent_far, sent_near), Swapped(got_far, got_near),
+        Swapped(around_far, around_near), links, even, odd_inverse, dagger, odd_field, result,
+    )
+    begin_schur(result, links, odd_inverse, not dagger, odd, Swapped(far, near))
 
 
 def column_sum(left, right):
@@ -408,13 +426,13 @@
 
 
 def last_kernel(
-    vector, partial, sent_high, sent_low, got_high, got_low, around_high, around_low,
+    vector, partial, sent_far, sent_near, got_far, got_near, around_far, around_near,
     links, even, odd_inverse, first, image,
     odd_field, sums, result,
 ):
     end_schur(
-        vector, partial, sent_high, sent_low, got_high, got_low, around_high, around_low,
-        links, even, odd_inverse, False, odd_field, result,
+        vector, partial, Swapped(sent_far, sent_near), Swapped(got_far, got_near),
+        Swapped(around_far, around_near), links, even, odd_inverse, False, odd_field, result,
     )
     first_at = lambda time, n: first[time, n]
     image_at = lambda time, n: image[time, n]
@@ -442,7 +460,8 @@
         sums[n] = block
 
 
-def trace_kernel(sums, probes, turned, first, first_odd, second, second_odd, out):
+def trace_kernel(sums, probes, turned, first, first_odd, second, second_odd, *outs):
+    core, chip = lax.rem(lax.axis_index("sub"), 2), lax.axis_index("sub") // 2
     whole = lambda x: jnp.sum(jnp.sum(x, axis=0, keepdims=True), axis=1, keepdims=True)
     row = [sums[:, n, :] for n in range(8)]
     norm, crossed, about, rest, rest_first, image_rest, image_cross, image_norm = row
@@ -494,22 +513,33 @@
             for hop_dir in range(4):
                 for part in range(2):
                     value = columns[hop_dir][part]
-                    for q in range(4):
-                        out[q, parity * 8 + part * 4 + hop_dir, time] = value[2 * q : 2 * q + 2]
+                    place = parity * 8 + part * 4 + hop_dir
+                    quarters = [value[2 * q : 2 * q + 2] for q in range(4)]
+                    for low in range(2):
+                        halves = [
+                            lax.select(core != low, quarters[2 * n + 1], quarters[2 * n])
+                            for n in range(2)
+                        ]
+                        for high in range(2):
+                            outs[2 * high + low][place, time] = lax.select(
+                                chip != high, halves[1], halves[0]
+                            )
 
 
 VMEM = pl.BlockSpec(memory_space=pltpu.VMEM)
 SMEM = pl.BlockSpec(memory_space=pltpu.SMEM)
-
-
-def call(kernel, name, shapes, scalars, arrays, scratch=()):
+ANY = pl.BlockSpec(memory_space=pl.ANY)
+
+
+def call(kernel, name, shapes, scalars, arrays, scratch=(), outside=()):
     return pl.pallas_call(
         kernel,
         out_shape=tuple(jax.ShapeDtypeStruct(s, F32) for s in shapes),
-        in_specs=[SMEM] * len(scalars) + [VMEM] * len(arrays),
+        in_specs=[SMEM] * len(scalars)
+        + [ANY if n in outside else VMEM for n in range(len(arrays))],
         out_specs=tuple(VMEM for _ in shapes),
         scratch_shapes=[pltpu.VMEM(s, F32) for s in scratch],
-        compiler_params=pltpu.CompilerParams(vmem_limit_bytes=24 * 1024 * 1024),
+        compiler_params=pltpu.CompilerParams(vmem_limit_bytes=16 * 1024 * 1024),
         name=name,
     )(*scalars, *arrays)
 
@@ -518,101 +548,85 @@
 EDGE = (24, 8, 128)
 
 
-def to_neighbour(array, by):
-    length, subs = lax.axis_size("lat"), lax.axis_size("sub")
-    flip = lambda place: 2 * (place // (length // 2))
-    pairs = []
-    for place in range(length):
-        target = (place + by) % length
-        for vector in range(subs):
-            pairs.append(
-                (
-                    (vector ^ flip(place)) * length + place,
-                    (vector ^ flip(target)) * length + target,
-                )
-            )
-    return lax.ppermute(array, ("sub", "lat"), pairs)
-
-
-def exchange(high, low):
-    return to_neighbour(high, -1), to_neighbour(low, 1)
-
-
-def shards(noise, colours, probe_rows, links, clover_even, clover_odd_inverse):
-    own = jnp.concatenate(
-        [noise.reshape((48,) + noise.shape[4:]), colours.astype(F32)], axis=0
+def swap(far, near):
+    length = lax.axis_size("lat")
+    place = range(length)
+    return (
+        lax.ppermute(far, "lat", [(i, (i + (1 if i % 2 else -1)) % length) for i in place]),
+        lax.ppermute(near, "lat", [(i, i ^ 1) for i in place]),
+    )
+
+
+def whole(noise, colours, probe_rows, links, even, odd_inverse):
+    (own,) = call(
+        pack_kernel,
+        "pack",
+        ((50,) + noise.shape[4:],),
+        (),
+        (noise.reshape((48,) + noise.shape[4:]), colours),
     )
     gathered = lax.all_gather(own, "sub")
-    around = call(
-        around_kernel, "around", ((36, 8, 128),) * 2, (), (links, clover_odd_inverse)
-    )
-    around = exchange(*around)
-    probes, turned, partial, high, low = call(
+    probes, turned, partial, *sent = call(
         start_kernel,
         "start",
         ((2,) + FIELD, FIELD, FIELD, (12, 8, 128), (12, 8, 128)),
         (probe_rows,),
-        (gathered, links, clover_odd_inverse),
+        (gathered, links, odd_inverse),
         ((50, 2, 8, 128),),
     )
-    got = exchange(high, low)
-    vector, odd, high, low = call(
-        rhs_kernel, "rhs", (FIELD, FIELD, EDGE, EDGE), (), (partial, *got, links, clover_odd_inverse)
+    got = swap(*sent)
+    around = swap(
+        *call(
+            around_kernel,
+            "around",
+            ((36, 8, 128),) * 2,
+            (),
+            (links, odd_inverse, turned),
+            (),
+            (2,),
+        )
+    )
+    vector, odd, *sent = call(
+        rhs_kernel, "rhs", (FIELD, FIELD, EDGE, EDGE), (), (partial, *got, links, odd_inverse)
     )
     kept = []
     for step in range(3):
-        got = exchange(high, low)
-        result, odd_field, odd, high, low = call(
+        got = swap(*sent)
+        arrays = (vector, odd, *sent, *got, *around, links, even, odd_inverse)
+        keep = step == 1
+        vector, odd, *sent = call(
             functools.partial(step_kernel, step % 2 == 0),
             "step%d" % step,
-            (FIELD, FIELD, FIELD, EDGE, EDGE),
+            (FIELD, FIELD, EDGE, EDGE) + (FIELD,) * keep,
             (),
-            (vector, odd, high, low, *got, *around, links, clover_even, clover_odd_inverse),
-        )
-        kept.append((result, odd_field))
-        vector = result
-    first, image, second = kept[0][0], kept[1][0], kept[2][0]
-    first_odd = kept[1][1]
-    got = exchange(high, low)
+            arrays,
+            () if keep else (FIELD,),
+        )
+        if keep:
+            first_odd = sent.pop()
+        kept.append(vector)
+    first, image, second = kept
+    got = swap(*sent)
     second_odd, sums = call(
         last_kernel,
         "last",
         (FIELD, (lax.axis_size("lat"), 8, 128)),
         (),
-        (
-            second, odd, high, low, *got, *around, links, clover_even, clover_odd_inverse,
-            first, image,
-        ),
+        (second, odd, *sent, *got, *around, links, even, odd_inverse, first, image),
         (FIELD,),
     )
-    return probes, turned, first, first_odd, second, second_odd, sums
-
-
-def gather_sums(sums):
-    length, subs = lax.axis_size("lat"), lax.axis_size("sub")
-    groups = [
-        [(vector ^ (2 * (place // (length // 2)))) * length + place for place in range(length)]
-        for vector in range(subs)
-    ]
-    return lax.all_to_all(
-        sums, ("sub", "lat"), 0, 0, tiled=True, axis_index_groups=groups
-    )
-
-
-def whole(noise, colours, probe_rows, links, clover_even, clover_odd_inverse):
-    probes, turned, first, first_odd, second, second_odd, sums = shards(
-        noise, colours, probe_rows, links, clover_even, clover_odd_inverse
-    )
-    sums = gather_sums(sums)
-    (traces,) = call(
+    sums = lax.all_to_all(sums, "lat", 0, 0, tiled=True)
+    traces = call(
         trace_kernel,
         "trace",
-        ((4, 16, 2, 2, 128),),
+        ((16, 2, 2, 128),) * 4,
         (),
         (sums, probes, turned, first, first_odd, second, second_odd),
     )
-    traces = lax.all_to_all(traces, "sub", 0, 0, tiled=True)
-    return jnp.sum(traces, axis=0).reshape(2, 2, 4, 2, 2, 128)
+    total = traces[0]
+    for n in (3, 2, 1):
+        total = total + lax.ppermute(traces[n], "sub", [(i, i ^ n) for i in range(4)])
+    return total.reshape(2, 2, 4, 2, 2, 128)
 
 
 def solution(mesh):

time: 104 us -> 95.8 us (0.921)
  starting transfers between devices: 25.2 us -> 41.3 us
  waiting for transfers between devices: 32.5 us -> 18.2 us
  blocking collectives: 32.8 us -> 23.7 us
  other arithmetic: 2.35 us -> 0.66 us
  local copies, waits for them, and re-layouts: 1.73 us -> 3.37 us
    ppermute x12 -> x15, starting transfers between devices: 25.2 us -> 41.3 us  [the longest x6 31.6 us: swap(): lax.ppermute(far, 'lat', [(i, (i + (1 if i % 2 else -1)) % length) for i...]
    ppermute x12 -> x15, waiting for transfers between devices: 32.5 us -> 18.2 us  [the longest x6 14.8 us: swap(): lax.ppermute(far, 'lat', [(i, (i + (1 if i % 2 else -1)) % length) for i...]
    all_to_all x2 -> x1, blocking collectives: 24.8 us -> 15.7 us  [whole(): sums = lax.all_to_all(sums, 'lat', 0, 0, tiled=True)]
    unnamed x10 -> x14, local copies, waits for them, and re-layouts: 1.73 us -> 3.37 us
    pallas_call x8 -> x9, Pallas kernels: 8.96 us -> 8.3 us  [call(): pl.pallas_call(kernel, out_shape=tuple((jax.ShapeDtypeStruct(s, F32) for...]
  transfers between devices with their start and end apart: 12 -> 15, of which waited for: 9 -> 9; matrix products, arithmetic and copies ran while one was open for 0% -> 0% of each run, Pallas kernels for 1% -> 1%
where the time goes in v1:
time: 95.8 us; the launch traced here: 95.6 us
  starting transfers between devices  41.3 us (43%)
  blocking collectives  23.7 us (25%)
  waiting for transfers between devices  18.2 us (19%)
  Pallas kernels  8.3 us (9%)
  local copies, waits for them, and re-layouts  3.37 us (4%)
    ppermute x6, starting transfers between devices, swap(): lax.ppermute(far, 'lat', [(i, (i + (1 if i % 2 else -1)) % length) for i...  31.6 us
    all_to_all x1, blocking collectives, whole(): sums = lax.all_to_all(sums, 'lat', 0, 0, tiled=True)  15.7 us
    ppermute x6, waiting for transfers between devices, swap(): lax.ppermute(far, 'lat', [(i, (i + (1 if i % 2 else -1)) % length) for i...  14.8 us
    ppermute x3, starting transfers between devices, whole(): lax.ppermute(traces[n], 'sub', [(i, i ^ n) for i in range(4)])  8.94 us
    pallas_call x9, Pallas kernels, call(): pl.pallas_call(kernel, out_shape=tuple((jax.ShapeDtypeStruct(s, F32) for...  8.3 us
    all_gather x1, blocking collectives, whole(): gathered = lax.all_gather(own, 'sub')  7.97 us
    unnamed x14, local copies, waits for them, and re-layouts  3.37 us
    ppermute x3, waiting for transfers between devices, whole(): lax.ppermute(traces[n], 'sub', [(i, i ^ n) for i in range(4)])  2.03 us
  transfers between devices with their start and end apart: 15, of which 9 were waited for; matrix products, arithmetic and copies ran while one was open for 0% of the time, Pallas kernels for 1%

profile of v1, /device:TPU:1, one launch (start us, length us, event | category | flops | bytes accessed | tf_op | source)
XLA Modules:
  0.0 95.6 jit_solution(13570181455520207768)
XLA Ops:
  0.0 0.0 copy-start
  0.0 0.0 copy-start.4
  0.0 1.0 copy-done.4
  1.0 0.0 copy-start.5
  1.0 0.7 copy-done.5
  1.7 8.0 %all-gather = f32[200,2,2,128]{3,2,1,0:T(2,128)S(1)} all-gather(f32[50,2,2,128]{3,2,1,0:T(2,128)S(1)} %pack.1), channel_id=2, replica_groups=mesh['sub'=4,'lat'=32] {'sub'}, dimensions={0}, use_global_device_ids=true | all-gather | bytes 512000 | tf_op jit(solution)/shard_map/all_gather | solution.py:568
  9.6 0.0 copy-start.6
  9.6 0.0 copy-done
  9.6 0.7 copy-done.6
  10.3 0.0 copy-start.1
  10.3 1.1 %copy-done.1 = bf16[2,2,6,6,2,8,128]{6,5,4,3,2,1,0:T(8,128)(2,1)S(1)} copy-done((bf16[2,2,6,6,2,8,128]{6,5,4,3,2,1,0:T(8,128)(2,1)S(1)}, bf16[2,2,6,6,2,8,128]{6,5,4,3,2,1,0:T(8,128)(2,1)}, u32[]{:S(2)}) %copy-start.1) | copy-done | bytes 589848
  11.4 1.3 %start.1 = (f32[2,2,24,8,128]{4,3,2,1,0:T(8,128)S(1)}, f32[2,24,8,128]{3,2,1,0:T(8,128)S(1)}, f32[2,24,8,128]{3,2,1,0:T(8,128)S(1)}, f32[12,8,128]{2,1,0:T(8,128)S(1)}, f32[12,8,128]{2,1,0:T(8,128)S(1)}) custom-call(s32[4]{0:T(128)S(1)} %copy-done.6, f32[4,50,2,2,128]{4,3,2,1,0:T(2,128)S(1)} %bitcast.3, bf16[2,4,2,3,3,2,8,128]{7,6,5,4,3,2,1,0:T(8,128)(2,1)S(1)} %copy-done, ...), custom_call_target="tpu_custom_call" | custom-call | tf_op jit(solution)/shard_map/start/pallas_call | solution.py:535
  12.6 8.4 %collective-permute-start = (f32[12,8,128]{2,1,0:T(8,128)S(1)}, f32[12,8,128]{2,1,0:T(8,128)S(1)}, u32[]{:S(2)}, u32[]{:S(2)}) collective-permute-start(f32[12,8,128]{2,1,0:T(8,128)S(1)} %get-tuple-element.36), channel_id=1, source_target_pairs={{0,31},{1,2},{2,1},{3,4},{4,3},{5,6},{6,5},{7,8},{8,7},{9,10},{10,... | collective-permute-start | bytes 147464 | tf_op jit(solution)/shard_map/ppermute | solution.py:555
  21.0 0.0 collective-permute-start.1
  21.0 0.2 around.1
  21.2 0.9 collective-permute-start.4
  22.0 0.8 collective-permute-start.5
  22.8 0.1 collective-permute-done.got_far
  22.9 1.0 %collective-permute-done.1.got_near = f32[12,8,128]{2,1,0:T(8,128)S(1)} collective-permute-done((f32[12,8,128]{2,1,0:T(8,128)S(1)}, f32[12,8,128]{2,1,0:T(8,128)S(1)}, u32[]{:S(2)}, u32[]{:S(2)}) %collective-permute-start.1) | collective-permute-done | bytes 49184 | tf_op jit(solution)/shard_map/ppermute | solution.py:556
  23.9 0.0 copy-start.2
  23.9 0.0 copy-start.3
  23.9 0.7 rhs.1
  24.6 5.8 %collective-permute-start.2 = (f32[24,8,128]{2,1,0:T(8,128)S(1)}, f32[24,8,128]{2,1,0:T(8,128)S(1)}, u32[]{:S(2)}, u32[]{:S(2)}) collective-permute-start(f32[24,8,128]{2,1,0:T(8,128)S(1)} %get-tuple-element.40.sent_far), channel_id=1, source_target_pairs={{0,31},{1,2},{2,1},{3,4},{4,3},{5,6},{6,5},{7,8},{8,7},{9,10},{10,... | collective-permute-start | bytes 294920 | tf_op jit(solution)/shard_map/ppermute | solution.py:555
  30.4 0.0 collective-permute-start.3
  30.4 3.5 %collective-permute-done.2.got_far = f32[24,8,128]{2,1,0:T(8,128)S(1)} collective-permute-done((f32[24,8,128]{2,1,0:T(8,128)S(1)}, f32[24,8,128]{2,1,0:T(8,128)S(1)}, u32[]{:S(2)}, u32[]{:S(2)}) %collective-permute-start.2) | collective-permute-done | bytes 98336 | tf_op jit(solution)/shard_map/ppermute | solution.py:555
  33.9 0.3 collective-permute-done.3.got_near
  34.2 0.0 collective-permute-done.4.around_far
  34.2 0.0 collective-permute-done.5.around_near
  34.2 0.0 copy-done.2
  34.2 0.0 copy-done.3
  34.2 1.5 %step0.1 = (f32[2,24,8,128]{3,2,1,0:T(8,128)S(1)}, f32[2,24,8,128]{3,2,1,0:T(8,128)S(1)}, f32[24,8,128]{2,1,0:T(8,128)S(1)}, f32[24,8,128]{2,1,0:T(8,128)S(1)}) custom-call(f32[2,24,8,128]{3,2,1,0:T(8,128)S(1)} %get-tuple-element.38.vector, f32[2,24,8,128]{3,2,1,0:T(8,128)S(1)} %get-tuple-element.39.partial, f32[24,8,128]{2,1,0:T(8,128)S(1)} %get-tuple-element.40.sent_far, ...), custom_call_target="tpu_custom_call" | custom-call | tf_op jit(solution)/shard_map/step0/pallas_call | solution.py:535
  35.7 5.5 %collective-permute-start.6 = (f32[24,8,128]{2,1,0:T(8,128)S(1)}, f32[24,8,128]{2,1,0:T(8,128)S(1)}, u32[]{:S(2)}, u32[]{:S(2)}) collective-permute-start(f32[24,8,128]{2,1,0:T(8,128)S(1)} %get-tuple-element.47.sent_far), channel_id=1, source_target_pairs={{0,31},{1,2},{2,1},{3,4},{4,3},{5,6},{6,5},{7,8},{8,7},{9,10},{10,... | collective-permute-start | bytes 294920 | tf_op jit(solution)/shard_map/ppermute | solution.py:555
  41.3 0.0 collective-permute-start.7
  41.3 3.7 %collective-permute-done.6.got_far = f32[24,8,128]{2,1,0:T(8,128)S(1)} collective-permute-done((f32[24,8,128]{2,1,0:T(8,128)S(1)}, f32[24,8,128]{2,1,0:T(8,128)S(1)}, u32[]{:S(2)}, u32[]{:S(2)}) %collective-permute-start.6) | collective-permute-done | bytes 98336 | tf_op jit(solution)/shard_map/ppermute | solution.py:555
  45.0 0.0 collective-permute-done.7.got_near
  45.0 1.5 %step1.1 = (f32[2,24,8,128]{3,2,1,0:T(8,128)S(1)}, f32[2,24,8,128]{3,2,1,0:T(8,128)S(1)}, f32[24,8,128]{2,1,0:T(8,128)S(1)}, f32[24,8,128]{2,1,0:T(8,128)S(1)}, f32[2,24,8,128]{3,2,1,0:T(8,128)S(1)}) custom-call(f32[2,24,8,128]{3,2,1,0:T(8,128)S(1)} %get-tuple-element.45.vector.first, f32[2,24,8,128]{3,2,1,0:T(8,128)S(1)} %get-tuple-element.46.partial, ...), custom_call_target="tpu_custom_call" | custom-call | tf_op jit(solution)/shard_map/step1/pallas_call | solution.py:535
  46.5 5.5 %collective-permute-start.8 = (f32[24,8,128]{2,1,0:T(8,128)S(1)}, f32[24,8,128]{2,1,0:T(8,128)S(1)}, u32[]{:S(2)}, u32[]{:S(2)}) collective-permute-start(f32[24,8,128]{2,1,0:T(8,128)S(1)} %get-tuple-element.51.sent_far), channel_id=1, source_target_pairs={{0,31},{1,2},{2,1},{3,4},{4,3},{5,6},{6,5},{7,8},{8,7},{9,10},{10,... | collective-permute-start | bytes 294920 | tf_op jit(solution)/shard_map/ppermute | solution.py:555
  52.1 0.0 collective-permute-start.9
  52.1 3.7 %collective-permute-done.8.got_far = f32[24,8,128]{2,1,0:T(8,128)S(1)} collective-permute-done((f32[24,8,128]{2,1,0:T(8,128)S(1)}, f32[24,8,128]{2,1,0:T(8,128)S(1)}, u32[]{:S(2)}, u32[]{:S(2)}) %collective-permute-start.8) | collective-permute-done | bytes 98336 | tf_op jit(solution)/shard_map/ppermute | solution.py:555
  55.8 0.0 collective-permute-done.9.got_near
  55.8 1.5 %step2.1 = (f32[2,24,8,128]{3,2,1,0:T(8,128)S(1)}, f32[2,24,8,128]{3,2,1,0:T(8,128)S(1)}, f32[24,8,128]{2,1,0:T(8,128)S(1)}, f32[24,8,128]{2,1,0:T(8,128)S(1)}) custom-call(f32[2,24,8,128]{3,2,1,0:T(8,128)S(1)} %get-tuple-element.49.vector.image, f32[2,24,8,128]{3,2,1,0:T(8,128)S(1)} %get-tuple-element.50.partial, ...), custom_call_target="tpu_custom_call" | custom-call | tf_op jit(solution)/shard_map/step2/pallas_call | solution.py:535
  57.4 5.5 %collective-permute-start.10 = (f32[24,8,128]{2,1,0:T(8,128)S(1)}, f32[24,8,128]{2,1,0:T(8,128)S(1)}, u32[]{:S(2)}, u32[]{:S(2)}) collective-permute-start(f32[24,8,128]{2,1,0:T(8,128)S(1)} %get-tuple-element.55.sent_far), channel_id=1, source_target_pairs={{0,31},{1,2},{2,1},{3,4},{4,3},{5,6},{6,5},{7,8},{8,7},{9,10},{10,... | collective-permute-start | bytes 294920 | tf_op jit(solution)/shard_map/ppermute | solution.py:555
  62.9 0.0 collective-permute-start.11
  62.9 3.8 %collective-permute-done.10.got_far = f32[24,8,128]{2,1,0:T(8,128)S(1)} collective-permute-done((f32[24,8,128]{2,1,0:T(8,128)S(1)}, f32[24,8,128]{2,1,0:T(8,128)S(1)}, u32[]{:S(2)}, u32[]{:S(2)}) %collective-permute-start.10) | collective-permute-done | bytes 98336 | tf_op jit(solution)/shard_map/ppermute | solution.py:555
  66.6 0.0 collective-permute-done.11.got_near
  66.6 1.0 %last.1 = (f32[2,24,8,128]{3,2,1,0:T(8,128)S(1)}, f32[32,8,128]{2,1,0:T(8,128)S(1)}) custom-call(f32[2,24,8,128]{3,2,1,0:T(8,128)S(1)} %get-tuple-element.53.vector.second, f32[2,24,8,128]{3,2,1,0:T(8,128)S(1)} %get-tuple-element.54.partial, f32[24,8,128]{2,1,0:T(8,128)S(1)} %get-tuple-element.55.sent_far, f32[24,8,128]{2,1,0:T(8,128)S(1)} %get-tuple-element.56.sent_near, ...), custom_call_target="tpu_custom_call" | custom-call | tf_op jit(solution)/shard_map/last/pallas_call | solution.py:535
  67.7 15.7 %all_to_all.5.sums = f32[32,8,128]{2,1,0:T(8,128)S(1)} all-to-all(f32[32,8,128]{2,1,0:T(8,128)S(1)} %get-tuple-element.57), channel_id=1, replica_groups=mesh['sub'=4,'lat'=32] {'lat'}, dimensions={0} | all-to-all | bytes 262144 | tf_op jit(solution)/shard_map/all_to_all | solution.py:618
  83.4 0.6 trace.1
  84.0 7.7 %collective-permute-start.12 = (f32[16,2,2,128]{3,2,1,0:T(2,128)S(1)}, f32[16,2,2,128]{3,2,1,0:T(2,128)S(1)}, u32[]{:S(2)}, u32[]{:S(2)}) collective-permute-start(f32[16,2,2,128]{3,2,1,0:T(2,128)S(1)} %get-tuple-element.62), channel_id=1, source_target_pairs={{0,96},{32,64},{64,32},{96,0},{1,97},{33,65},{65,33},{97,1},{2,98}... | collective-permute-start | bytes 98312 | tf_op jit(solution)/shard_map/ppermute | solution.py:628
  91.7 1.2 %collective-permute-start.13 = (f32[16,2,2,128]{3,2,1,0:T(2,128)S(1)}, f32[16,2,2,128]{3,2,1,0:T(2,128)S(1)}, u32[]{:S(2)}, u32[]{:S(2)}) collective-permute-start(f32[16,2,2,128]{3,2,1,0:T(2,128)S(1)} %get-tuple-element.63), channel_id=1, source_target_pairs={{0,64},{32,96},{64,0},{96,32},{1,65},{33,97},{65,1},{97,33},{2,66}... | collective-permute-start | bytes 98312 | tf_op jit(solution)/shard_map/ppermute | solution.py:628
  92.9 0.0 collective-permute-start.14
  92.9 0.4 collective-permute-done.12
  93.3 1.6 %collective-permute-done.13 = f32[16,2,2,128]{3,2,1,0:T(2,128)S(1)} collective-permute-done((f32[16,2,2,128]{3,2,1,0:T(2,128)S(1)}, f32[16,2,2,128]{3,2,1,0:T(2,128)S(1)}, u32[]{:S(2)}, u32[]{:S(2)}) %collective-permute-start.13) | collective-permute-done | bytes 32800 | tf_op jit(solution)/shard_map/ppermute | solution.py:628
  94.9 0.0 collective-permute-done.14
  94.9 0.7 add_add_fusion
  (1 shorter events, 0.0 us)
Async XLA Ops:
  0.0 9.6 %copy-start = (bf16[2,4,2,3,3,2,8,128]{7,6,5,4,3,2,1,0:T(8,128)(2,1)S(1)}, bf16[2,4,2,3,3,2,8,128]{7,6,5,4,3,2,1,0:T(8,128)(2,1)}, u32[]{:S(2)}) copy-start(bf16[2,4,2,3,3,2,8,128]{7,6,5,4,3,2,1,0:T(8,128)(2,1)} %links.13) | copy-start | bytes 1769476
  0.0 1.0 copy-start.4
  1.0 0.7 copy-start.5
  9.6 0.7 copy-start.6
  10.3 1.1 %copy-start.1 = (bf16[2,2,6,6,2,8,128]{6,5,4,3,2,1,0:T(8,128)(2,1)S(1)}, bf16[2,2,6,6,2,8,128]{6,5,4,3,2,1,0:T(8,128)(2,1)}, u32[]{:S(2)}) copy-start(bf16[2,2,6,6,2,8,128]{6,5,4,3,2,1,0:T(8,128)(2,1)} %odd_inverse.13) | copy-start | bytes 1769476
  12.6 10.3 %collective-permute-start = (f32[12,8,128]{2,1,0:T(8,128)S(1)}, f32[12,8,128]{2,1,0:T(8,128)S(1)}, u32[]{:S(2)}, u32[]{:S(2)}) collective-permute-start(f32[12,8,128]{2,1,0:T(8,128)S(1)} %get-tuple-element.36), channel_id=1, source_target_pairs={{0,31},{1,2},{2,1},{3,4},{4,3},{5,6},{6,5},{7,8},{8,7},{9,10},{10,... | collective-permute-start | bytes 147464 | tf_op jit(solution)/shard_map/ppermute | solution.py:555
  21.0 2.9 %collective-permute-start.1 = (f32[12,8,128]{2,1,0:T(8,128)S(1)}, f32[12,8,128]{2,1,0:T(8,128)S(1)}, u32[]{:S(2)}, u32[]{:S(2)}) collective-permute-start(f32[12,8,128]{2,1,0:T(8,128)S(1)} %get-tuple-element.37), channel_id=1, source_target_pairs={{0,1},{1,0},{2,3},{3,2},{4,5},{5,4},{6,7},{7,6},{8,9},{9,8},{10,11... | collective-permute-start | bytes 147464 | tf_op jit(solution)/shard_map/ppermute | solution.py:556
  21.2 13.0 %collective-permute-start.4 = (f32[36,8,128]{2,1,0:T(8,128)S(1)}, f32[36,8,128]{2,1,0:T(8,128)S(1)}, u32[]{:S(2)}, u32[]{:S(2)}) collective-permute-start(f32[36,8,128]{2,1,0:T(8,128)S(1)} %get-tuple-element.43), channel_id=1, source_target_pairs={{0,31},{1,2},{2,1},{3,4},{4,3},{5,6},{6,5},{7,8},{8,7},{9,10},{10,... | collective-permute-start | bytes 442376 | tf_op jit(solution)/shard_map/ppermute | solution.py:555
  22.0 12.1 %collective-permute-start.5 = (f32[36,8,128]{2,1,0:T(8,128)S(1)}, f32[36,8,128]{2,1,0:T(8,128)S(1)}, u32[]{:S(2)}, u32[]{:S(2)}) collective-permute-start(f32[36,8,128]{2,1,0:T(8,128)S(1)} %get-tuple-element.44), channel_id=1, source_target_pairs={{0,1},{1,0},{2,3},{3,2},{4,5},{5,4},{6,7},{7,6},{8,9},{9,8},{10,11... | collective-permute-start | bytes 442376 | tf_op jit(solution)/shard_map/ppermute | solution.py:556
  23.9 10.3 %copy-start.2 = (bf16[2,2,6,6,2,8,128]{6,5,4,3,2,1,0:T(8,128)(2,1)S(1)}, bf16[2,2,6,6,2,8,128]{6,5,4,3,2,1,0:T(8,128)(2,1)}, u32[]{:S(2)}) copy-start(bf16[2,2,6,6,2,8,128]{6,5,4,3,2,1,0:T(8,128)(2,1)} %odd_inverse.13) | copy-start | bytes 1769476
  23.9 10.3 %copy-start.3 = (bf16[2,2,6,6,2,8,128]{6,5,4,3,2,1,0:T(8,128)(2,1)S(1)}, bf16[2,2,6,6,2,8,128]{6,5,4,3,2,1,0:T(8,128)(2,1)}, u32[]{:S(2)}) copy-start(bf16[2,2,6,6,2,8,128]{6,5,4,3,2,1,0:T(8,128)(2,1)} %even.7) | copy-start | bytes 1769476
  24.6 9.3 %collective-permute-start.2 = (f32[24,8,128]{2,1,0:T(8,128)S(1)}, f32[24,8,128]{2,1,0:T(8,128)S(1)}, u32[]{:S(2)}, u32[]{:S(2)}) collective-permute-start(f32[24,8,128]{2,1,0:T(8,128)S(1)} %get-tuple-element.40.sent_far), channel_id=1, source_target_pairs={{0,31},{1,2},{2,1},{3,4},{4,3},{5,6},{6,5},{7,8},{8,7},{9,10},{10,... | collective-permute-start | bytes 294920 | tf_op jit(solution)/shard_map/ppermute | solution.py:555
  30.4 3.8 %collective-permute-start.3 = (f32[24,8,128]{2,1,0:T(8,128)S(1)}, f32[24,8,128]{2,1,0:T(8,128)S(1)}, u32[]{:S(2)}, u32[]{:S(2)}) collective-permute-start(f32[24,8,128]{2,1,0:T(8,128)S(1)} %get-tuple-element.41.sent_near), channel_id=1, source_target_pairs={{0,1},{1,0},{2,3},{3,2},{4,5},{5,4},{6,7},{7,6},{8,9},{9,8},{10,11... | collective-permute-start | bytes 294920 | tf_op jit(solution)/shard_map/ppermute | solution.py:556
  35.7 9.3 %collective-permute-start.6 = (f32[24,8,128]{2,1,0:T(8,128)S(1)}, f32[24,8,128]{2,1,0:T(8,128)S(1)}, u32[]{:S(2)}, u32[]{:S(2)}) collective-permute-start(f32[24,8,128]{2,1,0:T(8,128)S(1)} %get-tuple-element.47.sent_far), channel_id=1, source_target_pairs={{0,31},{1,2},{2,1},{3,4},{4,3},{5,6},{6,5},{7,8},{8,7},{9,10},{10,... | collective-permute-start | bytes 294920 | tf_op jit(solution)/shard_map/ppermute | solution.py:555
  41.3 3.8 %collective-permute-start.7 = (f32[24,8,128]{2,1,0:T(8,128)S(1)}, f32[24,8,128]{2,1,0:T(8,128)S(1)}, u32[]{:S(2)}, u32[]{:S(2)}) collective-permute-start(f32[24,8,128]{2,1,0:T(8,128)S(1)} %get-tuple-element.48.sent_near), channel_id=1, source_target_pairs={{0,1},{1,0},{2,3},{3,2},{4,5},{5,4},{6,7},{7,6},{8,9},{9,8},{10,11... | collective-permute-start | bytes 294920 | tf_op jit(solution)/shard_map/ppermute | solution.py:556
  46.5 9.3 %collective-permute-start.8 = (f32[24,8,128]{2,1,0:T(8,128)S(1)}, f32[24,8,128]{2,1,0:T(8,128)S(1)}, u32[]{:S(2)}, u32[]{:S(2)}) collective-permute-start(f32[24,8,128]{2,1,0:T(8,128)S(1)} %get-tuple-element.51.sent_far), channel_id=1, source_target_pairs={{0,31},{1,2},{2,1},{3,4},{4,3},{5,6},{6,5},{7,8},{8,7},{9,10},{10,... | collective-permute-start | bytes 294920 | tf_op jit(solution)/shard_map/ppermute | solution.py:555
  52.1 3.8 %collective-permute-start.9 = (f32[24,8,128]{2,1,0:T(8,128)S(1)}, f32[24,8,128]{2,1,0:T(8,128)S(1)}, u32[]{:S(2)}, u32[]{:S(2)}) collective-permute-start(f32[24,8,128]{2,1,0:T(8,128)S(1)} %get-tuple-element.52.sent_near), channel_id=1, source_target_pairs={{0,1},{1,0},{2,3},{3,2},{4,5},{5,4},{6,7},{7,6},{8,9},{9,8},{10,11... | collective-permute-start | bytes 294920 | tf_op jit(solution)/shard_map/ppermute | solution.py:556
  57.4 9.3 %collective-permute-start.10 = (f32[24,8,128]{2,1,0:T(8,128)S(1)}, f32[24,8,128]{2,1,0:T(8,128)S(1)}, u32[]{:S(2)}, u32[]{:S(2)}) collective-permute-start(f32[24,8,128]{2,1,0:T(8,128)S(1)} %get-tuple-element.55.sent_far), channel_id=1, source_target_pairs={{0,31},{1,2},{2,1},{3,4},{4,3},{5,6},{6,5},{7,8},{8,7},{9,10},{10,... | collective-permute-start | bytes 294920 | tf_op jit(solution)/shard_map/ppermute | solution.py:555
  62.9 3.8 %collective-permute-start.11 = (f32[24,8,128]{2,1,0:T(8,128)S(1)}, f32[24,8,128]{2,1,0:T(8,128)S(1)}, u32[]{:S(2)}, u32[]{:S(2)}) collective-permute-start(f32[24,8,128]{2,1,0:T(8,128)S(1)} %get-tuple-element.56.sent_near), channel_id=1, source_target_pairs={{0,1},{1,0},{2,3},{3,2},{4,5},{5,4},{6,7},{7,6},{8,9},{9,8},{10,11... | collective-permute-start | bytes 294920 | tf_op jit(solution)/shard_map/ppermute | solution.py:556
  84.0 9.3 %collective-permute-start.12 = (f32[16,2,2,128]{3,2,1,0:T(2,128)S(1)}, f32[16,2,2,128]{3,2,1,0:T(2,128)S(1)}, u32[]{:S(2)}, u32[]{:S(2)}) collective-permute-start(f32[16,2,2,128]{3,2,1,0:T(2,128)S(1)} %get-tuple-element.62), channel_id=1, source_target_pairs={{0,96},{32,64},{64,32},{96,0},{1,97},{33,65},{65,33},{97,1},{2,98}... | collective-permute-start | bytes 98312 | tf_op jit(solution)/shard_map/ppermute | solution.py:628
  91.7 3.2 %collective-permute-start.13 = (f32[16,2,2,128]{3,2,1,0:T(2,128)S(1)}, f32[16,2,2,128]{3,2,1,0:T(2,128)S(1)}, u32[]{:S(2)}, u32[]{:S(2)}) collective-permute-start(f32[16,2,2,128]{3,2,1,0:T(2,128)S(1)} %get-tuple-element.63), channel_id=1, source_target_pairs={{0,64},{32,96},{64,0},{96,32},{1,65},{33,97},{65,1},{97,33},{2,66}... | collective-permute-start | bytes 98312 | tf_op jit(solution)/shard_map/ppermute | solution.py:628
  92.9 2.0 %collective-permute-start.14 = (f32[16,2,2,128]{3,2,1,0:T(2,128)S(1)}, f32[16,2,2,128]{3,2,1,0:T(2,128)S(1)}, u32[]{:S(2)}, u32[]{:S(2)}) collective-permute-start(f32[16,2,2,128]{3,2,1,0:T(2,128)S(1)} %get-tuple-element.64), channel_id=1, source_target_pairs={{0,32},{32,0},{64,96},{96,64},{1,33},{33,1},{65,97},{97,65},{2,34}... | collective-permute-start | bytes 98312 | tf_op jit(solution)/shard_map/ppermute | solution.py:628

commit v2 on v1

--- a/solution.py
+++ b/solution.py
@@ -264,7 +264,7 @@
 
 
 def end_schur(
-    vector, partial, sent, got, around, links, even, odd_inverse, dagger, odd_field, result
+    direct, partial, sent, got, around, links, odd_inverse, dagger, odd_field, result
 ):
     forward, backward = (1, -1) if dagger else (-1, 1)
     at_first, at_last = edge_signs()
@@ -288,15 +288,15 @@
     low = add_half(load_half(got.low, 12), scaled_half(back, at_first))
     for time in range(2):
         returned = hop_at(odd_field, links, time, 0, dagger, high, low)
-        direct = clover_at(even, load_spinor(vector, time), time)
+        own = load_spinor(direct, time)
         factor = KAPPA * KAPPA
         store_spinor(
             result,
             [
                 [
                     (
-                        direct[s][a][0] - factor * returned[s][a][0],
-                        direct[s][a][1] - factor * returned[s][a][1],
+                        own[s][a][0] - factor * returned[s][a][0],
+                        own[s][a][1] - factor * returned[s][a][1],
                     )
                     for a in range(3)
                 ]
@@ -362,23 +362,37 @@
     out[48:] = colours[...].astype(F32)
 
 
-def start_kernel(probe_rows, gathered, links, odd_inverse, probes, turned, rhs, far, near, raw):
+def unpack_probes(probe_rows, gathered, raw, parity, probes):
+    probe_row = probe_rows[lax.axis_index("sub")]
     for q in range(4):
-        raw[:, :, 2 * q : 2 * q + 2, :] = gathered[q]
-    probe_row = probe_rows[lax.axis_index("sub")]
-    for parity in range(2):
-        for time in range(2):
-            masked = jnp.bitwise_and(raw[48 + parity, time].astype(jnp.int32), probe_row)
-            masked = jnp.bitwise_xor(masked, jnp.right_shift(masked, 2))
-            masked = jnp.bitwise_xor(masked, jnp.right_shift(masked, 1))
-            sign = (1 - 2 * jnp.bitwise_and(masked, 1)).astype(F32)
-            for n in range(24):
-                probes[parity, time, n] = raw[parity * 24 + n, time] * sign
-    for time in range(2):
-        store_spinor(turned, clover_at(odd_inverse, load_spinor(probes, 1, time), time), time)
+        raw[:24, :, 2 * q : 2 * q + 2, :] = gathered[q, 24 * parity : 24 * parity + 24]
+        raw[24, :, 2 * q : 2 * q + 2, :] = gathered[q, 48 + parity]
+    for time in range(2):
+        masked = jnp.bitwise_and(raw[24, time].astype(jnp.int32), probe_row)
+        masked = jnp.bitwise_xor(masked, jnp.right_shift(masked, 2))
+        masked = jnp.bitwise_xor(masked, jnp.right_shift(masked, 1))
+        sign = (1 - 2 * jnp.bitwise_and(masked, 1)).astype(F32)
+        for n in range(24):
+            probes[time, n] = raw[n, time] * sign
+
+
+def start_kernel(probe_rows, gathered, time_link, odd_inverse, probes, turned, far, near, raw):
+    unpack_probes(probe_rows, gathered, raw, 1, probes)
+    for time in range(2):
+        store_spinor(turned, clover_at(odd_inverse, load_spinor(probes, time), time), time)
+    link = [
+        [(time_link[0, i, j, 1].astype(F32), time_link[1, i, j, 1].astype(F32)) for j in range(3)]
+        for i in range(3)
+    ]
+    half = link_mul_adj(link, project(load_spinor(turned, 1), 3, 1))
+    store_halves(Swapped(far, near), project(load_spinor(turned, 0), 3, -1), half, 0)
+
+
+def own_rhs_kernel(probe_rows, gathered, turned, links, probes, rhs, raw):
+    unpack_probes(probe_rows, gathered, raw, 0, probes)
     for time in range(2):
         total = hop_at(turned, links, time, 0, False)
-        own = load_spinor(probes, 0, time)
+        own = load_spinor(probes, time)
         store_spinor(
             rhs,
             [
@@ -390,8 +404,11 @@
             ],
             time,
         )
-    half = link_mul_adj(link_at(links, 1, 3, 1), project(load_spinor(turned, 1), 3, 1))
-    store_halves(Swapped(far, near), project(load_spinor(turned, 0), 3, -1), half, 0)
+
+
+def direct_kernel(vector, even, out):
+    for time in range(2):
+        store_spinor(out, clover_at(even, load_spinor(vector, time), time), time)
 
 
 def rhs_kernel(partial, got_far, got_near, links, odd_inverse, rhs, odd, far, near):
@@ -405,13 +422,13 @@
 
 def step_kernel(
     dagger,
-    vector, partial, sent_far, sent_near, got_far, got_near, around_far, around_near,
-    links, even, odd_inverse,
+    direct, partial, sent_far, sent_near, got_far, got_near, around_far, around_near,
+    links, odd_inverse,
     result, odd, far, near, odd_field,
 ):
     end_schur(
-        vector, partial, Swapped(sent_far, sent_near), Swapped(got_far, got_near),
-        Swapped(around_far, around_near), links, even, odd_inverse, dagger, odd_field, result,
+        direct, partial, Swapped(sent_far, sent_near), Swapped(got_far, got_near),
+        Swapped(around_far, around_near), links, odd_inverse, dagger, odd_field, result,
     )
     begin_schur(result, links, odd_inverse, not dagger, odd, Swapped(far, near))
 
@@ -425,50 +442,101 @@
     return jnp.sum(total, axis=0, keepdims=True)
 
 
+def traces_at(left, right):
+    def dot(s, r):
+        total = mul_conj(left[s][0], right[r][0])
+        for a in (1, 2):
+            total = plus(total, mul_conj(left[s][a], right[r][a]), 0)
+        return total
+
+    up = [[dot(s, 2 + r) for r in range(2)] for s in range(2)]
+    down = [[dot(2 + s, r) for r in range(2)] for s in range(2)]
+    x_sum = plus(plus(down[0][1], down[1][0], 0), plus(up[0][1], up[1][0], 0), 2)
+    y_sum = plus(plus(down[0][1], down[1][0], 2), plus(up[0][1], up[1][0], 2), 2)
+    z_sum = plus(plus(down[0][0], down[1][1], 2), plus(up[0][0], up[1][1], 2), 2)
+    t_sum = plus(plus(down[0][0], down[1][1], 0), plus(up[0][0], up[1][1], 0), 0)
+    columns = ((-x_sum[1], x_sum[0]), y_sum, (-z_sum[1], z_sum[0]), t_sum)
+    return [columns[hop_dir][part] for part in range(2) for hop_dir in range(4)]
+
+
+def store_traces(out, place, probes, field, time):
+    for n, value in enumerate(traces_at(load_spinor(probes, time), load_spinor(field, time))):
+        out[place, n, time] = value
+
+
+def traces_kernel(probes_even, probes_odd, turned, first, first_odd, second, second_odd, out):
+    for time in range(2):
+        store_traces(out, 0, probes_even, first, time)
+        store_traces(out, 1, probes_even, second, time)
+        store_traces(out, 2, probes_odd, turned, time)
+        store_traces(out, 3, probes_odd, first_odd, time)
+        store_traces(out, 4, probes_odd, second_odd, time)
+
+
+def in_lanes(row, values):
+    lane = lax.broadcasted_iota(jnp.int32, (1, 128), 1)
+    for n, value in values.items():
+        value = jnp.broadcast_to(jnp.sum(value, axis=1, keepdims=True), (1, 128))
+        row = jnp.where(lane == n, value, row)
+    return row
+
+
+def sums_kernel(first, image, vector, row, about):
+    first_at = lambda time, n: first[time, n]
+    image_at = lambda time, n: image[time, n]
+    vector_at = lambda time, n: vector[time, n]
+    whole = lambda x: jnp.sum(x, axis=1, keepdims=True)
+    norm = column_sum(first_at, first_at)
+    image_norm = column_sum(image_at, image_at)
+    norm_all = whole(norm)
+    shift_by = jnp.broadcast_to(
+        whole(image_norm) / jnp.where(norm_all > 0, norm_all, 1.0), (8, 128)
+    )
+    about[...] = shift_by
+    rest_at = lambda time, n: vector[time, n] - shift_by * first[time, n]
+    lane = lax.broadcasted_iota(jnp.int32, (1, 128), 1)
+    row[...] = in_lanes(
+        jnp.where(lane == 2, shift_by[:1], 0.0),
+        {
+            0: norm,
+            1: column_sum(first_at, vector_at),
+            3: column_sum(rest_at, rest_at),
+            4: column_sum(rest_at, first_at),
+            7: image_norm,
+        },
+    )
+
+
 def last_kernel(
-    vector, partial, sent_far, sent_near, got_far, got_near, around_far, around_near,
-    links, even, odd_inverse, first, image,
+    direct, partial, sent_far, sent_near, got_far, got_near, around_far, around_near,
+    links, odd_inverse, image, row, about,
     odd_field, sums, result,
 ):
     end_schur(
-        vector, partial, Swapped(sent_far, sent_near), Swapped(got_far, got_near),
-        Swapped(around_far, around_near), links, even, odd_inverse, False, odd_field, result,
-    )
-    first_at = lambda time, n: first[time, n]
+        direct, partial, Swapped(sent_far, sent_near), Swapped(got_far, got_near),
+        Swapped(around_far, around_near), links, odd_inverse, False, odd_field, result,
+    )
     image_at = lambda time, n: image[time, n]
-    vector_at = lambda time, n: vector[time, n]
-    norm = column_sum(first_at, first_at)
-    image_norm = column_sum(image_at, image_at)
-    norm_all = jnp.sum(norm, axis=1, keepdims=True)
-    about = jnp.sum(image_norm, axis=1, keepdims=True) / jnp.where(norm_all > 0, norm_all, 1.0)
-    about = jnp.broadcast_to(about, (1, 128))
-    about_full = jnp.broadcast_to(about, (8, 128))
-    rest_at = lambda time, n: vector[time, n] - about_full * first[time, n]
-    image_rest_at = lambda time, n: result[time, n] - about_full * image[time, n]
-    rows = [
-        norm,
-        column_sum(first_at, vector_at),
-        about,
-        column_sum(rest_at, rest_at),
-        column_sum(rest_at, first_at),
-        column_sum(image_rest_at, image_rest_at),
-        column_sum(image_rest_at, image_at),
-        image_norm,
+    rest_at = lambda time, n: result[time, n] - about[...] * image[time, n]
+    sums[...] = jnp.broadcast_to(
+        in_lanes(row[...], {5: column_sum(rest_at, rest_at), 6: column_sum(rest_at, image_at)}),
+        sums.shape,
+    )
+
+
+def final_kernel(sums, own, *outs):
+    core, chip = lax.rem(lax.axis_index("sub"), 2), lax.axis_index("sub") // 2
+    table = sums[...]
+    first_lane = lax.broadcasted_iota(jnp.int32, table.shape, 1) == 0
+    norm, crossed, about, rest, rest_first, image_rest, image_cross, image_norm = [
+        table if n == 0 else pltpu.roll(table, 128 - n, 1) for n in range(8)
     ]
-    block = jnp.concatenate(rows, axis=0)
-    for n in range(sums.shape[0]):
-        sums[n] = block
-
-
-def trace_kernel(sums, probes, turned, first, first_odd, second, second_odd, *outs):
-    core, chip = lax.rem(lax.axis_index("sub"), 2), lax.axis_index("sub") // 2
-    whole = lambda x: jnp.sum(jnp.sum(x, axis=0, keepdims=True), axis=1, keepdims=True)
-    row = [sums[:, n, :] for n in range(8)]
-    norm, crossed, about, rest, rest_first, image_rest, image_cross, image_norm = row
-    norm_all = whole(norm)
-    inverse = whole(crossed) / norm_all
-    alpha = norm_all / whole(crossed)
-    off = about - inverse
+    whole = lambda x: jnp.sum(
+        jnp.sum(jnp.where(first_lane, x, 0.0), axis=0, keepdims=True), axis=1, keepdims=True
+    )
+    norm_all, crossed_all = whole(norm), whole(crossed)
+    alpha = norm_all / crossed_all
+    off = about - crossed_all / norm_all
     norm_next = alpha * alpha * whole(rest + 2.0 * off * rest_first + off * off * norm)
     beta = norm_next / norm_all
     off = about - (1.0 + beta) / alpha
@@ -476,54 +544,25 @@
         image_rest + 2.0 * off * image_cross + off * off * image_norm
     )
     alpha_next = norm_next / curved
-    alpha = jnp.broadcast_to(alpha, (8, 128))
-    alpha_next = jnp.broadcast_to(alpha_next, (8, 128))
-    beta = jnp.broadcast_to(beta, (8, 128))
-    for time in range(2):
-        for parity in range(2):
-            values = []
-            for n in range(24):
-                if parity == 0:
-                    base, other = first[time, n], second[time, n]
-                else:
-                    base, other = first_odd[time, n], second_odd[time, n]
-                search = (base - alpha * other) + beta * base
-                value = alpha * base + alpha_next * search
-                if parity == 1:
-                    value = turned[time, n] + KAPPA * value
-                values.append(value)
-            right = [
-                [(values[s * 3 + a], values[12 + s * 3 + a]) for a in range(3)] for s in range(4)
-            ]
-            left = load_spinor(probes, parity, time)
-
-            def dot(s, r):
-                total = mul_conj(left[s][0], right[r][0])
-                for a in (1, 2):
-                    total = plus(total, mul_conj(left[s][a], right[r][a]), 0)
-                return total
-
-            up = [[dot(s, 2 + r) for r in range(2)] for s in range(2)]
-            down = [[dot(2 + s, r) for r in range(2)] for s in range(2)]
-            x_sum = plus(plus(down[0][1], down[1][0], 0), plus(up[0][1], up[1][0], 0), 2)
-            y_sum = plus(plus(down[0][1], down[1][0], 2), plus(up[0][1], up[1][0], 2), 2)
-            z_sum = plus(plus(down[0][0], down[1][1], 2), plus(up[0][0], up[1][1], 2), 2)
-            t_sum = plus(plus(down[0][0], down[1][1], 0), plus(up[0][0], up[1][1], 0), 0)
-            columns = ((-x_sum[1], x_sum[0]), y_sum, (-z_sum[1], z_sum[0]), t_sum)
-            for hop_dir in range(4):
-                for part in range(2):
-                    value = columns[hop_dir][part]
-                    place = parity * 8 + part * 4 + hop_dir
-                    quarters = [value[2 * q : 2 * q + 2] for q in range(4)]
-                    for low in range(2):
-                        halves = [
-                            lax.select(core != low, quarters[2 * n + 1], quarters[2 * n])
-                            for n in range(2)
-                        ]
-                        for high in range(2):
-                            outs[2 * high + low][place, time] = lax.select(
-                                chip != high, halves[1], halves[0]
-                            )
+    of_first = jnp.broadcast_to(alpha + alpha_next * (1.0 + beta), (8, 128))
+    of_second = jnp.broadcast_to(-alpha * alpha_next, (8, 128))
+    for time in range(2):
+        for n in range(8):
+            even = of_first * own[0, n, time] + of_second * own[1, n, time]
+            odd = own[2, n, time] + KAPPA * (
+                of_first * own[3, n, time] + of_second * own[4, n, time]
+            )
+            for place, value in ((n, even), (8 + n, odd)):
+                quarters = [value[2 * q : 2 * q + 2] for q in range(4)]
+                for low in range(2):
+                    halves = [
+                        lax.select(core != low, quarters[2 * q + 1], quarters[2 * q])
+                        for q in range(2)
+                    ]
+                    for high in range(2):
+                        outs[2 * high + low][place, time] = lax.select(
+                            chip != high, halves[1], halves[0]
+                        )
 
 
 VMEM = pl.BlockSpec(memory_space=pltpu.VMEM)
@@ -566,15 +605,23 @@
         (noise.reshape((48,) + noise.shape[4:]), colours),
     )
     gathered = lax.all_gather(own, "sub")
-    probes, turned, partial, *sent = call(
+    probes_odd, turned, *sent = call(
         start_kernel,
         "start",
-        ((2,) + FIELD, FIELD, FIELD, (12, 8, 128), (12, 8, 128)),
+        (FIELD, FIELD, (12, 8, 128), (12, 8, 128)),
         (probe_rows,),
-        (gathered, links, odd_inverse),
-        ((50, 2, 8, 128),),
+        (gathered, links[1, 3], odd_inverse),
+        ((25, 2, 8, 128),),
     )
     got = swap(*sent)
+    probes_even, partial = call(
+        own_rhs_kernel,
+        "own_rhs",
+        (FIELD, FIELD),
+        (probe_rows,),
+        (gathered, turned, links),
+        ((25, 2, 8, 128),),
+    )
     around = swap(
         *call(
             around_kernel,
@@ -592,7 +639,8 @@
     kept = []
     for step in range(3):
         got = swap(*sent)
-        arrays = (vector, odd, *sent, *got, *around, links, even, odd_inverse)
+        (direct,) = call(direct_kernel, "direct%d" % step, (FIELD,), (), (vector, even))
+        arrays = (direct, odd, *sent, *got, *around, links, odd_inverse)
         keep = step == 1
         vector, odd, *sent = call(
             functools.partial(step_kernel, step % 2 == 0),
@@ -607,21 +655,28 @@
         kept.append(vector)
     first, image, second = kept
     got = swap(*sent)
+    (direct,) = call(direct_kernel, "direct3", (FIELD,), (), (second, even))
+    row, about = call(
+        sums_kernel, "sums", ((1, 128), (8, 128)), (), (first, image, second)
+    )
     second_odd, sums = call(
         last_kernel,
         "last",
-        (FIELD, (lax.axis_size("lat"), 8, 128)),
+        (FIELD, (lax.axis_size("lat"), 128)),
         (),
-        (second, odd, *sent, *got, *around, links, even, odd_inverse, first, image),
+        (direct, odd, *sent, *got, *around, links, odd_inverse, image, row, about),
         (FIELD,),
+    )
+    (own_traces,) = call(
+        traces_kernel,
+        "traces",
+        ((5, 8, 2, 8, 128),),
+        (),
+        (probes_even, probes_odd, turned, first, first_odd, second, second_odd),
     )
     sums = lax.all_to_all(sums, "lat", 0, 0, tiled=True)
     traces = call(
-        trace_kernel,
-        "trace",
-        ((16, 2, 2, 128),) * 4,
-        (),
-        (sums, probes, turned, first, first_odd, second, second_odd),
+        final_kernel, "final", ((16, 2, 2, 128),) * 4, (), (sums, own_traces)
     )
     total = traces[0]
     for n in (3, 2, 1):

time: 95.8 us -> 93.3 us (0.974)
  blocking collectives: 23.7 us -> 7.97 us
  starting transfers between devices: 41.3 us -> 48.4 us
  waiting for transfers between devices: 18.2 us -> 24.5 us
  local copies, waits for them, and re-layouts: 3.37 us -> 1.66 us
  Pallas kernels: 8.3 us -> 9.75 us
    all_to_all x1 -> x0, blocking collectives: 15.7 us -> none  [whole(): sums = lax.all_to_all(sums, 'lat', 0, 0, tiled=True)]
    all_to_all x0 -> x1, waiting for transfers between devices: none -> 8.26 us  [whole(): sums = lax.all_to_all(sums, 'lat', 0, 0, tiled=True)]
    all_to_all x0 -> x1, starting transfers between devices: none -> 7.1 us  [whole(): sums = lax.all_to_all(sums, 'lat', 0, 0, tiled=True)]
    unnamed x14 -> x12, local copies, waits for them, and re-layouts: 3.37 us -> 0.7 us
    pallas_call x9 -> x16, Pallas kernels: 8.3 us -> 9.75 us  [call(): pl.pallas_call(kernel, out_shape=tuple((jax.ShapeDtypeStruct(s, F32) for...]
    ppermute x6, waiting for transfers between devices: 14.8 us -> 13.8 us  [swap(): lax.ppermute(far, 'lat', [(i, (i + (1 if i % 2 else -1)) % length) for i...]
  transfers between devices with their start and end apart: 15 -> 16, of which waited for: 9 -> 9; matrix products, arithmetic and copies ran while one was open for 0% -> 0% of each run, Pallas kernels for 1% -> 3%
where the time goes in v2:
time: 93.3 us; the launch traced here: 93.1 us
  starting transfers between devices  48.4 us (52%)
  waiting for transfers between devices  24.5 us (26%)
  Pallas kernels  9.75 us (10%)
  blocking collectives  7.97 us (9%)
  local copies, waits for them, and re-layouts  1.66 us (2%)
    ppermute x6, starting transfers between devices, swap(): lax.ppermute(far, 'lat', [(i, (i + (1 if i % 2 else -1)) % length) for i...  31.6 us
    ppermute x6, waiting for transfers between devices, swap(): lax.ppermute(far, 'lat', [(i, (i + (1 if i % 2 else -1)) % length) for i...  13.8 us
    pallas_call x16, Pallas kernels, call(): pl.pallas_call(kernel, out_shape=tuple((jax.ShapeDtypeStruct(s, F32) for...  9.75 us
    ppermute x3, starting transfers between devices, whole(): lax.ppermute(traces[n], 'sub', [(i, i ^ n) for i in range(4)])  8.94 us
    all_to_all x1, waiting for transfers between devices, whole(): sums = lax.all_to_all(sums, 'lat', 0, 0, tiled=True)  8.26 us
    all_gather x1, blocking collectives, whole(): gathered = lax.all_gather(own, 'sub')  7.97 us
    all_to_all x1, starting transfers between devices, whole(): sums = lax.all_to_all(sums, 'lat', 0, 0, tiled=True)  7.1 us
    ppermute x3, waiting for transfers between devices, whole(): lax.ppermute(traces[n], 'sub', [(i, i ^ n) for i in range(4)])  2.03 us
  transfers between devices with their start and end apart: 16, of which 9 were waited for; matrix products, arithmetic and copies ran while one was open for 0% of the time, Pallas kernels for 3%

profile of v2, /device:TPU:1, one launch (start us, length us, event | category | flops | bytes accessed | tf_op | source)
XLA Modules:
  0.0 93.1 jit_solution(9722768312449096030)
XLA Ops:
  0.0 0.0 copy-start.3
  0.0 0.0 copy-start.1
  0.0 1.0 %slice_bitcast_fusion.time_link = bf16[2,3,3,2,8,128]{5,4,3,2,1,0:T(8,128)(2,1)S(1)} fusion(bf16[2,4,2,3,3,2,8,128]{7,6,5,4,3,2,1,0:T(8,128)(2,1)} %links.13), kind=kLoop, calls=%fused_computation | loop fusion | bytes 147456 | tf_op jit(solution)/shard_map/squeeze | solution.py:613
  1.0 0.0 copy-done.3
  1.0 0.0 copy-start.4
  1.0 0.7 copy-done.4
  1.7 0.0 copy-start.5
  1.7 8.0 %all-gather = f32[200,2,2,128]{3,2,1,0:T(2,128)S(1)} all-gather(f32[50,2,2,128]{3,2,1,0:T(2,128)S(1)} %pack.1), channel_id=2, replica_groups=mesh['sub'=4,'lat'=32] {'sub'}, dimensions={0}, use_global_device_ids=true | all-gather | bytes 512000 | tf_op jit(solution)/shard_map/all_gather | solution.py:607
  9.7 0.0 copy-start
  9.7 0.0 copy-done.1
  9.7 0.0 copy-done.5
  9.7 0.8 start.1
  10.5 8.4 %collective-permute-start = (f32[12,8,128]{2,1,0:T(8,128)S(1)}, f32[12,8,128]{2,1,0:T(8,128)S(1)}, u32[]{:S(2)}, u32[]{:S(2)}) collective-permute-start(f32[12,8,128]{2,1,0:T(8,128)S(1)} %get-tuple-element.40), channel_id=1, source_target_pairs={{0,31},{1,2},{2,1},{3,4},{4,3},{5,6},{6,5},{7,8},{8,7},{9,10},{10,... | collective-permute-start | bytes 147464 | tf_op jit(solution)/shard_map/ppermute | solution.py:594
  18.9 0.0 collective-permute-start.1
  18.9 0.0 copy-done
  18.9 0.2 around.1
  19.0 0.9 collective-permute-start.4
  19.9 0.8 collective-permute-start.5
  20.7 1.0 %own_rhs.1 = (f32[2,24,8,128]{3,2,1,0:T(8,128)S(1)}, f32[2,24,8,128]{3,2,1,0:T(8,128)S(1)}) custom-call(s32[4]{0:T(128)S(1)} %copy-done.5, f32[4,50,2,2,128]{4,3,2,1,0:T(2,128)S(1)} %bitcast.10, f32[2,24,8,128]{3,2,1,0:T(8,128)S(1)} %get-tuple-element.38.turned._, bf16[2,4,2,3,3,2,8,128]{7,6,5,4,3,2,1,0:T(8,128)(2,1)S(1)} %copy-done), custom_call_target="tpu_custom_call" | custom-call | tf_op jit(solution)/shard_map/own_rhs/pallas_call | solution.py:574
  21.6 0.0 collective-permute-done.got_far
  21.7 0.1 collective-permute-done.1.got_near
  21.8 0.0 copy-start.2
  21.8 0.7 rhs.1
  22.5 5.8 %collective-permute-start.2 = (f32[24,8,128]{2,1,0:T(8,128)S(1)}, f32[24,8,128]{2,1,0:T(8,128)S(1)}, u32[]{:S(2)}, u32[]{:S(2)}) collective-permute-start(f32[24,8,128]{2,1,0:T(8,128)S(1)} %get-tuple-element.44.sent_far), channel_id=1, source_target_pairs={{0,31},{1,2},{2,1},{3,4},{4,3},{5,6},{6,5},{7,8},{8,7},{9,10},{10,... | collective-permute-start | bytes 294920 | tf_op jit(solution)/shard_map/ppermute | solution.py:594
  28.3 0.0 collective-permute-start.3
  28.3 0.0 copy-done.2
  28.3 0.2 direct0.1.direct
  28.5 3.3 %collective-permute-done.2.got_far = f32[24,8,128]{2,1,0:T(8,128)S(1)} collective-permute-done((f32[24,8,128]{2,1,0:T(8,128)S(1)}, f32[24,8,128]{2,1,0:T(8,128)S(1)}, u32[]{:S(2)}, u32[]{:S(2)}) %collective-permute-start.2) | collective-permute-done | bytes 98336 | tf_op jit(solution)/shard_map/ppermute | solution.py:594
  31.7 0.3 collective-permute-done.3.got_near
  32.0 0.0 collective-permute-done.4.around_far
  32.1 0.0 collective-permute-done.5.around_near
  32.1 1.3 %step0.1 = (f32[2,24,8,128]{3,2,1,0:T(8,128)S(1)}, f32[2,24,8,128]{3,2,1,0:T(8,128)S(1)}, f32[24,8,128]{2,1,0:T(8,128)S(1)}, f32[24,8,128]{2,1,0:T(8,128)S(1)}) custom-call(f32[2,24,8,128]{3,2,1,0:T(8,128)S(1)} %direct0.1.direct, f32[2,24,8,128]{3,2,1,0:T(8,128)S(1)} %get-tuple-element.43.partial, f32[24,8,128]{2,1,0:T(8,128)S(1)} %get-tuple-element.44.sent_far, ...), custom_call_target="tpu_custom_call" | custom-call | tf_op jit(solution)/shard_map/step0/pallas_call | solution.py:574
  33.4 5.5 %collective-permute-start.6 = (f32[24,8,128]{2,1,0:T(8,128)S(1)}, f32[24,8,128]{2,1,0:T(8,128)S(1)}, u32[]{:S(2)}, u32[]{:S(2)}) collective-permute-start(f32[24,8,128]{2,1,0:T(8,128)S(1)} %get-tuple-element.50.sent_far), channel_id=1, source_target_pairs={{0,31},{1,2},{2,1},{3,4},{4,3},{5,6},{6,5},{7,8},{8,7},{9,10},{10,... | collective-permute-start | bytes 294920 | tf_op jit(solution)/shard_map/ppermute | solution.py:594
  38.9 0.0 collective-permute-start.7
  38.9 0.2 direct1.1.direct
  39.1 3.6 %collective-permute-done.6.got_far = f32[24,8,128]{2,1,0:T(8,128)S(1)} collective-permute-done((f32[24,8,128]{2,1,0:T(8,128)S(1)}, f32[24,8,128]{2,1,0:T(8,128)S(1)}, u32[]{:S(2)}, u32[]{:S(2)}) %collective-permute-start.6) | collective-permute-done | bytes 98336 | tf_op jit(solution)/shard_map/ppermute | solution.py:594
  42.7 0.0 collective-permute-done.7.got_near
  42.7 1.4 %step1.1 = (f32[2,24,8,128]{3,2,1,0:T(8,128)S(1)}, f32[2,24,8,128]{3,2,1,0:T(8,128)S(1)}, f32[24,8,128]{2,1,0:T(8,128)S(1)}, f32[24,8,128]{2,1,0:T(8,128)S(1)}, f32[2,24,8,128]{3,2,1,0:T(8,128)S(1)}) custom-call(f32[2,24,8,128]{3,2,1,0:T(8,128)S(1)} %direct1.1.direct, f32[2,24,8,128]{3,2,1,0:T(8,128)S(1)} %get-tuple-element.49.partial, ...), custom_call_target="tpu_custom_call" | custom-call | tf_op jit(solution)/shard_map/step1/pallas_call | solution.py:574
  44.0 5.5 %collective-permute-start.8 = (f32[24,8,128]{2,1,0:T(8,128)S(1)}, f32[24,8,128]{2,1,0:T(8,128)S(1)}, u32[]{:S(2)}, u32[]{:S(2)}) collective-permute-start(f32[24,8,128]{2,1,0:T(8,128)S(1)} %get-tuple-element.54.sent_far), channel_id=1, source_target_pairs={{0,31},{1,2},{2,1},{3,4},{4,3},{5,6},{6,5},{7,8},{8,7},{9,10},{10,... | collective-permute-start | bytes 294920 | tf_op jit(solution)/shard_map/ppermute | solution.py:594
  49.6 0.0 collective-permute-start.9
  49.6 0.2 direct2.1.direct
  49.7 3.6 %collective-permute-done.8.got_far = f32[24,8,128]{2,1,0:T(8,128)S(1)} collective-permute-done((f32[24,8,128]{2,1,0:T(8,128)S(1)}, f32[24,8,128]{2,1,0:T(8,128)S(1)}, u32[]{:S(2)}, u32[]{:S(2)}) %collective-permute-start.8) | collective-permute-done | bytes 98336 | tf_op jit(solution)/shard_map/ppermute | solution.py:594
  53.3 0.0 collective-permute-done.9.got_near
  53.3 1.3 %step2.1 = (f32[2,24,8,128]{3,2,1,0:T(8,128)S(1)}, f32[2,24,8,128]{3,2,1,0:T(8,128)S(1)}, f32[24,8,128]{2,1,0:T(8,128)S(1)}, f32[24,8,128]{2,1,0:T(8,128)S(1)}) custom-call(f32[2,24,8,128]{3,2,1,0:T(8,128)S(1)} %direct2.1.direct, f32[2,24,8,128]{3,2,1,0:T(8,128)S(1)} %get-tuple-element.53.partial, f32[24,8,128]{2,1,0:T(8,128)S(1)} %get-tuple-element.54.sent_far, ...), custom_call_target="tpu_custom_call" | custom-call | tf_op jit(solution)/shard_map/step2/pallas_call | solution.py:574
  54.7 5.5 %collective-permute-start.10 = (f32[24,8,128]{2,1,0:T(8,128)S(1)}, f32[24,8,128]{2,1,0:T(8,128)S(1)}, u32[]{:S(2)}, u32[]{:S(2)}) collective-permute-start(f32[24,8,128]{2,1,0:T(8,128)S(1)} %get-tuple-element.58.sent_far), channel_id=1, source_target_pairs={{0,31},{1,2},{2,1},{3,4},{4,3},{5,6},{6,5},{7,8},{8,7},{9,10},{10,... | collective-permute-start | bytes 294920 | tf_op jit(solution)/shard_map/ppermute | solution.py:594
  60.2 0.0 collective-permute-start.11
  60.2 0.3 sums.1
  60.5 0.2 direct3.1.direct
  60.6 3.3 %collective-permute-done.10.got_far = f32[24,8,128]{2,1,0:T(8,128)S(1)} collective-permute-done((f32[24,8,128]{2,1,0:T(8,128)S(1)}, f32[24,8,128]{2,1,0:T(8,128)S(1)}, u32[]{:S(2)}, u32[]{:S(2)}) %collective-permute-start.10) | collective-permute-done | bytes 98336 | tf_op jit(solution)/shard_map/ppermute | solution.py:594
  63.9 0.0 collective-permute-done.11.got_near
  63.9 1.5 %last.1 = (f32[2,24,8,128]{3,2,1,0:T(8,128)S(1)}, f32[32,128]{1,0:T(8,128)}) custom-call(f32[2,24,8,128]{3,2,1,0:T(8,128)S(1)} %direct3.1.direct, f32[2,24,8,128]{3,2,1,0:T(8,128)S(1)} %get-tuple-element.57.partial, f32[24,8,128]{2,1,0:T(8,128)S(1)} %get-tuple-element.58.sent_far, f32[24,8,128]{2,1,0:T(8,128)S(1)} %get-tuple-element.59.sent_near, ...), custom_call_target="tpu_custom_call" | custom-call | tf_op jit(solution)/shard_map/last/pallas_call | solution.py:574
  65.4 7.1 %all-to-all-start = ((f32[32,1,128]{2,1,0:T(1,128)}), f32[32,1,128]{2,1,0:T(1,128)S(1)}, u32[]{:S(2)}, u32[]{:S(2)}) async-start(f32[32,1,128]{2,1,0:T(1,128)} %bitcast.4), calls=%async_computation | async-start | bytes 32768 | tf_op jit(solution)/shard_map/all_to_all | solution.py:677
  72.5 0.3 traces.1.own
  72.8 8.3 %all-to-all-done = f32[32,1,128]{2,1,0:T(1,128)S(1)} async-done(((f32[32,1,128]{2,1,0:T(1,128)}), f32[32,1,128]{2,1,0:T(1,128)S(1)}, u32[]{:S(2)}, u32[]{:S(2)}) %all-to-all-start) | async-done | bytes 16416 | tf_op jit(solution)/shard_map/all_to_all | solution.py:677
  81.1 0.4 final.1
  81.5 7.7 %collective-permute-start.12 = (f32[16,2,2,128]{3,2,1,0:T(2,128)S(1)}, f32[16,2,2,128]{3,2,1,0:T(2,128)S(1)}, u32[]{:S(2)}, u32[]{:S(2)}) collective-permute-start(f32[16,2,2,128]{3,2,1,0:T(2,128)S(1)} %get-tuple-element.68), channel_id=1, source_target_pairs={{0,96},{32,64},{64,32},{96,0},{1,97},{33,65},{65,33},{97,1},{2,98}... | collective-permute-start | bytes 98312 | tf_op jit(solution)/shard_map/ppermute | solution.py:683
  89.2 1.2 %collective-permute-start.13 = (f32[16,2,2,128]{3,2,1,0:T(2,128)S(1)}, f32[16,2,2,128]{3,2,1,0:T(2,128)S(1)}, u32[]{:S(2)}, u32[]{:S(2)}) collective-permute-start(f32[16,2,2,128]{3,2,1,0:T(2,128)S(1)} %get-tuple-element.69), channel_id=1, source_target_pairs={{0,64},{32,96},{64,0},{96,32},{1,65},{33,97},{65,1},{97,33},{2,66}... | collective-permute-start | bytes 98312 | tf_op jit(solution)/shard_map/ppermute | solution.py:683
  90.4 0.0 collective-permute-start.14
  90.4 0.4 collective-permute-done.12
  90.8 1.6 %collective-permute-done.13 = f32[16,2,2,128]{3,2,1,0:T(2,128)S(1)} collective-permute-done((f32[16,2,2,128]{3,2,1,0:T(2,128)S(1)}, f32[16,2,2,128]{3,2,1,0:T(2,128)S(1)}, u32[]{:S(2)}, u32[]{:S(2)}) %collective-permute-start.13) | collective-permute-done | bytes 32800 | tf_op jit(solution)/shard_map/ppermute | solution.py:683
  92.4 0.0 collective-permute-done.14
  92.4 0.7 add_add_fusion
  (1 shorter events, 0.0 us)
Async XLA Ops:
  0.0 1.0 %copy-start.3 = (f32[2,2,4,3,2,2,128]{6,5,4,3,2,1,0:T(2,128)S(1)}, f32[2,2,4,3,2,2,128]{6,5,4,3,2,1,0:T(2,128)}, u32[]{:S(2)}) copy-start(f32[2,2,4,3,2,2,128]{6,5,4,3,2,1,0:T(2,128)} %param.6) | copy-start | bytes 294916
  0.0 9.7 %copy-start.1 = (bf16[2,2,6,6,2,8,128]{6,5,4,3,2,1,0:T(8,128)(2,1)S(1)}, bf16[2,2,6,6,2,8,128]{6,5,4,3,2,1,0:T(8,128)(2,1)}, u32[]{:S(2)}) copy-start(bf16[2,2,6,6,2,8,128]{6,5,4,3,2,1,0:T(8,128)(2,1)} %odd_inverse.13) | copy-start | bytes 1769476
  1.0 0.7 copy-start.4
  1.7 8.0 %copy-start.5 = (s32[4]{0:T(128)S(1)}, s32[4]{0:T(128)}, u32[]{:S(2)}) copy-start(s32[4]{0:T(128)} %probe_rows.3) | copy-start | bytes 52
  9.7 9.2 %copy-start = (bf16[2,4,2,3,3,2,8,128]{7,6,5,4,3,2,1,0:T(8,128)(2,1)S(1)}, bf16[2,4,2,3,3,2,8,128]{7,6,5,4,3,2,1,0:T(8,128)(2,1)}, u32[]{:S(2)}) copy-start(bf16[2,4,2,3,3,2,8,128]{7,6,5,4,3,2,1,0:T(8,128)(2,1)} %links.13) | copy-start | bytes 1769476
  10.5 11.2 %collective-permute-start = (f32[12,8,128]{2,1,0:T(8,128)S(1)}, f32[12,8,128]{2,1,0:T(8,128)S(1)}, u32[]{:S(2)}, u32[]{:S(2)}) collective-permute-start(f32[12,8,128]{2,1,0:T(8,128)S(1)} %get-tuple-element.40), channel_id=1, source_target_pairs={{0,31},{1,2},{2,1},{3,4},{4,3},{5,6},{6,5},{7,8},{8,7},{9,10},{10,... | collective-permute-start | bytes 147464 | tf_op jit(solution)/shard_map/ppermute | solution.py:594
  18.9 2.9 %collective-permute-start.1 = (f32[12,8,128]{2,1,0:T(8,128)S(1)}, f32[12,8,128]{2,1,0:T(8,128)S(1)}, u32[]{:S(2)}, u32[]{:S(2)}) collective-permute-start(f32[12,8,128]{2,1,0:T(8,128)S(1)} %get-tuple-element.41), channel_id=1, source_target_pairs={{0,1},{1,0},{2,3},{3,2},{4,5},{5,4},{6,7},{7,6},{8,9},{9,8},{10,11... | collective-permute-start | bytes 147464 | tf_op jit(solution)/shard_map/ppermute | solution.py:595
  19.0 13.0 %collective-permute-start.4 = (f32[36,8,128]{2,1,0:T(8,128)S(1)}, f32[36,8,128]{2,1,0:T(8,128)S(1)}, u32[]{:S(2)}, u32[]{:S(2)}) collective-permute-start(f32[36,8,128]{2,1,0:T(8,128)S(1)} %get-tuple-element.46), channel_id=1, source_target_pairs={{0,31},{1,2},{2,1},{3,4},{4,3},{5,6},{6,5},{7,8},{8,7},{9,10},{10,... | collective-permute-start | bytes 442376 | tf_op jit(solution)/shard_map/ppermute | solution.py:594
  19.9 12.1 %collective-permute-start.5 = (f32[36,8,128]{2,1,0:T(8,128)S(1)}, f32[36,8,128]{2,1,0:T(8,128)S(1)}, u32[]{:S(2)}, u32[]{:S(2)}) collective-permute-start(f32[36,8,128]{2,1,0:T(8,128)S(1)} %get-tuple-element.47), channel_id=1, source_target_pairs={{0,1},{1,0},{2,3},{3,2},{4,5},{5,4},{6,7},{7,6},{8,9},{9,8},{10,11... | collective-permute-start | bytes 442376 | tf_op jit(solution)/shard_map/ppermute | solution.py:595
  21.8 6.5 %copy-start.2 = (bf16[2,2,6,6,2,8,128]{6,5,4,3,2,1,0:T(8,128)(2,1)S(1)}, bf16[2,2,6,6,2,8,128]{6,5,4,3,2,1,0:T(8,128)(2,1)}, u32[]{:S(2)}) copy-start(bf16[2,2,6,6,2,8,128]{6,5,4,3,2,1,0:T(8,128)(2,1)} %even.7) | copy-start | bytes 1769476
  22.5 9.3 %collective-permute-start.2 = (f32[24,8,128]{2,1,0:T(8,128)S(1)}, f32[24,8,128]{2,1,0:T(8,128)S(1)}, u32[]{:S(2)}, u32[]{:S(2)}) collective-permute-start(f32[24,8,128]{2,1,0:T(8,128)S(1)} %get-tuple-element.44.sent_far), channel_id=1, source_target_pairs={{0,31},{1,2},{2,1},{3,4},{4,3},{5,6},{6,5},{7,8},{8,7},{9,10},{10,... | collective-permute-start | bytes 294920 | tf_op jit(solution)/shard_map/ppermute | solution.py:594
  28.3 3.8 %collective-permute-start.3 = (f32[24,8,128]{2,1,0:T(8,128)S(1)}, f32[24,8,128]{2,1,0:T(8,128)S(1)}, u32[]{:S(2)}, u32[]{:S(2)}) collective-permute-start(f32[24,8,128]{2,1,0:T(8,128)S(1)} %get-tuple-element.45.sent_near), channel_id=1, source_target_pairs={{0,1},{1,0},{2,3},{3,2},{4,5},{5,4},{6,7},{7,6},{8,9},{9,8},{10,11... | collective-permute-start | bytes 294920 | tf_op jit(solution)/shard_map/ppermute | solution.py:595
  33.4 9.3 %collective-permute-start.6 = (f32[24,8,128]{2,1,0:T(8,128)S(1)}, f32[24,8,128]{2,1,0:T(8,128)S(1)}, u32[]{:S(2)}, u32[]{:S(2)}) collective-permute-start(f32[24,8,128]{2,1,0:T(8,128)S(1)} %get-tuple-element.50.sent_far), channel_id=1, source_target_pairs={{0,31},{1,2},{2,1},{3,4},{4,3},{5,6},{6,5},{7,8},{8,7},{9,10},{10,... | collective-permute-start | bytes 294920 | tf_op jit(solution)/shard_map/ppermute | solution.py:594
  38.9 3.8 %collective-permute-start.7 = (f32[24,8,128]{2,1,0:T(8,128)S(1)}, f32[24,8,128]{2,1,0:T(8,128)S(1)}, u32[]{:S(2)}, u32[]{:S(2)}) collective-permute-start(f32[24,8,128]{2,1,0:T(8,128)S(1)} %get-tuple-element.51.sent_near), channel_id=1, source_target_pairs={{0,1},{1,0},{2,3},{3,2},{4,5},{5,4},{6,7},{7,6},{8,9},{9,8},{10,11... | collective-permute-start | bytes 294920 | tf_op jit(solution)/shard_map/ppermute | solution.py:595
  44.0 9.3 %collective-permute-start.8 = (f32[24,8,128]{2,1,0:T(8,128)S(1)}, f32[24,8,128]{2,1,0:T(8,128)S(1)}, u32[]{:S(2)}, u32[]{:S(2)}) collective-permute-start(f32[24,8,128]{2,1,0:T(8,128)S(1)} %get-tuple-element.54.sent_far), channel_id=1, source_target_pairs={{0,31},{1,2},{2,1},{3,4},{4,3},{5,6},{6,5},{7,8},{8,7},{9,10},{10,... | collective-permute-start | bytes 294920 | tf_op jit(solution)/shard_map/ppermute | solution.py:594
  49.6 3.8 %collective-permute-start.9 = (f32[24,8,128]{2,1,0:T(8,128)S(1)}, f32[24,8,128]{2,1,0:T(8,128)S(1)}, u32[]{:S(2)}, u32[]{:S(2)}) collective-permute-start(f32[24,8,128]{2,1,0:T(8,128)S(1)} %get-tuple-element.55.sent_near), channel_id=1, source_target_pairs={{0,1},{1,0},{2,3},{3,2},{4,5},{5,4},{6,7},{7,6},{8,9},{9,8},{10,11... | collective-permute-start | bytes 294920 | tf_op jit(solution)/shard_map/ppermute | solution.py:595
  54.7 9.3 %collective-permute-start.10 = (f32[24,8,128]{2,1,0:T(8,128)S(1)}, f32[24,8,128]{2,1,0:T(8,128)S(1)}, u32[]{:S(2)}, u32[]{:S(2)}) collective-permute-start(f32[24,8,128]{2,1,0:T(8,128)S(1)} %get-tuple-element.58.sent_far), channel_id=1, source_target_pairs={{0,31},{1,2},{2,1},{3,4},{4,3},{5,6},{6,5},{7,8},{8,7},{9,10},{10,... | collective-permute-start | bytes 294920 | tf_op jit(solution)/shard_map/ppermute | solution.py:594
  60.2 3.8 %collective-permute-start.11 = (f32[24,8,128]{2,1,0:T(8,128)S(1)}, f32[24,8,128]{2,1,0:T(8,128)S(1)}, u32[]{:S(2)}, u32[]{:S(2)}) collective-permute-start(f32[24,8,128]{2,1,0:T(8,128)S(1)} %get-tuple-element.59.sent_near), channel_id=1, source_target_pairs={{0,1},{1,0},{2,3},{3,2},{4,5},{5,4},{6,7},{7,6},{8,9},{9,8},{10,11... | collective-permute-start | bytes 294920 | tf_op jit(solution)/shard_map/ppermute | solution.py:595
  65.4 15.7 %all-to-all-start = ((f32[32,1,128]{2,1,0:T(1,128)}), f32[32,1,128]{2,1,0:T(1,128)S(1)}, u32[]{:S(2)}, u32[]{:S(2)}) async-start(f32[32,1,128]{2,1,0:T(1,128)} %bitcast.4), calls=%async_computation | async-start | bytes 32768 | tf_op jit(solution)/shard_map/all_to_all | solution.py:677
  81.5 9.3 %collective-permute-start.12 = (f32[16,2,2,128]{3,2,1,0:T(2,128)S(1)}, f32[16,2,2,128]{3,2,1,0:T(2,128)S(1)}, u32[]{:S(2)}, u32[]{:S(2)}) collective-permute-start(f32[16,2,2,128]{3,2,1,0:T(2,128)S(1)} %get-tuple-element.68), channel_id=1, source_target_pairs={{0,96},{32,64},{64,32},{96,0},{1,97},{33,65},{65,33},{97,1},{2,98}... | collective-permute-start | bytes 98312 | tf_op jit(solution)/shard_map/ppermute | solution.py:683
  89.2 3.2 %collective-permute-start.13 = (f32[16,2,2,128]{3,2,1,0:T(2,128)S(1)}, f32[16,2,2,128]{3,2,1,0:T(2,128)S(1)}, u32[]{:S(2)}, u32[]{:S(2)}) collective-permute-start(f32[16,2,2,128]{3,2,1,0:T(2,128)S(1)} %get-tuple-element.69), channel_id=1, source_target_pairs={{0,64},{32,96},{64,0},{96,32},{1,65},{33,97},{65,1},{97,33},{2,66}... | collective-permute-start | bytes 98312 | tf_op jit(solution)/shard_map/ppermute | solution.py:683
  90.4 2.0 %collective-permute-start.14 = (f32[16,2,2,128]{3,2,1,0:T(2,128)S(1)}, f32[16,2,2,128]{3,2,1,0:T(2,128)S(1)}, u32[]{:S(2)}, u32[]{:S(2)}) collective-permute-start(f32[16,2,2,128]{3,2,1,0:T(2,128)S(1)} %get-tuple-element.70), channel_id=1, source_target_pairs={{0,32},{32,0},{64,96},{96,64},{1,33},{33,1},{65,97},{97,65},{2,34}... | collective-permute-start | bytes 98312 | tf_op jit(solution)/shard_map/ppermute | solution.py:683

commit v3 on v2

--- a/solution.py
+++ b/solution.py
@@ -363,7 +363,8 @@
 
 
 def unpack_probes(probe_rows, gathered, raw, parity, probes):
-    probe_row = probe_rows[lax.axis_index("sub")]
+    upper = lax.axis_index("lat") // (lax.axis_size("lat") // 2)
+    probe_row = probe_rows[jnp.bitwise_xor(lax.axis_index("sub"), 2 * upper)]
     for q in range(4):
         raw[:24, :, 2 * q : 2 * q + 2, :] = gathered[q, 24 * parity : 24 * parity + 24]
         raw[24, :, 2 * q : 2 * q + 2, :] = gathered[q, 48 + parity]
@@ -587,12 +588,23 @@
 EDGE = (24, 8, 128)
 
 
+def device_of(vector, place):
+    length = lax.axis_size("lat")
+    return (vector ^ (2 * (place // (length // 2)))) * length + place
+
+
 def swap(far, near):
-    length = lax.axis_size("lat")
-    place = range(length)
+    length, vectors = lax.axis_size("lat"), range(lax.axis_size("sub"))
+
+    def moved(array, partner):
+        pairs = [
+            (device_of(v, i), device_of(v, partner(i))) for v in vectors for i in range(length)
+        ]
+        return lax.ppermute(array, ("sub", "lat"), pairs)
+
     return (
-        lax.ppermute(far, "lat", [(i, (i + (1 if i % 2 else -1)) % length) for i in place]),
-        lax.ppermute(near, "lat", [(i, i ^ 1) for i in place]),
+        moved(far, lambda i: (i + (1 if i % 2 else -1)) % length),
+        moved(near, lambda i: i ^ 1),
     )
 
 
@@ -674,7 +686,12 @@
         (),
         (probes_even, probes_odd, turned, first, first_odd, second, second_odd),
     )
-    sums = lax.all_to_all(sums, "lat", 0, 0, tiled=True)
+    groups = [
+        [device_of(v, i) for i in range(lax.axis_size("lat"))] for v in range(lax.axis_size("sub"))
+    ]
+    sums = lax.all_to_all(
+        sums, ("sub", "lat"), 0, 0, tiled=True, axis_index_groups=groups
+    )
     traces = call(
         final_kernel, "final", ((16, 2, 2, 128),) * 4, (), (sums, own_traces)
     )

time: 93.3 us -> 91.2 us (0.977)
  starting transfers between devices: 48.4 us -> 46.6 us
    ppermute x12, starting transfers between devices: 32.4 us -> 30.9 us  [moved(): return lax.ppermute(array, ('sub', 'lat'), pairs)]
  transfers between devices with their start and end apart: 16 -> 16, of which waited for: 9 -> 8; matrix products, arithmetic and copies ran while one was open for 0% -> 0% of each run, Pallas kernels for 3% -> 3%
where the time goes in v3:
time: 91.2 us; the launch traced here: 91 us
  starting transfers between devices  46.6 us (51%)
  waiting for transfers between devices  24.2 us (27%)
  Pallas kernels  9.75 us (11%)
  blocking collectives  7.97 us (9%)
  local copies, waits for them, and re-layouts  1.66 us (2%)
    ppermute x12, starting transfers between devices, moved(): return lax.ppermute(array, ('sub', 'lat'), pairs)  30.9 us
    ppermute x12, waiting for transfers between devices, moved(): return lax.ppermute(array, ('sub', 'lat'), pairs)  14.3 us
    pallas_call x16, Pallas kernels, call(): pl.pallas_call(kernel, out_shape=tuple((jax.ShapeDtypeStruct(s, F32) for...  9.75 us
    ppermute x3, starting transfers between devices, whole(): lax.ppermute(traces[n], 'sub', [(i, i ^ n) for i in range(4)])  8.94 us
    all_gather x1, blocking collectives, whole(): gathered = lax.all_gather(own, 'sub')  7.97 us
    all_to_all x1, waiting for transfers between devices, whole(): lax.all_to_all(sums, ('sub', 'lat'), 0, 0, tiled=True, axis_index_groups=...  7.96 us
    all_to_all x1, starting transfers between devices, whole(): lax.all_to_all(sums, ('sub', 'lat'), 0, 0, tiled=True, axis_index_groups=...  6.81 us
    ppermute x3, waiting for transfers between devices, whole(): lax.ppermute(traces[n], 'sub', [(i, i ^ n) for i in range(4)])  2.03 us
  transfers between devices with their start and end apart: 16, of which 8 were waited for; matrix products, arithmetic and copies ran while one was open for 0% of the time, Pallas kernels for 3%

profile of v3, /device:TPU:1, one launch (start us, length us, event | category | flops | bytes accessed | tf_op | source)
XLA Modules:
  0.0 91.0 jit_solution(16510044948830143285)
XLA Ops:
  0.0 0.0 copy-start.3
  0.0 0.0 copy-start.1
  0.0 1.0 %slice_bitcast_fusion.time_link = bf16[2,3,3,2,8,128]{5,4,3,2,1,0:T(8,128)(2,1)S(1)} fusion(bf16[2,4,2,3,3,2,8,128]{7,6,5,4,3,2,1,0:T(8,128)(2,1)} %links.13), kind=kLoop, calls=%fused_computation | loop fusion | bytes 147456 | tf_op jit(solution)/shard_map/squeeze | solution.py:625
  1.0 0.0 copy-done.3
  1.0 0.0 copy-start.4
  1.0 0.7 copy-done.4
  1.7 0.0 copy-start.5
  1.7 8.0 %all-gather = f32[200,2,2,128]{3,2,1,0:T(2,128)S(1)} all-gather(f32[50,2,2,128]{3,2,1,0:T(2,128)S(1)} %pack.1), channel_id=2, replica_groups=mesh['sub'=4,'lat'=32] {'sub'}, dimensions={0}, use_global_device_ids=true | all-gather | bytes 512000 | tf_op jit(solution)/shard_map/all_gather | solution.py:619
  9.7 0.0 copy-start
  9.7 0.0 copy-done.1
  9.7 0.0 copy-done.5
  9.7 0.8 start.1
  10.5 8.0 %collective-permute-start = (f32[12,8,128]{2,1,0:T(8,128)S(1)}, f32[12,8,128]{2,1,0:T(8,128)S(1)}, u32[]{:S(2)}, u32[]{:S(2)}) collective-permute-start(f32[12,8,128]{2,1,0:T(8,128)S(1)} %get-tuple-element.40), channel_id=1, source_target_pairs={{0,95},{1,2},{2,1},{3,4},{4,3},{5,6},{6,5},{7,8},{8,7},{9,10},{10,... | collective-permute-start | bytes 147464 | tf_op jit(solution)/shard_map/ppermute | solution.py:603
  18.5 0.0 collective-permute-start.1
  18.5 0.0 copy-done
  18.5 0.2 around.1
  18.7 0.9 collective-permute-start.4
  19.6 0.8 collective-permute-start.5
  20.4 1.0 %own_rhs.1 = (f32[2,24,8,128]{3,2,1,0:T(8,128)S(1)}, f32[2,24,8,128]{3,2,1,0:T(8,128)S(1)}) custom-call(s32[4]{0:T(128)S(1)} %copy-done.5, f32[4,50,2,2,128]{4,3,2,1,0:T(2,128)S(1)} %bitcast.10, f32[2,24,8,128]{3,2,1,0:T(8,128)S(1)} %get-tuple-element.38.turned._, bf16[2,4,2,3,3,2,8,128]{7,6,5,4,3,2,1,0:T(8,128)(2,1)S(1)} %copy-done), custom_call_target="tpu_custom_call" | custom-call | tf_op jit(solution)/shard_map/own_rhs/pallas_call | solution.py:575
  21.3 0.0 collective-permute-done.got_far
  21.3 0.1 collective-permute-done.1.got_near
  21.5 0.0 copy-start.2
  21.5 0.7 rhs.1
  22.2 5.5 %collective-permute-start.2 = (f32[24,8,128]{2,1,0:T(8,128)S(1)}, f32[24,8,128]{2,1,0:T(8,128)S(1)}, u32[]{:S(2)}, u32[]{:S(2)}) collective-permute-start(f32[24,8,128]{2,1,0:T(8,128)S(1)} %get-tuple-element.44.sent_far), channel_id=1, source_target_pairs={{0,95},{1,2},{2,1},{3,4},{4,3},{5,6},{6,5},{7,8},{8,7},{9,10},{10,... | collective-permute-start | bytes 294920 | tf_op jit(solution)/shard_map/ppermute | solution.py:603
  27.7 0.0 collective-permute-start.3
  27.7 0.0 copy-done.2
  27.7 0.2 direct0.1.direct
  27.8 3.3 %collective-permute-done.2.got_far = f32[24,8,128]{2,1,0:T(8,128)S(1)} collective-permute-done((f32[24,8,128]{2,1,0:T(8,128)S(1)}, f32[24,8,128]{2,1,0:T(8,128)S(1)}, u32[]{:S(2)}, u32[]{:S(2)}) %collective-permute-start.2) | collective-permute-done | bytes 98336 | tf_op jit(solution)/shard_map/ppermute | solution.py:603
  31.1 0.3 collective-permute-done.3.got_near
  31.4 0.0 collective-permute-done.4.around_far
  31.4 0.0 collective-permute-done.5.around_near
  31.4 1.3 %step0.1 = (f32[2,24,8,128]{3,2,1,0:T(8,128)S(1)}, f32[2,24,8,128]{3,2,1,0:T(8,128)S(1)}, f32[24,8,128]{2,1,0:T(8,128)S(1)}, f32[24,8,128]{2,1,0:T(8,128)S(1)}) custom-call(f32[2,24,8,128]{3,2,1,0:T(8,128)S(1)} %direct0.1.direct, f32[2,24,8,128]{3,2,1,0:T(8,128)S(1)} %get-tuple-element.43.partial, f32[24,8,128]{2,1,0:T(8,128)S(1)} %get-tuple-element.44.sent_far, ...), custom_call_target="tpu_custom_call" | custom-call | tf_op jit(solution)/shard_map/step0/pallas_call | solution.py:575
  32.8 5.2 %collective-permute-start.6 = (f32[24,8,128]{2,1,0:T(8,128)S(1)}, f32[24,8,128]{2,1,0:T(8,128)S(1)}, u32[]{:S(2)}, u32[]{:S(2)}) collective-permute-start(f32[24,8,128]{2,1,0:T(8,128)S(1)} %get-tuple-element.50.sent_far), channel_id=1, source_target_pairs={{0,95},{1,2},{2,1},{3,4},{4,3},{5,6},{6,5},{7,8},{8,7},{9,10},{10,... | collective-permute-start | bytes 294920 | tf_op jit(solution)/shard_map/ppermute | solution.py:603
  38.0 0.0 collective-permute-start.7
  38.0 0.2 direct1.1.direct
  38.2 3.6 %collective-permute-done.6.got_far = f32[24,8,128]{2,1,0:T(8,128)S(1)} collective-permute-done((f32[24,8,128]{2,1,0:T(8,128)S(1)}, f32[24,8,128]{2,1,0:T(8,128)S(1)}, u32[]{:S(2)}, u32[]{:S(2)}) %collective-permute-start.6) | collective-permute-done | bytes 98336 | tf_op jit(solution)/shard_map/ppermute | solution.py:603
  41.8 0.0 collective-permute-done.7.got_near
  41.8 1.4 %step1.1 = (f32[2,24,8,128]{3,2,1,0:T(8,128)S(1)}, f32[2,24,8,128]{3,2,1,0:T(8,128)S(1)}, f32[24,8,128]{2,1,0:T(8,128)S(1)}, f32[24,8,128]{2,1,0:T(8,128)S(1)}, f32[2,24,8,128]{3,2,1,0:T(8,128)S(1)}) custom-call(f32[2,24,8,128]{3,2,1,0:T(8,128)S(1)} %direct1.1.direct, f32[2,24,8,128]{3,2,1,0:T(8,128)S(1)} %get-tuple-element.49.partial, ...), custom_call_target="tpu_custom_call" | custom-call | tf_op jit(solution)/shard_map/step1/pallas_call | solution.py:575
  43.1 5.2 %collective-permute-start.8 = (f32[24,8,128]{2,1,0:T(8,128)S(1)}, f32[24,8,128]{2,1,0:T(8,128)S(1)}, u32[]{:S(2)}, u32[]{:S(2)}) collective-permute-start(f32[24,8,128]{2,1,0:T(8,128)S(1)} %get-tuple-element.54.sent_far), channel_id=1, source_target_pairs={{0,95},{1,2},{2,1},{3,4},{4,3},{5,6},{6,5},{7,8},{8,7},{9,10},{10,... | collective-permute-start | bytes 294920 | tf_op jit(solution)/shard_map/ppermute | solution.py:603
  48.3 0.0 collective-permute-start.9
  48.4 0.2 direct2.1.direct
  48.5 3.6 %collective-permute-done.8.got_far = f32[24,8,128]{2,1,0:T(8,128)S(1)} collective-permute-done((f32[24,8,128]{2,1,0:T(8,128)S(1)}, f32[24,8,128]{2,1,0:T(8,128)S(1)}, u32[]{:S(2)}, u32[]{:S(2)}) %collective-permute-start.8) | collective-permute-done | bytes 98336 | tf_op jit(solution)/shard_map/ppermute | solution.py:603
  52.1 0.0 collective-permute-done.9.got_near
  52.1 1.3 %step2.1 = (f32[2,24,8,128]{3,2,1,0:T(8,128)S(1)}, f32[2,24,8,128]{3,2,1,0:T(8,128)S(1)}, f32[24,8,128]{2,1,0:T(8,128)S(1)}, f32[24,8,128]{2,1,0:T(8,128)S(1)}) custom-call(f32[2,24,8,128]{3,2,1,0:T(8,128)S(1)} %direct2.1.direct, f32[2,24,8,128]{3,2,1,0:T(8,128)S(1)} %get-tuple-element.53.partial, f32[24,8,128]{2,1,0:T(8,128)S(1)} %get-tuple-element.54.sent_far, ...), custom_call_target="tpu_custom_call" | custom-call | tf_op jit(solution)/shard_map/step2/pallas_call | solution.py:575
  53.5 5.2 %collective-permute-start.10 = (f32[24,8,128]{2,1,0:T(8,128)S(1)}, f32[24,8,128]{2,1,0:T(8,128)S(1)}, u32[]{:S(2)}, u32[]{:S(2)}) collective-permute-start(f32[24,8,128]{2,1,0:T(8,128)S(1)} %get-tuple-element.58.sent_far), channel_id=1, source_target_pairs={{0,95},{1,2},{2,1},{3,4},{4,3},{5,6},{6,5},{7,8},{8,7},{9,10},{10,... | collective-permute-start | bytes 294920 | tf_op jit(solution)/shard_map/ppermute | solution.py:603
  58.7 0.0 collective-permute-start.11
  58.7 0.3 sums.1
  59.0 0.2 direct3.1.direct
  59.1 3.3 %collective-permute-done.10.got_far = f32[24,8,128]{2,1,0:T(8,128)S(1)} collective-permute-done((f32[24,8,128]{2,1,0:T(8,128)S(1)}, f32[24,8,128]{2,1,0:T(8,128)S(1)}, u32[]{:S(2)}, u32[]{:S(2)}) %collective-permute-start.10) | collective-permute-done | bytes 98336 | tf_op jit(solution)/shard_map/ppermute | solution.py:603
  62.4 0.0 collective-permute-done.11.got_near
  62.4 1.5 %last.1 = (f32[2,24,8,128]{3,2,1,0:T(8,128)S(1)}, f32[32,128]{1,0:T(8,128)}) custom-call(f32[2,24,8,128]{3,2,1,0:T(8,128)S(1)} %direct3.1.direct, f32[2,24,8,128]{3,2,1,0:T(8,128)S(1)} %get-tuple-element.57.partial, f32[24,8,128]{2,1,0:T(8,128)S(1)} %get-tuple-element.58.sent_far, f32[24,8,128]{2,1,0:T(8,128)S(1)} %get-tuple-element.59.sent_near, ...), custom_call_target="tpu_custom_call" | custom-call | tf_op jit(solution)/shard_map/last/pallas_call | solution.py:575
  63.9 6.8 %all-to-all-start = ((f32[32,1,128]{2,1,0:T(1,128)}), f32[32,1,128]{2,1,0:T(1,128)S(1)}, u32[]{:S(2)}, u32[]{:S(2)}) async-start(f32[32,1,128]{2,1,0:T(1,128)} %bitcast.4), calls=%async_computation | async-start | bytes 32768 | tf_op jit(solution)/shard_map/all_to_all | solution.py:692
  70.7 0.3 traces.1.own
  71.0 8.0 %all-to-all-done = f32[32,1,128]{2,1,0:T(1,128)S(1)} async-done(((f32[32,1,128]{2,1,0:T(1,128)}), f32[32,1,128]{2,1,0:T(1,128)S(1)}, u32[]{:S(2)}, u32[]{:S(2)}) %all-to-all-start) | async-done | bytes 16416 | tf_op jit(solution)/shard_map/all_to_all | solution.py:692
  79.0 0.4 final.1
  79.4 0.2 collective-permute-start.12
  79.6 8.7 %collective-permute-start.13 = (f32[16,2,2,128]{3,2,1,0:T(2,128)S(1)}, f32[16,2,2,128]{3,2,1,0:T(2,128)S(1)}, u32[]{:S(2)}, u32[]{:S(2)}) collective-permute-start(f32[16,2,2,128]{3,2,1,0:T(2,128)S(1)} %get-tuple-element.69), channel_id=1, source_target_pairs={{0,64},{32,96},{64,0},{96,32},{1,65},{33,97},{65,1},{97,33},{2,66}... | collective-permute-start | bytes 98312 | tf_op jit(solution)/shard_map/ppermute | solution.py:700
  88.3 0.0 collective-permute-start.14
  88.3 0.0 collective-permute-done.12
  88.3 2.0 %collective-permute-done.13 = f32[16,2,2,128]{3,2,1,0:T(2,128)S(1)} collective-permute-done((f32[16,2,2,128]{3,2,1,0:T(2,128)S(1)}, f32[16,2,2,128]{3,2,1,0:T(2,128)S(1)}, u32[]{:S(2)}, u32[]{:S(2)}) %collective-permute-start.13) | collective-permute-done | bytes 32800 | tf_op jit(solution)/shard_map/ppermute | solution.py:700
  90.4 0.0 collective-permute-done.14
  90.4 0.7 add_add_fusion
  (1 shorter events, 0.0 us)
Async XLA Ops:
  0.0 1.0 %copy-start.3 = (f32[2,2,4,3,2,2,128]{6,5,4,3,2,1,0:T(2,128)S(1)}, f32[2,2,4,3,2,2,128]{6,5,4,3,2,1,0:T(2,128)}, u32[]{:S(2)}) copy-start(f32[2,2,4,3,2,2,128]{6,5,4,3,2,1,0:T(2,128)} %param.6) | copy-start | bytes 294916
  0.0 9.7 %copy-start.1 = (bf16[2,2,6,6,2,8,128]{6,5,4,3,2,1,0:T(8,128)(2,1)S(1)}, bf16[2,2,6,6,2,8,128]{6,5,4,3,2,1,0:T(8,128)(2,1)}, u32[]{:S(2)}) copy-start(bf16[2,2,6,6,2,8,128]{6,5,4,3,2,1,0:T(8,128)(2,1)} %odd_inverse.13) | copy-start | bytes 1769476
  1.0 0.7 copy-start.4
  1.7 8.0 %copy-start.5 = (s32[4]{0:T(128)S(1)}, s32[4]{0:T(128)}, u32[]{:S(2)}) copy-start(s32[4]{0:T(128)} %probe_rows.3) | copy-start | bytes 52
  9.7 8.9 %copy-start = (bf16[2,4,2,3,3,2,8,128]{7,6,5,4,3,2,1,0:T(8,128)(2,1)S(1)}, bf16[2,4,2,3,3,2,8,128]{7,6,5,4,3,2,1,0:T(8,128)(2,1)}, u32[]{:S(2)}) copy-start(bf16[2,4,2,3,3,2,8,128]{7,6,5,4,3,2,1,0:T(8,128)(2,1)} %links.13) | copy-start | bytes 1769476
  10.5 10.8 %collective-permute-start = (f32[12,8,128]{2,1,0:T(8,128)S(1)}, f32[12,8,128]{2,1,0:T(8,128)S(1)}, u32[]{:S(2)}, u32[]{:S(2)}) collective-permute-start(f32[12,8,128]{2,1,0:T(8,128)S(1)} %get-tuple-element.40), channel_id=1, source_target_pairs={{0,95},{1,2},{2,1},{3,4},{4,3},{5,6},{6,5},{7,8},{8,7},{9,10},{10,... | collective-permute-start | bytes 147464 | tf_op jit(solution)/shard_map/ppermute | solution.py:603
  18.5 2.9 %collective-permute-start.1 = (f32[12,8,128]{2,1,0:T(8,128)S(1)}, f32[12,8,128]{2,1,0:T(8,128)S(1)}, u32[]{:S(2)}, u32[]{:S(2)}) collective-permute-start(f32[12,8,128]{2,1,0:T(8,128)S(1)} %get-tuple-element.41), channel_id=1, source_target_pairs={{0,1},{1,0},{2,3},{3,2},{4,5},{5,4},{6,7},{7,6},{8,9},{9,8},{10,11... | collective-permute-start | bytes 147464 | tf_op jit(solution)/shard_map/ppermute | solution.py:603
  18.7 12.7 %collective-permute-start.4 = (f32[36,8,128]{2,1,0:T(8,128)S(1)}, f32[36,8,128]{2,1,0:T(8,128)S(1)}, u32[]{:S(2)}, u32[]{:S(2)}) collective-permute-start(f32[36,8,128]{2,1,0:T(8,128)S(1)} %get-tuple-element.46), channel_id=1, source_target_pairs={{0,95},{1,2},{2,1},{3,4},{4,3},{5,6},{6,5},{7,8},{8,7},{9,10},{10,... | collective-permute-start | bytes 442376 | tf_op jit(solution)/shard_map/ppermute | solution.py:603
  19.6 11.8 %collective-permute-start.5 = (f32[36,8,128]{2,1,0:T(8,128)S(1)}, f32[36,8,128]{2,1,0:T(8,128)S(1)}, u32[]{:S(2)}, u32[]{:S(2)}) collective-permute-start(f32[36,8,128]{2,1,0:T(8,128)S(1)} %get-tuple-element.47), channel_id=1, source_target_pairs={{0,1},{1,0},{2,3},{3,2},{4,5},{5,4},{6,7},{7,6},{8,9},{9,8},{10,11... | collective-permute-start | bytes 442376 | tf_op jit(solution)/shard_map/ppermute | solution.py:603
  21.5 6.2 %copy-start.2 = (bf16[2,2,6,6,2,8,128]{6,5,4,3,2,1,0:T(8,128)(2,1)S(1)}, bf16[2,2,6,6,2,8,128]{6,5,4,3,2,1,0:T(8,128)(2,1)}, u32[]{:S(2)}) copy-start(bf16[2,2,6,6,2,8,128]{6,5,4,3,2,1,0:T(8,128)(2,1)} %even.7) | copy-start | bytes 1769476
  22.2 9.0 %collective-permute-start.2 = (f32[24,8,128]{2,1,0:T(8,128)S(1)}, f32[24,8,128]{2,1,0:T(8,128)S(1)}, u32[]{:S(2)}, u32[]{:S(2)}) collective-permute-start(f32[24,8,128]{2,1,0:T(8,128)S(1)} %get-tuple-element.44.sent_far), channel_id=1, source_target_pairs={{0,95},{1,2},{2,1},{3,4},{4,3},{5,6},{6,5},{7,8},{8,7},{9,10},{10,... | collective-permute-start | bytes 294920 | tf_op jit(solution)/shard_map/ppermute | solution.py:603
  27.7 3.8 %collective-permute-start.3 = (f32[24,8,128]{2,1,0:T(8,128)S(1)}, f32[24,8,128]{2,1,0:T(8,128)S(1)}, u32[]{:S(2)}, u32[]{:S(2)}) collective-permute-start(f32[24,8,128]{2,1,0:T(8,128)S(1)} %get-tuple-element.45.sent_near), channel_id=1, source_target_pairs={{0,1},{1,0},{2,3},{3,2},{4,5},{5,4},{6,7},{7,6},{8,9},{9,8},{10,11... | collective-permute-start | bytes 294920 | tf_op jit(solution)/shard_map/ppermute | solution.py:603
  32.8 9.0 %collective-permute-start.6 = (f32[24,8,128]{2,1,0:T(8,128)S(1)}, f32[24,8,128]{2,1,0:T(8,128)S(1)}, u32[]{:S(2)}, u32[]{:S(2)}) collective-permute-start(f32[24,8,128]{2,1,0:T(8,128)S(1)} %get-tuple-element.50.sent_far), channel_id=1, source_target_pairs={{0,95},{1,2},{2,1},{3,4},{4,3},{5,6},{6,5},{7,8},{8,7},{9,10},{10,... | collective-permute-start | bytes 294920 | tf_op jit(solution)/shard_map/ppermute | solution.py:603
  38.0 3.8 %collective-permute-start.7 = (f32[24,8,128]{2,1,0:T(8,128)S(1)}, f32[24,8,128]{2,1,0:T(8,128)S(1)}, u32[]{:S(2)}, u32[]{:S(2)}) collective-permute-start(f32[24,8,128]{2,1,0:T(8,128)S(1)} %get-tuple-element.51.sent_near), channel_id=1, source_target_pairs={{0,1},{1,0},{2,3},{3,2},{4,5},{5,4},{6,7},{7,6},{8,9},{9,8},{10,11... | collective-permute-start | bytes 294920 | tf_op jit(solution)/shard_map/ppermute | solution.py:603
  43.1 9.0 %collective-permute-start.8 = (f32[24,8,128]{2,1,0:T(8,128)S(1)}, f32[24,8,128]{2,1,0:T(8,128)S(1)}, u32[]{:S(2)}, u32[]{:S(2)}) collective-permute-start(f32[24,8,128]{2,1,0:T(8,128)S(1)} %get-tuple-element.54.sent_far), channel_id=1, source_target_pairs={{0,95},{1,2},{2,1},{3,4},{4,3},{5,6},{6,5},{7,8},{8,7},{9,10},{10,... | collective-permute-start | bytes 294920 | tf_op jit(solution)/shard_map/ppermute | solution.py:603
  48.3 3.8 %collective-permute-start.9 = (f32[24,8,128]{2,1,0:T(8,128)S(1)}, f32[24,8,128]{2,1,0:T(8,128)S(1)}, u32[]{:S(2)}, u32[]{:S(2)}) collective-permute-start(f32[24,8,128]{2,1,0:T(8,128)S(1)} %get-tuple-element.55.sent_near), channel_id=1, source_target_pairs={{0,1},{1,0},{2,3},{3,2},{4,5},{5,4},{6,7},{7,6},{8,9},{9,8},{10,11... | collective-permute-start | bytes 294920 | tf_op jit(solution)/shard_map/ppermute | solution.py:603
  53.5 9.0 %collective-permute-start.10 = (f32[24,8,128]{2,1,0:T(8,128)S(1)}, f32[24,8,128]{2,1,0:T(8,128)S(1)}, u32[]{:S(2)}, u32[]{:S(2)}) collective-permute-start(f32[24,8,128]{2,1,0:T(8,128)S(1)} %get-tuple-element.58.sent_far), channel_id=1, source_target_pairs={{0,95},{1,2},{2,1},{3,4},{4,3},{5,6},{6,5},{7,8},{8,7},{9,10},{10,... | collective-permute-start | bytes 294920 | tf_op jit(solution)/shard_map/ppermute | solution.py:603
  58.7 3.8 %collective-permute-start.11 = (f32[24,8,128]{2,1,0:T(8,128)S(1)}, f32[24,8,128]{2,1,0:T(8,128)S(1)}, u32[]{:S(2)}, u32[]{:S(2)}) collective-permute-start(f32[24,8,128]{2,1,0:T(8,128)S(1)} %get-tuple-element.59.sent_near), channel_id=1, source_target_pairs={{0,1},{1,0},{2,3},{3,2},{4,5},{5,4},{6,7},{7,6},{8,9},{9,8},{10,11... | collective-permute-start | bytes 294920 | tf_op jit(solution)/shard_map/ppermute | solution.py:603
  63.9 15.1 %all-to-all-start = ((f32[32,1,128]{2,1,0:T(1,128)}), f32[32,1,128]{2,1,0:T(1,128)S(1)}, u32[]{:S(2)}, u32[]{:S(2)}) async-start(f32[32,1,128]{2,1,0:T(1,128)} %bitcast.4), calls=%async_computation | async-start | bytes 32768 | tf_op jit(solution)/shard_map/all_to_all | solution.py:692
  79.4 8.9 %collective-permute-start.12 = (f32[16,2,2,128]{3,2,1,0:T(2,128)S(1)}, f32[16,2,2,128]{3,2,1,0:T(2,128)S(1)}, u32[]{:S(2)}, u32[]{:S(2)}) collective-permute-start(f32[16,2,2,128]{3,2,1,0:T(2,128)S(1)} %get-tuple-element.68), channel_id=1, source_target_pairs={{0,96},{32,64},{64,32},{96,0},{1,97},{33,65},{65,33},{97,1},{2,98}... | collective-permute-start | bytes 98312 | tf_op jit(solution)/shard_map/ppermute | solution.py:700
  79.6 10.8 %collective-permute-start.13 = (f32[16,2,2,128]{3,2,1,0:T(2,128)S(1)}, f32[16,2,2,128]{3,2,1,0:T(2,128)S(1)}, u32[]{:S(2)}, u32[]{:S(2)}) collective-permute-start(f32[16,2,2,128]{3,2,1,0:T(2,128)S(1)} %get-tuple-element.69), channel_id=1, source_target_pairs={{0,64},{32,96},{64,0},{96,32},{1,65},{33,97},{65,1},{97,33},{2,66}... | collective-permute-start | bytes 98312 | tf_op jit(solution)/shard_map/ppermute | solution.py:700
  88.3 2.0 %collective-permute-start.14 = (f32[16,2,2,128]{3,2,1,0:T(2,128)S(1)}, f32[16,2,2,128]{3,2,1,0:T(2,128)S(1)}, u32[]{:S(2)}, u32[]{:S(2)}) collective-permute-start(f32[16,2,2,128]{3,2,1,0:T(2,128)S(1)} %get-tuple-element.70), channel_id=1, source_target_pairs={{0,32},{32,0},{64,96},{96,64},{1,33},{33,1},{65,97},{97,65},{2,34}... | collective-permute-start | bytes 98312 | tf_op jit(solution)/shard_map/ppermute | solution.py:700

commit v4 on v3

--- a/solution.py
+++ b/solution.py
@@ -362,9 +362,13 @@
     out[48:] = colours[...].astype(F32)
 
 
+def vector_index():
+    upper = lax.axis_index("lat") // (lax.axis_size("lat") // 2)
+    return jnp.bitwise_xor(lax.axis_index("sub"), 2 * upper)
+
+
 def unpack_probes(probe_rows, gathered, raw, parity, probes):
-    upper = lax.axis_index("lat") // (lax.axis_size("lat") // 2)
-    probe_row = probe_rows[jnp.bitwise_xor(lax.axis_index("sub"), 2 * upper)]
+    probe_row = probe_rows[vector_index()]
     for q in range(4):
         raw[:24, :, 2 * q : 2 * q + 2, :] = gathered[q, 24 * parity : 24 * parity + 24]
         raw[24, :, 2 * q : 2 * q + 2, :] = gathered[q, 48 + parity]
@@ -460,18 +464,31 @@
     return [columns[hop_dir][part] for part in range(2) for hop_dir in range(4)]
 
 
-def store_traces(out, place, probes, field, time):
+def store_traces(outs, base, probes, field, time):
+    core, chip = lax.rem(lax.axis_index("sub"), 2), lax.axis_index("sub") // 2
     for n, value in enumerate(traces_at(load_spinor(probes, time), load_spinor(field, time))):
-        out[place, n, time] = value
-
-
-def traces_kernel(probes_even, probes_odd, turned, first, first_odd, second, second_odd, out):
-    for time in range(2):
-        store_traces(out, 0, probes_even, first, time)
-        store_traces(out, 1, probes_even, second, time)
-        store_traces(out, 2, probes_odd, turned, time)
-        store_traces(out, 3, probes_odd, first_odd, time)
-        store_traces(out, 4, probes_odd, second_odd, time)
+        quarters = [value[2 * q : 2 * q + 2] for q in range(4)]
+        for low in range(2):
+            halves = [
+                lax.select(core != low, quarters[2 * q + 1], quarters[2 * q]) for q in range(2)
+            ]
+            for high in range(2):
+                outs[2 * high + low][base + n, time] = lax.select(
+                    chip != high, halves[1], halves[0]
+                )
+
+
+def traces_kernel(probes_even, probes_odd, turned, first, first_odd, second, *outs):
+    for time in range(2):
+        store_traces(outs, 0, probes_even, first, time)
+        store_traces(outs, 8, probes_even, second, time)
+        store_traces(outs, 16, probes_odd, first_odd, time)
+        store_traces(outs, 24, probes_odd, turned, time)
+
+
+def last_traces_kernel(probes_odd, second_odd, *outs):
+    for time in range(2):
+        store_traces(outs, 0, probes_odd, second_odd, time)
 
 
 def in_lanes(row, values):
@@ -525,9 +542,7 @@
     )
 
 
-def final_kernel(sums, own, *outs):
-    core, chip = lax.rem(lax.axis_index("sub"), 2), lax.axis_index("sub") // 2
-    table = sums[...]
+def factors(table):
     first_lane = lax.broadcasted_iota(jnp.int32, table.shape, 1) == 0
     norm, crossed, about, rest, rest_first, image_rest, image_cross, image_norm = [
         table if n == 0 else pltpu.roll(table, 128 - n, 1) for n in range(8)
@@ -545,25 +560,47 @@
         image_rest + 2.0 * off * image_cross + off * off * image_norm
     )
     alpha_next = norm_next / curved
-    of_first = jnp.broadcast_to(alpha + alpha_next * (1.0 + beta), (8, 128))
-    of_second = jnp.broadcast_to(-alpha * alpha_next, (8, 128))
+    return [
+        jnp.broadcast_to(value, (2, 128))
+        for value in (alpha + alpha_next * (1.0 + beta), -alpha * alpha_next)
+    ]
+
+
+def final_kernel(sums, *refs):
+    early, late, out = refs[:4], refs[4:8], refs[8]
+    length = lax.axis_size("lat")
+    half = length // 2
+    by_vector = []
+    for vector in range(4):
+        lower = sums[vector * length : vector * length + half]
+        upper = sums[(vector ^ 2) * length + half : (vector ^ 2) * length + length]
+        by_vector.append(factors(jnp.concatenate([lower, upper], axis=0)))
+    mine = vector_index()
+    core, chip = lax.rem(mine, 2), mine // 2
+    weights = []
+    for peer in range(4):
+        weights.append([])
+        for n in range(2):
+            halves = [
+                lax.select(
+                    core != peer % 2, by_vector[2 * q + 1][n], by_vector[2 * q][n]
+                )
+                for q in range(2)
+            ]
+            weights[-1].append(lax.select(chip != peer // 2, halves[1], halves[0]))
     for time in range(2):
         for n in range(8):
-            even = of_first * own[0, n, time] + of_second * own[1, n, time]
-            odd = own[2, n, time] + KAPPA * (
-                of_first * own[3, n, time] + of_second * own[4, n, time]
-            )
-            for place, value in ((n, even), (8 + n, odd)):
-                quarters = [value[2 * q : 2 * q + 2] for q in range(4)]
-                for low in range(2):
-                    halves = [
-                        lax.select(core != low, quarters[2 * q + 1], quarters[2 * q])
-                        for q in range(2)
-                    ]
-                    for high in range(2):
-                        outs[2 * high + low][place, time] = lax.select(
-                            chip != high, halves[1], halves[0]
-                        )
+            even = odd = plain = None
+            for peer, (of_first, of_second) in enumerate(weights):
+                ref, last = early[peer], late[peer]
+                even_part = of_first * ref[n, time] + of_second * ref[8 + n, time]
+                odd_part = of_first * ref[16 + n, time] + of_second * last[n, time]
+                plain_part = ref[24 + n, time]
+                even = even_part if even is None else even + even_part
+                odd = odd_part if odd is None else odd + odd_part
+                plain = plain_part if plain is None else plain + plain_part
+            out[n, time] = even
+            out[8 + n, time] = plain + KAPPA * odd
 
 
 VMEM = pl.BlockSpec(memory_space=pltpu.VMEM)
@@ -606,6 +643,13 @@
         moved(far, lambda i: (i + (1 if i % 2 else -1)) % length),
         moved(near, lambda i: i ^ 1),
     )
+
+
+def swap_depths(traces):
+    subs = range(lax.axis_size("sub"))
+    return [traces[0]] + [
+        lax.ppermute(traces[n], "sub", [(i, i ^ n) for i in subs]) for n in (1, 2, 3)
+    ]
 
 
 def whole(noise, colours, probe_rows, links, even, odd_inverse):
@@ -671,34 +715,30 @@
     row, about = call(
         sums_kernel, "sums", ((1, 128), (8, 128)), (), (first, image, second)
     )
+    early = swap_depths(
+        call(
+            traces_kernel,
+            "traces",
+            ((32, 2, 2, 128),) * 4,
+            (),
+            (probes_even, probes_odd, turned, first, first_odd, second),
+        )
+    )
+    devices = lax.axis_size("lat") * lax.axis_size("sub")
     second_odd, sums = call(
         last_kernel,
         "last",
-        (FIELD, (lax.axis_size("lat"), 128)),
+        (FIELD, (devices, 128)),
         (),
         (direct, odd, *sent, *got, *around, links, odd_inverse, image, row, about),
         (FIELD,),
     )
-    (own_traces,) = call(
-        traces_kernel,
-        "traces",
-        ((5, 8, 2, 8, 128),),
-        (),
-        (probes_even, probes_odd, turned, first, first_odd, second, second_odd),
-    )
-    groups = [
-        [device_of(v, i) for i in range(lax.axis_size("lat"))] for v in range(lax.axis_size("sub"))
-    ]
-    sums = lax.all_to_all(
-        sums, ("sub", "lat"), 0, 0, tiled=True, axis_index_groups=groups
-    )
-    traces = call(
-        final_kernel, "final", ((16, 2, 2, 128),) * 4, (), (sums, own_traces)
-    )
-    total = traces[0]
-    for n in (3, 2, 1):
-        total = total + lax.ppermute(traces[n], "sub", [(i, i ^ n) for i in range(4)])
-    return total.reshape(2, 2, 4, 2, 2, 128)
+    sums = lax.all_to_all(sums, ("sub", "lat"), 0, 0, tiled=True)
+    late = swap_depths(
+        call(last_traces_kernel, "last_traces", ((8, 2, 2, 128),) * 4, (), (probes_odd, second_odd))
+    )
+    (out,) = call(final_kernel, "final", ((16, 2, 2, 128),), (), (sums, *early, *late))
+    return out.reshape(2, 2, 4, 2, 2, 128)
 
 
 def solution(mesh):

time: 91.2 us -> 87.3 us (0.957)
  waiting for transfers between devices: 24.2 us -> 17.7 us
  starting transfers between devices: 46.6 us -> 49.1 us
    all_to_all x1, waiting for transfers between devices: 7.96 us -> 4.29 us  [whole(): sums = lax.all_to_all(sums, ('sub', 'lat'), 0, 0, tiled=True)]
    ppermute x12, waiting for transfers between devices: 14.3 us -> 10.9 us  [moved(): return lax.ppermute(array, ('sub', 'lat'), pairs)]
    all_to_all x1, starting transfers between devices: 6.81 us -> 8.32 us  [whole(): sums = lax.all_to_all(sums, ('sub', 'lat'), 0, 0, tiled=True)]
    ppermute x3 -> x6, starting transfers between devices: 8.94 us -> 9.88 us  [swap_depths(): lax.ppermute(traces[n], 'sub', [(i, i ^ n) for i in subs])]
    pallas_call x16 -> x17, Pallas kernels: 9.75 us -> 10.6 us  [call(): pl.pallas_call(kernel, out_shape=tuple((jax.ShapeDtypeStruct(s, F32) for...]
    ppermute x3 -> x6, waiting for transfers between devices: 2.03 us -> 2.46 us  [swap_depths(): lax.ppermute(traces[n], 'sub', [(i, i ^ n) for i in subs])]
  transfers between devices with their start and end apart: 16 -> 19, of which waited for: 8 -> 8; matrix products, arithmetic and copies ran while one was open for 0% -> 0% of each run, Pallas kernels for 3% -> 5%
where the time goes in v4:
time: 87.3 us; the launch traced here: 87.1 us
  starting transfers between devices  49.1 us (56%)
  waiting for transfers between devices  17.7 us (20%)
  Pallas kernels  10.6 us (12%)
  blocking collectives  7.97 us (9%)
  local copies, waits for them, and re-layouts  1.66 us (2%)
    ppermute x12, starting transfers between devices, moved(): return lax.ppermute(array, ('sub', 'lat'), pairs)  30.9 us
    ppermute x12, waiting for transfers between devices, moved(): return lax.ppermute(array, ('sub', 'lat'), pairs)  10.9 us
    pallas_call x17, Pallas kernels, call(): pl.pallas_call(kernel, out_shape=tuple((jax.ShapeDtypeStruct(s, F32) for...  10.6 us
    ppermute x6, starting transfers between devices, swap_depths(): lax.ppermute(traces[n], 'sub', [(i, i ^ n) for i in subs])  9.88 us
    all_to_all x1, starting transfers between devices, whole(): sums = lax.all_to_all(sums, ('sub', 'lat'), 0, 0, tiled=True)  8.32 us
    all_gather x1, blocking collectives, whole(): gathered = lax.all_gather(own, 'sub')  7.97 us
    all_to_all x1, waiting for transfers between devices, whole(): sums = lax.all_to_all(sums, ('sub', 'lat'), 0, 0, tiled=True)  4.29 us
    ppermute x6, waiting for transfers between devices, swap_depths(): lax.ppermute(traces[n], 'sub', [(i, i ^ n) for i in subs])  2.46 us
  transfers between devices with their start and end apart: 19, of which 8 were waited for; matrix products, arithmetic and copies ran while one was open for 0% of the time, Pallas kernels for 5%

profile of v4, /device:TPU:1, one launch (start us, length us, event | category | flops | bytes accessed | tf_op | source)
XLA Modules:
  0.0 87.1 jit_solution(6972878618759241187)
XLA Ops:
  0.0 0.0 copy-start.3
  0.0 1.0 %slice_bitcast_fusion.time_link = bf16[2,3,3,2,8,128]{5,4,3,2,1,0:T(8,128)(2,1)S(1)} fusion(bf16[2,4,2,3,3,2,8,128]{7,6,5,4,3,2,1,0:T(8,128)(2,1)} %links.13), kind=kLoop, calls=%fused_computation | loop fusion | bytes 147456 | tf_op jit(solution)/shard_map/squeeze | solution.py:669
  1.0 0.0 copy-done.3
  1.0 0.7 copy-done.4
  1.7 0.0 copy-start.5
  1.7 8.0 %all-gather = f32[200,2,2,128]{3,2,1,0:T(2,128)S(1)} all-gather(f32[50,2,2,128]{3,2,1,0:T(2,128)S(1)} %pack.1), channel_id=2, replica_groups=mesh['sub'=4,'lat'=32] {'sub'}, dimensions={0}, use_global_device_ids=true | all-gather | bytes 512000 | tf_op jit(solution)/shard_map/all_gather | solution.py:663
  9.7 0.0 copy-done.1
  9.7 0.0 copy-done.5
  9.7 0.8 start.1
  10.5 8.0 %collective-permute-start = (f32[12,8,128]{2,1,0:T(8,128)S(1)}, f32[12,8,128]{2,1,0:T(8,128)S(1)}, u32[]{:S(2)}, u32[]{:S(2)}) collective-permute-start(f32[12,8,128]{2,1,0:T(8,128)S(1)} %get-tuple-element.44), channel_id=1, source_target_pairs={{0,95},{1,2},{2,1},{3,4},{4,3},{5,6},{6,5},{7,8},{8,7},{9,10},{10,... | collective-permute-start | bytes 147464 | tf_op jit(solution)/shard_map/ppermute | solution.py:640
  18.5 0.0 collective-permute-start.1
  18.5 0.0 copy-done
  18.5 0.2 around.1
  18.7 0.9 %collective-permute-start.4 = (f32[36,8,128]{2,1,0:T(8,128)S(1)}, f32[36,8,128]{2,1,0:T(8,128)S(1)}, u32[]{:S(2)}, u32[]{:S(2)}) collective-permute-start(f32[36,8,128]{2,1,0:T(8,128)S(1)} %get-tuple-element.50), channel_id=1, source_target_pairs={{0,95},{1,2},{2,1},{3,4},{4,3},{5,6},{6,5},{7,8},{8,7},{9,10},{10,... | collective-permute-start | bytes 442376 | tf_op jit(solution)/shard_map/ppermute | solution.py:640
  19.6 0.8 collective-permute-start.5
  20.4 1.0 %own_rhs.1 = (f32[2,24,8,128]{3,2,1,0:T(8,128)S(1)}, f32[2,24,8,128]{3,2,1,0:T(8,128)S(1)}) custom-call(s32[4]{0:T(128)S(1)} %copy-done.5, f32[4,50,2,2,128]{4,3,2,1,0:T(2,128)S(1)} %bitcast.10, f32[2,24,8,128]{3,2,1,0:T(8,128)S(1)} %get-tuple-element.42.turned._, bf16[2,4,2,3,3,2,8,128]{7,6,5,4,3,2,1,0:T(8,128)(2,1)S(1)} %copy-done), custom_call_target="tpu_custom_call" | custom-call | tf_op jit(solution)/shard_map/own_rhs/pallas_call | solution.py:612
  21.3 0.0 collective-permute-done.got_far
  21.3 0.1 collective-permute-done.1.got_near
  21.5 0.7 rhs.1
  22.2 5.5 %collective-permute-start.2 = (f32[24,8,128]{2,1,0:T(8,128)S(1)}, f32[24,8,128]{2,1,0:T(8,128)S(1)}, u32[]{:S(2)}, u32[]{:S(2)}) collective-permute-start(f32[24,8,128]{2,1,0:T(8,128)S(1)} %get-tuple-element.48.sent_far), channel_id=1, source_target_pairs={{0,95},{1,2},{2,1},{3,4},{4,3},{5,6},{6,5},{7,8},{8,7},{9,10},{10,... | collective-permute-start | bytes 294920 | tf_op jit(solution)/shard_map/ppermute | solution.py:640
  27.7 0.0 collective-permute-start.3
  27.7 0.0 copy-done.2
  27.7 0.2 direct0.1.direct
  27.8 3.3 %collective-permute-done.2.got_far = f32[24,8,128]{2,1,0:T(8,128)S(1)} collective-permute-done((f32[24,8,128]{2,1,0:T(8,128)S(1)}, f32[24,8,128]{2,1,0:T(8,128)S(1)}, u32[]{:S(2)}, u32[]{:S(2)}) %collective-permute-start.2) | collective-permute-done | bytes 98336 | tf_op jit(solution)/shard_map/ppermute | solution.py:640
  31.1 0.3 collective-permute-done.3.got_near
  31.4 0.0 collective-permute-done.4.around_far
  31.4 0.0 collective-permute-done.5.around_near
  31.4 1.3 %step0.1 = (f32[2,24,8,128]{3,2,1,0:T(8,128)S(1)}, f32[2,24,8,128]{3,2,1,0:T(8,128)S(1)}, f32[24,8,128]{2,1,0:T(8,128)S(1)}, f32[24,8,128]{2,1,0:T(8,128)S(1)}) custom-call(f32[2,24,8,128]{3,2,1,0:T(8,128)S(1)} %direct0.1.direct, f32[2,24,8,128]{3,2,1,0:T(8,128)S(1)} %get-tuple-element.47.partial, f32[24,8,128]{2,1,0:T(8,128)S(1)} %get-tuple-element.48.sent_far, ...), custom_call_target="tpu_custom_call" | custom-call | tf_op jit(solution)/shard_map/step0/pallas_call | solution.py:612
  32.8 5.2 %collective-permute-start.6 = (f32[24,8,128]{2,1,0:T(8,128)S(1)}, f32[24,8,128]{2,1,0:T(8,128)S(1)}, u32[]{:S(2)}, u32[]{:S(2)}) collective-permute-start(f32[24,8,128]{2,1,0:T(8,128)S(1)} %get-tuple-element.54.sent_far), channel_id=1, source_target_pairs={{0,95},{1,2},{2,1},{3,4},{4,3},{5,6},{6,5},{7,8},{8,7},{9,10},{10,... | collective-permute-start | bytes 294920 | tf_op jit(solution)/shard_map/ppermute | solution.py:640
  38.0 0.0 collective-permute-start.7
  38.0 0.2 direct1.1.direct
  38.2 3.6 %collective-permute-done.6.got_far = f32[24,8,128]{2,1,0:T(8,128)S(1)} collective-permute-done((f32[24,8,128]{2,1,0:T(8,128)S(1)}, f32[24,8,128]{2,1,0:T(8,128)S(1)}, u32[]{:S(2)}, u32[]{:S(2)}) %collective-permute-start.6) | collective-permute-done | bytes 98336 | tf_op jit(solution)/shard_map/ppermute | solution.py:640
  41.8 0.0 collective-permute-done.7.got_near
  41.8 1.4 %step1.1 = (f32[2,24,8,128]{3,2,1,0:T(8,128)S(1)}, f32[2,24,8,128]{3,2,1,0:T(8,128)S(1)}, f32[24,8,128]{2,1,0:T(8,128)S(1)}, f32[24,8,128]{2,1,0:T(8,128)S(1)}, f32[2,24,8,128]{3,2,1,0:T(8,128)S(1)}) custom-call(f32[2,24,8,128]{3,2,1,0:T(8,128)S(1)} %direct1.1.direct, f32[2,24,8,128]{3,2,1,0:T(8,128)S(1)} %get-tuple-element.53.partial, ...), custom_call_target="tpu_custom_call" | custom-call | tf_op jit(solution)/shard_map/step1/pallas_call | solution.py:612
  43.1 5.2 %collective-permute-start.8 = (f32[24,8,128]{2,1,0:T(8,128)S(1)}, f32[24,8,128]{2,1,0:T(8,128)S(1)}, u32[]{:S(2)}, u32[]{:S(2)}) collective-permute-start(f32[24,8,128]{2,1,0:T(8,128)S(1)} %get-tuple-element.58.sent_far), channel_id=1, source_target_pairs={{0,95},{1,2},{2,1},{3,4},{4,3},{5,6},{6,5},{7,8},{8,7},{9,10},{10,... | collective-permute-start | bytes 294920 | tf_op jit(solution)/shard_map/ppermute | solution.py:640
  48.3 0.0 collective-permute-start.9
  48.4 0.2 direct2.1.direct
  48.5 3.6 %collective-permute-done.8.got_far = f32[24,8,128]{2,1,0:T(8,128)S(1)} collective-permute-done((f32[24,8,128]{2,1,0:T(8,128)S(1)}, f32[24,8,128]{2,1,0:T(8,128)S(1)}, u32[]{:S(2)}, u32[]{:S(2)}) %collective-permute-start.8) | collective-permute-done | bytes 98336 | tf_op jit(solution)/shard_map/ppermute | solution.py:640
  52.1 0.0 collective-permute-done.9.got_near
  52.1 1.3 %step2.1 = (f32[2,24,8,128]{3,2,1,0:T(8,128)S(1)}, f32[2,24,8,128]{3,2,1,0:T(8,128)S(1)}, f32[24,8,128]{2,1,0:T(8,128)S(1)}, f32[24,8,128]{2,1,0:T(8,128)S(1)}) custom-call(f32[2,24,8,128]{3,2,1,0:T(8,128)S(1)} %direct2.1.direct, f32[2,24,8,128]{3,2,1,0:T(8,128)S(1)} %get-tuple-element.57.partial, f32[24,8,128]{2,1,0:T(8,128)S(1)} %get-tuple-element.58.sent_far, ...), custom_call_target="tpu_custom_call" | custom-call | tf_op jit(solution)/shard_map/step2/pallas_call | solution.py:612
  53.5 5.2 %collective-permute-start.10 = (f32[24,8,128]{2,1,0:T(8,128)S(1)}, f32[24,8,128]{2,1,0:T(8,128)S(1)}, u32[]{:S(2)}, u32[]{:S(2)}) collective-permute-start(f32[24,8,128]{2,1,0:T(8,128)S(1)} %get-tuple-element.62.sent_far), channel_id=1, source_target_pairs={{0,95},{1,2},{2,1},{3,4},{4,3},{5,6},{6,5},{7,8},{8,7},{9,10},{10,... | collective-permute-start | bytes 294920 | tf_op jit(solution)/shard_map/ppermute | solution.py:640
  58.7 0.0 collective-permute-start.11
  58.7 0.3 traces.1
  59.0 5.3 %collective-permute-start.12 = (f32[32,2,2,128]{3,2,1,0:T(2,128)S(1)}, f32[32,2,2,128]{3,2,1,0:T(2,128)S(1)}, u32[]{:S(2)}, u32[]{:S(2)}) collective-permute-start(f32[32,2,2,128]{3,2,1,0:T(2,128)S(1)} %get-tuple-element.71), channel_id=1, source_target_pairs={{0,32},{32,0},{64,96},{96,64},{1,33},{33,1},{65,97},{97,65},{2,34}... | collective-permute-start | bytes 196616 | tf_op jit(solution)/shard_map/ppermute | solution.py:651
  64.3 0.0 collective-permute-start.13
  64.3 1.7 %collective-permute-start.14 = (f32[32,2,2,128]{3,2,1,0:T(2,128)S(1)}, f32[32,2,2,128]{3,2,1,0:T(2,128)S(1)}, u32[]{:S(2)}, u32[]{:S(2)}) collective-permute-start(f32[32,2,2,128]{3,2,1,0:T(2,128)S(1)} %get-tuple-element.73), channel_id=1, source_target_pairs={{0,96},{32,64},{64,32},{96,0},{1,97},{33,65},{65,33},{97,1},{2,98}... | collective-permute-start | bytes 196616 | tf_op jit(solution)/shard_map/ppermute | solution.py:651
  66.0 0.3 sums.1
  66.3 0.2 direct3.1.direct
  66.5 0.0 collective-permute-done.10.got_far
  66.5 0.0 collective-permute-done.11.got_near
  66.5 1.5 %last.1 = (f32[2,24,8,128]{3,2,1,0:T(8,128)S(1)}, f32[128,128]{1,0:T(8,128)}) custom-call(f32[2,24,8,128]{3,2,1,0:T(8,128)S(1)} %direct3.1.direct, f32[2,24,8,128]{3,2,1,0:T(8,128)S(1)} %get-tuple-element.61.partial, f32[24,8,128]{2,1,0:T(8,128)S(1)} %get-tuple-element.62.sent_far, f32[24,8,128]{2,1,0:T(8,128)S(1)} %get-tuple-element.63.sent_near, ...), custom_call_target="tpu_custom_call" | custom-call | tf_op jit(solution)/shard_map/last/pallas_call | solution.py:612
  68.0 8.3 %all-to-all-start = ((f32[128,1,128]{2,1,0:T(1,128)}), f32[128,1,128]{2,1,0:T(1,128)S(1)}, u32[]{:S(2)}, u32[]{:S(2)}) async-start(f32[128,1,128]{2,1,0:T(1,128)} %bitcast.4), calls=%async_computation | async-start | bytes 131072 | tf_op jit(solution)/shard_map/all_to_all | solution.py:736
  76.3 0.1 last_traces.1
  76.4 1.1 %collective-permute-start.15 = (f32[8,2,2,128]{3,2,1,0:T(2,128)S(1)}, f32[8,2,2,128]{3,2,1,0:T(2,128)S(1)}, u32[]{:S(2)}, u32[]{:S(2)}) collective-permute-start(f32[8,2,2,128]{3,2,1,0:T(2,128)S(1)} %get-tuple-element.76), channel_id=1, source_target_pairs={{0,32},{32,0},{64,96},{96,64},{1,33},{33,1},{65,97},{97,65},{2,34}... | collective-permute-start | bytes 49160 | tf_op jit(solution)/shard_map/ppermute | solution.py:651
  77.5 0.7 collective-permute-start.16
  78.2 0.0 collective-permute-done.12.refs_1_
  78.2 1.0 %collective-permute-start.17 = (f32[8,2,2,128]{3,2,1,0:T(2,128)S(1)}, f32[8,2,2,128]{3,2,1,0:T(2,128)S(1)}, u32[]{:S(2)}, u32[]{:S(2)}) collective-permute-start(f32[8,2,2,128]{3,2,1,0:T(2,128)S(1)} %get-tuple-element.78), channel_id=1, source_target_pairs={{0,96},{32,64},{64,32},{96,0},{1,97},{33,65},{65,33},{97,1},{2,98}... | collective-permute-start | bytes 49160 | tf_op jit(solution)/shard_map/ppermute | solution.py:651
  79.3 0.0 collective-permute-done.13.refs_2_
  79.3 0.0 collective-permute-done.14.refs_3_
  79.3 0.0 collective-permute-done.15.refs_5_
  79.3 1.2 %collective-permute-done.16.refs_6_ = f32[8,2,2,128]{3,2,1,0:T(2,128)S(1)} collective-permute-done((f32[8,2,2,128]{3,2,1,0:T(2,128)S(1)}, f32[8,2,2,128]{3,2,1,0:T(2,128)S(1)}, u32[]{:S(2)}, u32[]{:S(2)}) %collective-permute-start.16) | collective-permute-done | bytes 16416 | tf_op jit(solution)/shard_map/ppermute | solution.py:651
  80.5 1.3 %collective-permute-done.17.refs_7_ = f32[8,2,2,128]{3,2,1,0:T(2,128)S(1)} collective-permute-done((f32[8,2,2,128]{3,2,1,0:T(2,128)S(1)}, f32[8,2,2,128]{3,2,1,0:T(2,128)S(1)}, u32[]{:S(2)}, u32[]{:S(2)}) %collective-permute-start.17) | collective-permute-done | bytes 16416 | tf_op jit(solution)/shard_map/ppermute | solution.py:651
  81.7 4.3 %all-to-all-done = f32[128,1,128]{2,1,0:T(1,128)S(1)} async-done(((f32[128,1,128]{2,1,0:T(1,128)}), f32[128,1,128]{2,1,0:T(1,128)S(1)}, u32[]{:S(2)}, u32[]{:S(2)}) %all-to-all-start) | async-done | bytes 65568 | tf_op jit(solution)/shard_map/all_to_all | solution.py:736
  86.0 1.1 %final.1 = f32[16,2,2,128]{3,2,1,0:T(2,128)} custom-call(f32[128,128]{1,0:T(8,128)S(1)} %bitcast.11, f32[32,2,2,128]{3,2,1,0:T(2,128)S(1)} %get-tuple-element.70.refs_0_, f32[32,2,2,128]{3,2,1,0:T(2,128)S(1)} %collective-permute-done.12.refs_1_, f32[32,2,2,128]{3,2,1,0:T(2,128)S(1)} %collective-permute-done.13.refs_2_, ...), custom_call_target="tpu_custom_call" | custom-call | tf_op jit(solution)/shard_map/final/pallas_call | solution.py:612
  (5 shorter events, 0.0 us)
Async XLA Ops:
  0.0 1.0 %copy-start.3 = (f32[2,2,4,3,2,2,128]{6,5,4,3,2,1,0:T(2,128)S(1)}, f32[2,2,4,3,2,2,128]{6,5,4,3,2,1,0:T(2,128)}, u32[]{:S(2)}) copy-start(f32[2,2,4,3,2,2,128]{6,5,4,3,2,1,0:T(2,128)} %param.6) | copy-start | bytes 294916
  0.0 9.7 %copy-start.1 = (bf16[2,2,6,6,2,8,128]{6,5,4,3,2,1,0:T(8,128)(2,1)S(1)}, bf16[2,2,6,6,2,8,128]{6,5,4,3,2,1,0:T(8,128)(2,1)}, u32[]{:S(2)}) copy-start(bf16[2,2,6,6,2,8,128]{6,5,4,3,2,1,0:T(8,128)(2,1)} %odd_inverse.13) | copy-start | bytes 1769476
  1.0 0.7 copy-start.4
  1.7 8.0 %copy-start.5 = (s32[4]{0:T(128)S(1)}, s32[4]{0:T(128)}, u32[]{:S(2)}) copy-start(s32[4]{0:T(128)} %probe_rows.3) | copy-start | bytes 52
  9.7 8.9 %copy-start = (bf16[2,4,2,3,3,2,8,128]{7,6,5,4,3,2,1,0:T(8,128)(2,1)S(1)}, bf16[2,4,2,3,3,2,8,128]{7,6,5,4,3,2,1,0:T(8,128)(2,1)}, u32[]{:S(2)}) copy-start(bf16[2,4,2,3,3,2,8,128]{7,6,5,4,3,2,1,0:T(8,128)(2,1)} %links.13) | copy-start | bytes 1769476
  10.5 10.8 %collective-permute-start = (f32[12,8,128]{2,1,0:T(8,128)S(1)}, f32[12,8,128]{2,1,0:T(8,128)S(1)}, u32[]{:S(2)}, u32[]{:S(2)}) collective-permute-start(f32[12,8,128]{2,1,0:T(8,128)S(1)} %get-tuple-element.44), channel_id=1, source_target_pairs={{0,95},{1,2},{2,1},{3,4},{4,3},{5,6},{6,5},{7,8},{8,7},{9,10},{10,... | collective-permute-start | bytes 147464 | tf_op jit(solution)/shard_map/ppermute | solution.py:640
  18.5 2.9 %collective-permute-start.1 = (f32[12,8,128]{2,1,0:T(8,128)S(1)}, f32[12,8,128]{2,1,0:T(8,128)S(1)}, u32[]{:S(2)}, u32[]{:S(2)}) collective-permute-start(f32[12,8,128]{2,1,0:T(8,128)S(1)} %get-tuple-element.45), channel_id=1, source_target_pairs={{0,1},{1,0},{2,3},{3,2},{4,5},{5,4},{6,7},{7,6},{8,9},{9,8},{10,11... | collective-permute-start | bytes 147464 | tf_op jit(solution)/shard_map/ppermute | solution.py:640
  18.7 12.7 %collective-permute-start.4 = (f32[36,8,128]{2,1,0:T(8,128)S(1)}, f32[36,8,128]{2,1,0:T(8,128)S(1)}, u32[]{:S(2)}, u32[]{:S(2)}) collective-permute-start(f32[36,8,128]{2,1,0:T(8,128)S(1)} %get-tuple-element.50), channel_id=1, source_target_pairs={{0,95},{1,2},{2,1},{3,4},{4,3},{5,6},{6,5},{7,8},{8,7},{9,10},{10,... | collective-permute-start | bytes 442376 | tf_op jit(solution)/shard_map/ppermute | solution.py:640
  19.6 11.8 %collective-permute-start.5 = (f32[36,8,128]{2,1,0:T(8,128)S(1)}, f32[36,8,128]{2,1,0:T(8,128)S(1)}, u32[]{:S(2)}, u32[]{:S(2)}) collective-permute-start(f32[36,8,128]{2,1,0:T(8,128)S(1)} %get-tuple-element.51), channel_id=1, source_target_pairs={{0,1},{1,0},{2,3},{3,2},{4,5},{5,4},{6,7},{7,6},{8,9},{9,8},{10,11... | collective-permute-start | bytes 442376 | tf_op jit(solution)/shard_map/ppermute | solution.py:640
  21.5 6.2 %copy-start.2 = (bf16[2,2,6,6,2,8,128]{6,5,4,3,2,1,0:T(8,128)(2,1)S(1)}, bf16[2,2,6,6,2,8,128]{6,5,4,3,2,1,0:T(8,128)(2,1)}, u32[]{:S(2)}) copy-start(bf16[2,2,6,6,2,8,128]{6,5,4,3,2,1,0:T(8,128)(2,1)} %even.7) | copy-start | bytes 1769476
  22.2 9.0 %collective-permute-start.2 = (f32[24,8,128]{2,1,0:T(8,128)S(1)}, f32[24,8,128]{2,1,0:T(8,128)S(1)}, u32[]{:S(2)}, u32[]{:S(2)}) collective-permute-start(f32[24,8,128]{2,1,0:T(8,128)S(1)} %get-tuple-element.48.sent_far), channel_id=1, source_target_pairs={{0,95},{1,2},{2,1},{3,4},{4,3},{5,6},{6,5},{7,8},{8,7},{9,10},{10,... | collective-permute-start | bytes 294920 | tf_op jit(solution)/shard_map/ppermute | solution.py:640
  27.7 3.8 %collective-permute-start.3 = (f32[24,8,128]{2,1,0:T(8,128)S(1)}, f32[24,8,128]{2,1,0:T(8,128)S(1)}, u32[]{:S(2)}, u32[]{:S(2)}) collective-permute-start(f32[24,8,128]{2,1,0:T(8,128)S(1)} %get-tuple-element.49.sent_near), channel_id=1, source_target_pairs={{0,1},{1,0},{2,3},{3,2},{4,5},{5,4},{6,7},{7,6},{8,9},{9,8},{10,11... | collective-permute-start | bytes 294920 | tf_op jit(solution)/shard_map/ppermute | solution.py:640
  32.8 9.0 %collective-permute-start.6 = (f32[24,8,128]{2,1,0:T(8,128)S(1)}, f32[24,8,128]{2,1,0:T(8,128)S(1)}, u32[]{:S(2)}, u32[]{:S(2)}) collective-permute-start(f32[24,8,128]{2,1,0:T(8,128)S(1)} %get-tuple-element.54.sent_far), channel_id=1, source_target_pairs={{0,95},{1,2},{2,1},{3,4},{4,3},{5,6},{6,5},{7,8},{8,7},{9,10},{10,... | collective-permute-start | bytes 294920 | tf_op jit(solution)/shard_map/ppermute | solution.py:640
  38.0 3.8 %collective-permute-start.7 = (f32[24,8,128]{2,1,0:T(8,128)S(1)}, f32[24,8,128]{2,1,0:T(8,128)S(1)}, u32[]{:S(2)}, u32[]{:S(2)}) collective-permute-start(f32[24,8,128]{2,1,0:T(8,128)S(1)} %get-tuple-element.55.sent_near), channel_id=1, source_target_pairs={{0,1},{1,0},{2,3},{3,2},{4,5},{5,4},{6,7},{7,6},{8,9},{9,8},{10,11... | collective-permute-start | bytes 294920 | tf_op jit(solution)/shard_map/ppermute | solution.py:640
  43.1 9.0 %collective-permute-start.8 = (f32[24,8,128]{2,1,0:T(8,128)S(1)}, f32[24,8,128]{2,1,0:T(8,128)S(1)}, u32[]{:S(2)}, u32[]{:S(2)}) collective-permute-start(f32[24,8,128]{2,1,0:T(8,128)S(1)} %get-tuple-element.58.sent_far), channel_id=1, source_target_pairs={{0,95},{1,2},{2,1},{3,4},{4,3},{5,6},{6,5},{7,8},{8,7},{9,10},{10,... | collective-permute-start | bytes 294920 | tf_op jit(solution)/shard_map/ppermute | solution.py:640
  48.3 3.8 %collective-permute-start.9 = (f32[24,8,128]{2,1,0:T(8,128)S(1)}, f32[24,8,128]{2,1,0:T(8,128)S(1)}, u32[]{:S(2)}, u32[]{:S(2)}) collective-permute-start(f32[24,8,128]{2,1,0:T(8,128)S(1)} %get-tuple-element.59.sent_near), channel_id=1, source_target_pairs={{0,1},{1,0},{2,3},{3,2},{4,5},{5,4},{6,7},{7,6},{8,9},{9,8},{10,11... | collective-permute-start | bytes 294920 | tf_op jit(solution)/shard_map/ppermute | solution.py:640
  53.5 13.0 %collective-permute-start.10 = (f32[24,8,128]{2,1,0:T(8,128)S(1)}, f32[24,8,128]{2,1,0:T(8,128)S(1)}, u32[]{:S(2)}, u32[]{:S(2)}) collective-permute-start(f32[24,8,128]{2,1,0:T(8,128)S(1)} %get-tuple-element.62.sent_far), channel_id=1, source_target_pairs={{0,95},{1,2},{2,1},{3,4},{4,3},{5,6},{6,5},{7,8},{8,7},{9,10},{10,... | collective-permute-start | bytes 294920 | tf_op jit(solution)/shard_map/ppermute | solution.py:640
  58.7 7.8 %collective-permute-start.11 = (f32[24,8,128]{2,1,0:T(8,128)S(1)}, f32[24,8,128]{2,1,0:T(8,128)S(1)}, u32[]{:S(2)}, u32[]{:S(2)}) collective-permute-start(f32[24,8,128]{2,1,0:T(8,128)S(1)} %get-tuple-element.63.sent_near), channel_id=1, source_target_pairs={{0,1},{1,0},{2,3},{3,2},{4,5},{5,4},{6,7},{7,6},{8,9},{9,8},{10,11... | collective-permute-start | bytes 294920 | tf_op jit(solution)/shard_map/ppermute | solution.py:640
  59.0 19.2 %collective-permute-start.12 = (f32[32,2,2,128]{3,2,1,0:T(2,128)S(1)}, f32[32,2,2,128]{3,2,1,0:T(2,128)S(1)}, u32[]{:S(2)}, u32[]{:S(2)}) collective-permute-start(f32[32,2,2,128]{3,2,1,0:T(2,128)S(1)} %get-tuple-element.71), channel_id=1, source_target_pairs={{0,32},{32,0},{64,96},{96,64},{1,33},{33,1},{65,97},{97,65},{2,34}... | collective-permute-start | bytes 196616 | tf_op jit(solution)/shard_map/ppermute | solution.py:651
  64.3 15.0 %collective-permute-start.13 = (f32[32,2,2,128]{3,2,1,0:T(2,128)S(1)}, f32[32,2,2,128]{3,2,1,0:T(2,128)S(1)}, u32[]{:S(2)}, u32[]{:S(2)}) collective-permute-start(f32[32,2,2,128]{3,2,1,0:T(2,128)S(1)} %get-tuple-element.72), channel_id=1, source_target_pairs={{0,64},{32,96},{64,0},{96,32},{1,65},{33,97},{65,1},{97,33},{2,66}... | collective-permute-start | bytes 196616 | tf_op jit(solution)/shard_map/ppermute | solution.py:651
  64.3 15.0 %collective-permute-start.14 = (f32[32,2,2,128]{3,2,1,0:T(2,128)S(1)}, f32[32,2,2,128]{3,2,1,0:T(2,128)S(1)}, u32[]{:S(2)}, u32[]{:S(2)}) collective-permute-start(f32[32,2,2,128]{3,2,1,0:T(2,128)S(1)} %get-tuple-element.73), channel_id=1, source_target_pairs={{0,96},{32,64},{64,32},{96,0},{1,97},{33,65},{65,33},{97,1},{2,98}... | collective-permute-start | bytes 196616 | tf_op jit(solution)/shard_map/ppermute | solution.py:651
  68.0 18.1 %all-to-all-start = ((f32[128,1,128]{2,1,0:T(1,128)}), f32[128,1,128]{2,1,0:T(1,128)S(1)}, u32[]{:S(2)}, u32[]{:S(2)}) async-start(f32[128,1,128]{2,1,0:T(1,128)} %bitcast.4), calls=%async_computation | async-start | bytes 131072 | tf_op jit(solution)/shard_map/all_to_all | solution.py:736
  76.4 2.9 %collective-permute-start.15 = (f32[8,2,2,128]{3,2,1,0:T(2,128)S(1)}, f32[8,2,2,128]{3,2,1,0:T(2,128)S(1)}, u32[]{:S(2)}, u32[]{:S(2)}) collective-permute-start(f32[8,2,2,128]{3,2,1,0:T(2,128)S(1)} %get-tuple-element.76), channel_id=1, source_target_pairs={{0,32},{32,0},{64,96},{96,64},{1,33},{33,1},{65,97},{97,65},{2,34}... | collective-permute-start | bytes 49160 | tf_op jit(solution)/shard_map/ppermute | solution.py:651
  77.5 2.9 %collective-permute-start.16 = (f32[8,2,2,128]{3,2,1,0:T(2,128)S(1)}, f32[8,2,2,128]{3,2,1,0:T(2,128)S(1)}, u32[]{:S(2)}, u32[]{:S(2)}) collective-permute-start(f32[8,2,2,128]{3,2,1,0:T(2,128)S(1)} %get-tuple-element.77), channel_id=1, source_target_pairs={{0,64},{32,96},{64,0},{96,32},{1,65},{33,97},{65,1},{97,33},{2,66}... | collective-permute-start | bytes 49160 | tf_op jit(solution)/shard_map/ppermute | solution.py:651
  78.2 3.5 %collective-permute-start.17 = (f32[8,2,2,128]{3,2,1,0:T(2,128)S(1)}, f32[8,2,2,128]{3,2,1,0:T(2,128)S(1)}, u32[]{:S(2)}, u32[]{:S(2)}) collective-permute-start(f32[8,2,2,128]{3,2,1,0:T(2,128)S(1)} %get-tuple-element.78), channel_id=1, source_target_pairs={{0,96},{32,64},{64,32},{96,0},{1,97},{33,65},{65,33},{97,1},{2,98}... | collective-permute-start | bytes 49160 | tf_op jit(solution)/shard_map/ppermute | solution.py:651

commit v5 on v4

--- a/solution.py
+++ b/solution.py
@@ -251,30 +251,47 @@
     return at_first, at_last
 
 
-def begin_schur(vector, links, odd_inverse, dagger, partial, sent):
+def begin_slice(vector, links, odd_inverse, dagger, time, partial, edge):
+    side = (1 if dagger else -1) * (1 if time == 0 else -1)
+    sign = edge_signs()[time]
+    whole = clover_at(odd_inverse, hop_at(vector, links, time, 1, dagger), time)
+    store_spinor(partial, whole)
+    for base, spinor, parity in ((0, load_spinor(vector, time), 0), (12, whole, 1)):
+        half = project(spinor, 3, side)
+        if time == 1:
+            half = link_mul_adj(link_at(links, parity, 3, 1), half)
+        for s in range(2):
+            for a in range(3):
+                for part in range(2):
+                    edge[base + part * 6 + s * 3 + a] = half[s][a][part] * sign
+
+
+def begin_schur(vector, links, odd_inverse, dagger, far_side, partial, edge):
+    odd = lax.rem(lax.axis_index("lat"), 2) == 1
+    later = odd if far_side else jnp.logical_not(odd)
+
+    @pl.when(later)
+    def _():
+        begin_slice(vector, links, odd_inverse, dagger, 1, partial, edge)
+
+    @pl.when(jnp.logical_not(later))
+    def _():
+        begin_slice(vector, links, odd_inverse, dagger, 0, partial, edge)
+
+
+def spinor_of(row):
+    return [[(row(s * 3 + a), row(12 + s * 3 + a)) for a in range(3)] for s in range(4)]
+
+
+def end_schur(direct, back, partial, got, links, odd_inverse, dagger, odd_field, result):
     forward, backward = (1, -1) if dagger else (-1, 1)
-    for time in range(2):
-        store_spinor(
-            partial, clover_at(odd_inverse, hop_at(vector, links, time, 1, dagger), time), time
-        )
-    for base, field, parity in ((0, vector, 0), (12, partial, 1)):
-        earlier = project(load_spinor(field, 0), 3, forward)
-        later = project(load_spinor(field, 1), 3, backward)
-        store_halves(sent, earlier, link_mul_adj(link_at(links, parity, 3, 1), later), base)
-
-
-def end_schur(
-    direct, partial, sent, got, around, links, odd_inverse, dagger, odd_field, result
-):
-    forward, backward = (1, -1) if dagger else (-1, 1)
-    at_first, at_last = edge_signs()
     for time in range(2):
         if time == 0:
             half, sign = load_half(got.low), backward
         else:
             half = link_mul(link_at(links, 1, 3, 1), load_half(got.high))
             sign = forward
-        own = load_spinor(partial, time)
+        own = spinor_of(partial.low if time == 0 else partial.high)
         top = block_mul(block_at(odd_inverse, 0, time), half)
         bottom = block_mul(block_at(odd_inverse, 1, time), half)
         whole = [[plus(own[s][a], top[s][a], 0) for a in range(3)] for s in range(2)] + [
@@ -282,10 +299,9 @@
             for s in range(2)
         ]
         store_spinor(odd_field, whole, time)
-    back = block_mul(block_packed(around.high), load_half(sent.high))
-    high = add_half(load_half(got.high, 12), scaled_half(back, at_last))
-    back = block_mul(block_packed(around.low), load_half(sent.low))
-    low = add_half(load_half(got.low, 12), scaled_half(back, at_first))
+    kept = lambda n: back[n]
+    high = add_half(load_half(got.high, 12), load_half(kept))
+    low = add_half(load_half(got.low, 12), load_half(kept, 12))
     for time in range(2):
         returned = hop_at(odd_field, links, time, 0, dagger, high, low)
         own = load_spinor(direct, time)
@@ -411,31 +427,47 @@
         )
 
 
-def direct_kernel(vector, even, out):
+def direct_kernel(
+    vector, even, sent_far, sent_near, around_far, around_near, out, back
+):
     for time in range(2):
         store_spinor(out, clover_at(even, load_spinor(vector, time), time), time)
-
-
-def rhs_kernel(partial, got_far, got_near, links, odd_inverse, rhs, odd, far, near):
+    sent, around = Swapped(sent_far, sent_near), Swapped(around_far, around_near)
+    at_first, at_last = edge_signs()
+    for base, matrix, half, sign in (
+        (0, around.high, sent.high, at_last),
+        (12, around.low, sent.low, at_first),
+    ):
+        half = block_mul(block_packed(matrix), load_half(half))
+        for s in range(2):
+            for a in range(3):
+                for part in range(2):
+                    back[base + part * 6 + s * 3 + a] = half[s][a][part] * sign
+
+
+def rhs_kernel(partial, got_far, got_near, links, odd_inverse, rhs, odd, far):
     got = Swapped(got_far, got_near)
     half = scaled_half(load_half(got.low), KAPPA)
     store_spinor(rhs, expand_onto(load_spinor(partial, 0), half, 3, 1), 0)
     half = scaled_half(link_mul(link_at(links, 0, 3, 1), load_half(got.high)), KAPPA)
     store_spinor(rhs, expand_onto(load_spinor(partial, 1), half, 3, -1), 1)
-    begin_schur(rhs, links, odd_inverse, True, odd, Swapped(far, near))
+    begin_schur(rhs, links, odd_inverse, True, True, odd, far)
+
+
+def near_kernel(dagger, vector, links, odd_inverse, odd, near):
+    begin_schur(vector, links, odd_inverse, dagger, False, odd, near)
 
 
 def step_kernel(
     dagger,
-    direct, partial, sent_far, sent_near, got_far, got_near, around_far, around_near,
-    links, odd_inverse,
-    result, odd, far, near, odd_field,
+    direct, back, odd_far, odd_near, got_far, got_near, links, odd_inverse,
+    result, odd, far, odd_field,
 ):
     end_schur(
-        direct, partial, Swapped(sent_far, sent_near), Swapped(got_far, got_near),
-        Swapped(around_far, around_near), links, odd_inverse, dagger, odd_field, result,
-    )
-    begin_schur(result, links, odd_inverse, not dagger, odd, Swapped(far, near))
+        direct, back, Swapped(odd_far, odd_near), Swapped(got_far, got_near),
+        links, odd_inverse, dagger, odd_field, result,
+    )
+    begin_schur(result, links, odd_inverse, not dagger, True, odd, far)
 
 
 def column_sum(left, right):
@@ -526,13 +558,12 @@
 
 
 def last_kernel(
-    direct, partial, sent_far, sent_near, got_far, got_near, around_far, around_near,
-    links, odd_inverse, image, row, about,
+    direct, back, odd_far, odd_near, got_far, got_near, links, odd_inverse, image, row, about,
     odd_field, sums, result,
 ):
     end_schur(
-        direct, partial, Swapped(sent_far, sent_near), Swapped(got_far, got_near),
-        Swapped(around_far, around_near), links, odd_inverse, False, odd_field, result,
+        direct, back, Swapped(odd_far, odd_near), Swapped(got_far, got_near),
+        links, odd_inverse, False, odd_field, result,
     )
     image_at = lambda time, n: image[time, n]
     rest_at = lambda time, n: result[time, n] - about[...] * image[time, n]
@@ -630,19 +661,11 @@
     return (vector ^ (2 * (place // (length // 2)))) * length + place
 
 
-def swap(far, near):
+def swap(array, far_side):
     length, vectors = lax.axis_size("lat"), range(lax.axis_size("sub"))
-
-    def moved(array, partner):
-        pairs = [
-            (device_of(v, i), device_of(v, partner(i))) for v in vectors for i in range(length)
-        ]
-        return lax.ppermute(array, ("sub", "lat"), pairs)
-
-    return (
-        moved(far, lambda i: (i + (1 if i % 2 else -1)) % length),
-        moved(near, lambda i: i ^ 1),
-    )
+    partner = (lambda i: (i + (1 if i % 2 else -1)) % length) if far_side else (lambda i: i ^ 1)
+    pairs = [(device_of(v, i), device_of(v, partner(i))) for v in vectors for i in range(length)]
+    return lax.ppermute(array, ("sub", "lat"), pairs)
 
 
 def swap_depths(traces):
@@ -669,7 +692,7 @@
         (gathered, links[1, 3], odd_inverse),
         ((25, 2, 8, 128),),
     )
-    got = swap(*sent)
+    got = (swap(sent[0], True), swap(sent[1], False))
     probes_even, partial = call(
         own_rhs_kernel,
         "own_rhs",
@@ -678,40 +701,53 @@
         (gathered, turned, links),
         ((25, 2, 8, 128),),
     )
-    around = swap(
-        *call(
-            around_kernel,
-            "around",
-            ((36, 8, 128),) * 2,
+    around = call(
+        around_kernel,
+        "around",
+        ((36, 8, 128),) * 2,
+        (),
+        (links, odd_inverse, turned),
+        (),
+        (2,),
+    )
+    around = (swap(around[0], True), swap(around[1], False))
+
+    def exchange(vector, odd, far, dagger, name):
+        got_far = swap(far, True)
+        odd_near, near = call(
+            functools.partial(near_kernel, dagger),
+            "near" + name,
+            (EDGE, EDGE),
             (),
-            (links, odd_inverse, turned),
-            (),
-            (2,),
-        )
-    )
-    vector, odd, *sent = call(
-        rhs_kernel, "rhs", (FIELD, FIELD, EDGE, EDGE), (), (partial, *got, links, odd_inverse)
+            (vector, links, odd_inverse),
+        )
+        got_near = swap(near, False)
+        direct, back = call(
+            direct_kernel, "direct" + name, (FIELD, EDGE), (), (vector, even, far, near, *around)
+        )
+        return (direct, back, odd, odd_near, got_far, got_near, links, odd_inverse)
+
+    vector, odd, far = call(
+        rhs_kernel, "rhs", (FIELD, EDGE, EDGE), (), (partial, *got, links, odd_inverse)
     )
     kept = []
     for step in range(3):
-        got = swap(*sent)
-        (direct,) = call(direct_kernel, "direct%d" % step, (FIELD,), (), (vector, even))
-        arrays = (direct, odd, *sent, *got, *around, links, odd_inverse)
+        dagger = step % 2 == 0
+        arrays = exchange(vector, odd, far, dagger, str(step))
         keep = step == 1
-        vector, odd, *sent = call(
-            functools.partial(step_kernel, step % 2 == 0),
+        vector, odd, far, *rest = call(
+            functools.partial(step_kernel, dagger),
             "step%d" % step,
-            (FIELD, FIELD, EDGE, EDGE) + (FIELD,) * keep,
+            (FIELD, EDGE, EDGE) + (FIELD,) * keep,
             (),
             arrays,
             () if keep else (FIELD,),
         )
         if keep:
-            first_odd = sent.pop()
+            first_odd = rest[0]
         kept.append(vector)
     first, image, second = kept
-    got = swap(*sent)
-    (direct,) = call(direct_kernel, "direct3", (FIELD,), (), (second, even))
+    arrays = exchange(second, odd, far, False, "3")
     row, about = call(
         sums_kernel, "sums", ((1, 128), (8, 128)), (), (first, image, second)
     )
@@ -730,7 +766,7 @@
         "last",
         (FIELD, (devices, 128)),
         (),
-        (direct, odd, *sent, *got, *around, links, odd_inverse, image, row, about),
+        (*arrays, image, row, about),
         (FIELD,),
     )
     sums = lax.all_to_all(sums, ("sub", "lat"), 0, 0, tiled=True)

time: 87.3 us -> 85.7 us (0.982)
  starting transfers between devices: 49.1 us -> 47.9 us
    pallas_call x17 -> x21, Pallas kernels: 10.6 us -> 10.5 us  [call(): pl.pallas_call(kernel, out_shape=tuple((jax.ShapeDtypeStruct(s, F32) for...]
  transfers between devices with their start and end apart: 19 -> 19, of which waited for: 8 -> 9; matrix products, arithmetic and copies ran while one was open for 0% -> 0% of each run, Pallas kernels for 5% -> 7%
where the time goes in v5:
time: 85.7 us; the launch traced here: 85.5 us
  starting transfers between devices  47.9 us (56%)
  waiting for transfers between devices  17.2 us (20%)
  Pallas kernels  10.5 us (12%)
  blocking collectives  7.97 us (9%)
  local copies, waits for them, and re-layouts  1.66 us (2%)
    ppermute x12, starting transfers between devices, swap(): return lax.ppermute(array, ('sub', 'lat'), pairs)  30.2 us
    ppermute x12, waiting for transfers between devices, swap(): return lax.ppermute(array, ('sub', 'lat'), pairs)  10.5 us
    pallas_call x21, Pallas kernels, call(): pl.pallas_call(kernel, out_shape=tuple((jax.ShapeDtypeStruct(s, F32) for...  10.5 us
    ppermute x6, starting transfers between devices, swap_depths(): lax.ppermute(traces[n], 'sub', [(i, i ^ n) for i in subs])  9.88 us
    all_gather x1, blocking collectives, whole(): gathered = lax.all_gather(own, 'sub')  7.97 us
    all_to_all x1, starting transfers between devices, whole(): sums = lax.all_to_all(sums, ('sub', 'lat'), 0, 0, tiled=True)  7.79 us
    all_to_all x1, waiting for transfers between devices, whole(): sums = lax.all_to_all(sums, ('sub', 'lat'), 0, 0, tiled=True)  4.25 us
    ppermute x6, waiting for transfers between devices, swap_depths(): lax.ppermute(traces[n], 'sub', [(i, i ^ n) for i in subs])  2.46 us
  transfers between devices with their start and end apart: 19, of which 9 were waited for; matrix products, arithmetic and copies ran while one was open for 0% of the time, Pallas kernels for 7%

profile of v5, /device:TPU:1, one launch (start us, length us, event | category | flops | bytes accessed | tf_op | source)
XLA Modules:
  0.0 85.5 jit_solution(18227142850413969713)
XLA Ops:
  0.0 1.0 %slice_bitcast_fusion.time_link = bf16[2,3,3,2,8,128]{5,4,3,2,1,0:T(8,128)(2,1)S(1)} fusion(bf16[2,4,2,3,3,2,8,128]{7,6,5,4,3,2,1,0:T(8,128)(2,1)} %links.21), kind=kLoop, calls=%fused_computation | loop fusion | bytes 147456 | tf_op jit(solution)/shard_map/squeeze | solution.py:692
  1.0 0.7 copy-done.4
  1.7 0.0 copy-start.5
  1.7 8.0 %all-gather = f32[200,2,2,128]{3,2,1,0:T(2,128)S(1)} all-gather(f32[50,2,2,128]{3,2,1,0:T(2,128)S(1)} %pack.1), channel_id=2, replica_groups=mesh['sub'=4,'lat'=32] {'sub'}, dimensions={0}, use_global_device_ids=true | all-gather | bytes 512000 | tf_op jit(solution)/shard_map/all_gather | solution.py:686
  9.7 0.0 copy-done.1
  9.7 0.8 start.1
  10.5 8.0 %collective-permute-start = (f32[12,8,128]{2,1,0:T(8,128)S(1)}, f32[12,8,128]{2,1,0:T(8,128)S(1)}, u32[]{:S(2)}, u32[]{:S(2)}) collective-permute-start(f32[12,8,128]{2,1,0:T(8,128)S(1)} %get-tuple-element.56), channel_id=1, source_target_pairs={{0,95},{1,2},{2,1},{3,4},{4,3},{5,6},{6,5},{7,8},{8,7},{9,10},{10,... | collective-permute-start | bytes 147464 | tf_op jit(solution)/shard_map/ppermute | solution.py:668
  18.5 0.0 collective-permute-start.1
  18.5 0.0 copy-done
  18.5 0.2 around.1
  18.7 0.9 %collective-permute-start.2 = (f32[36,8,128]{2,1,0:T(8,128)S(1)}, f32[36,8,128]{2,1,0:T(8,128)S(1)}, u32[]{:S(2)}, u32[]{:S(2)}) collective-permute-start(f32[36,8,128]{2,1,0:T(8,128)S(1)} %get-tuple-element.61), channel_id=1, source_target_pairs={{0,95},{1,2},{2,1},{3,4},{4,3},{5,6},{6,5},{7,8},{8,7},{9,10},{10,... | collective-permute-start | bytes 442376 | tf_op jit(solution)/shard_map/ppermute | solution.py:668
  19.6 0.8 collective-permute-start.3
  20.4 1.0 %own_rhs.1 = (f32[2,24,8,128]{3,2,1,0:T(8,128)S(1)}, f32[2,24,8,128]{3,2,1,0:T(8,128)S(1)}) custom-call(s32[4]{0:T(128)S(1)} %copy-done.5, f32[4,50,2,2,128]{4,3,2,1,0:T(2,128)S(1)} %bitcast.10, f32[2,24,8,128]{3,2,1,0:T(8,128)S(1)} %get-tuple-element.54.turned._, bf16[2,4,2,3,3,2,8,128]{7,6,5,4,3,2,1,0:T(8,128)(2,1)S(1)} %copy-done), custom_call_target="tpu_custom_call" | custom-call | tf_op jit(solution)/shard_map/own_rhs/pallas_call | solution.py:643
  21.3 0.0 collective-permute-done.got_far
  21.3 0.1 collective-permute-done.1.got_near
  21.5 0.3 rhs.1
  21.8 5.6 %collective-permute-start.4 = (f32[24,8,128]{2,1,0:T(8,128)S(1)}, f32[24,8,128]{2,1,0:T(8,128)S(1)}, u32[]{:S(2)}, u32[]{:S(2)}) collective-permute-start(f32[24,8,128]{2,1,0:T(8,128)S(1)} %get-tuple-element.59.sent_far), channel_id=1, source_target_pairs={{0,95},{1,2},{2,1},{3,4},{4,3},{5,6},{6,5},{7,8},{8,7},{9,10},{10,... | collective-permute-start | bytes 294920 | tf_op jit(solution)/shard_map/ppermute | solution.py:668
  27.4 0.3 near0.1
  27.7 0.1 collective-permute-start.5
  27.8 1.4 %collective-permute-done.2.around_far = f32[36,8,128]{2,1,0:T(8,128)S(1)} collective-permute-done((f32[36,8,128]{2,1,0:T(8,128)S(1)}, f32[36,8,128]{2,1,0:T(8,128)S(1)}, u32[]{:S(2)}, u32[]{:S(2)}) %collective-permute-start.2) | collective-permute-done | bytes 147488 | tf_op jit(solution)/shard_map/ppermute | solution.py:668
  29.2 0.0 collective-permute-done.3.around_near
  29.2 0.2 direct0.1
  29.5 1.4 %collective-permute-done.4.got_far = f32[24,8,128]{2,1,0:T(8,128)S(1)} collective-permute-done((f32[24,8,128]{2,1,0:T(8,128)S(1)}, f32[24,8,128]{2,1,0:T(8,128)S(1)}, u32[]{:S(2)}, u32[]{:S(2)}) %collective-permute-start.4) | collective-permute-done | bytes 98336 | tf_op jit(solution)/shard_map/ppermute | solution.py:668
  30.9 0.7 collective-permute-done.5.got_near
  31.6 0.9 %step0.1 = (f32[2,24,8,128]{3,2,1,0:T(8,128)S(1)}, f32[24,8,128]{2,1,0:T(8,128)S(1)}, f32[24,8,128]{2,1,0:T(8,128)S(1)}) custom-call(f32[2,24,8,128]{3,2,1,0:T(8,128)S(1)} %get-tuple-element.63.direct, f32[24,8,128]{2,1,0:T(8,128)S(1)} %get-tuple-element.64.back, f32[24,8,128]{2,1,0:T(8,128)S(1)} %get-tuple-element.65.odd_far, ...), custom_call_target="tpu_custom_call" | custom-call | tf_op jit(solution)/shard_map/step0/pallas_call | solution.py:643
  32.5 4.8 %collective-permute-start.6 = (f32[24,8,128]{2,1,0:T(8,128)S(1)}, f32[24,8,128]{2,1,0:T(8,128)S(1)}, u32[]{:S(2)}, u32[]{:S(2)}) collective-permute-start(f32[24,8,128]{2,1,0:T(8,128)S(1)} %get-tuple-element.68.sent_far), channel_id=1, source_target_pairs={{0,95},{1,2},{2,1},{3,4},{4,3},{5,6},{6,5},{7,8},{8,7},{9,10},{10,... | collective-permute-start | bytes 294920 | tf_op jit(solution)/shard_map/ppermute | solution.py:668
  37.3 0.3 near1.1
  37.7 0.1 collective-permute-start.7
  37.8 0.2 direct1.1
  38.0 3.4 %collective-permute-done.6.got_far = f32[24,8,128]{2,1,0:T(8,128)S(1)} collective-permute-done((f32[24,8,128]{2,1,0:T(8,128)S(1)}, f32[24,8,128]{2,1,0:T(8,128)S(1)}, u32[]{:S(2)}, u32[]{:S(2)}) %collective-permute-start.6) | collective-permute-done | bytes 98336 | tf_op jit(solution)/shard_map/ppermute | solution.py:668
  41.5 0.0 collective-permute-done.7.got_near
  41.5 0.9 %step1.1 = (f32[2,24,8,128]{3,2,1,0:T(8,128)S(1)}, f32[24,8,128]{2,1,0:T(8,128)S(1)}, f32[24,8,128]{2,1,0:T(8,128)S(1)}, f32[2,24,8,128]{3,2,1,0:T(8,128)S(1)}) custom-call(f32[2,24,8,128]{3,2,1,0:T(8,128)S(1)} %get-tuple-element.70.direct, f32[24,8,128]{2,1,0:T(8,128)S(1)} %get-tuple-element.71.back, f32[24,8,128]{2,1,0:T(8,128)S(1)} %get-tuple-element.72.odd_far, ...), custom_call_target="tpu_custom_call" | custom-call | tf_op jit(solution)/shard_map/step1/pallas_call | solution.py:643
  42.4 4.9 %collective-permute-start.8 = (f32[24,8,128]{2,1,0:T(8,128)S(1)}, f32[24,8,128]{2,1,0:T(8,128)S(1)}, u32[]{:S(2)}, u32[]{:S(2)}) collective-permute-start(f32[24,8,128]{2,1,0:T(8,128)S(1)} %get-tuple-element.75.sent_far), channel_id=1, source_target_pairs={{0,95},{1,2},{2,1},{3,4},{4,3},{5,6},{6,5},{7,8},{8,7},{9,10},{10,... | collective-permute-start | bytes 294920 | tf_op jit(solution)/shard_map/ppermute | solution.py:668
  47.3 0.3 near2.1
  47.6 0.1 collective-permute-start.9
  47.7 0.2 direct2.1
  47.9 3.4 %collective-permute-done.8.got_far = f32[24,8,128]{2,1,0:T(8,128)S(1)} collective-permute-done((f32[24,8,128]{2,1,0:T(8,128)S(1)}, f32[24,8,128]{2,1,0:T(8,128)S(1)}, u32[]{:S(2)}, u32[]{:S(2)}) %collective-permute-start.8) | collective-permute-done | bytes 98336 | tf_op jit(solution)/shard_map/ppermute | solution.py:668
  51.3 0.0 collective-permute-done.9.got_near
  51.4 0.9 %step2.1 = (f32[2,24,8,128]{3,2,1,0:T(8,128)S(1)}, f32[24,8,128]{2,1,0:T(8,128)S(1)}, f32[24,8,128]{2,1,0:T(8,128)S(1)}) custom-call(f32[2,24,8,128]{3,2,1,0:T(8,128)S(1)} %get-tuple-element.77.direct, f32[24,8,128]{2,1,0:T(8,128)S(1)} %get-tuple-element.78.back, f32[24,8,128]{2,1,0:T(8,128)S(1)} %get-tuple-element.79.odd_far, ...), custom_call_target="tpu_custom_call" | custom-call | tf_op jit(solution)/shard_map/step2/pallas_call | solution.py:643
  52.3 4.9 %collective-permute-start.10 = (f32[24,8,128]{2,1,0:T(8,128)S(1)}, f32[24,8,128]{2,1,0:T(8,128)S(1)}, u32[]{:S(2)}, u32[]{:S(2)}) collective-permute-start(f32[24,8,128]{2,1,0:T(8,128)S(1)} %get-tuple-element.82.sent_far), channel_id=1, source_target_pairs={{0,95},{1,2},{2,1},{3,4},{4,3},{5,6},{6,5},{7,8},{8,7},{9,10},{10,... | collective-permute-start | bytes 294920 | tf_op jit(solution)/shard_map/ppermute | solution.py:668
  57.2 0.3 near3.1
  57.5 0.1 collective-permute-start.11
  57.6 0.3 traces.1
  58.0 5.3 %collective-permute-start.12 = (f32[32,2,2,128]{3,2,1,0:T(2,128)S(1)}, f32[32,2,2,128]{3,2,1,0:T(2,128)S(1)}, u32[]{:S(2)}, u32[]{:S(2)}) collective-permute-start(f32[32,2,2,128]{3,2,1,0:T(2,128)S(1)} %get-tuple-element.95), channel_id=1, source_target_pairs={{0,32},{32,0},{64,96},{96,64},{1,33},{33,1},{65,97},{97,65},{2,34}... | collective-permute-start | bytes 196616 | tf_op jit(solution)/shard_map/ppermute | solution.py:674
  63.2 0.0 collective-permute-start.13
  63.2 1.7 %collective-permute-start.14 = (f32[32,2,2,128]{3,2,1,0:T(2,128)S(1)}, f32[32,2,2,128]{3,2,1,0:T(2,128)S(1)}, u32[]{:S(2)}, u32[]{:S(2)}) collective-permute-start(f32[32,2,2,128]{3,2,1,0:T(2,128)S(1)} %get-tuple-element.97), channel_id=1, source_target_pairs={{0,96},{32,64},{64,32},{96,0},{1,97},{33,65},{65,33},{97,1},{2,98}... | collective-permute-start | bytes 196616 | tf_op jit(solution)/shard_map/ppermute | solution.py:674
  65.0 0.3 sums.1
  65.2 0.3 direct3.1
  65.5 0.0 collective-permute-done.10.got_far
  65.5 0.0 collective-permute-done.11.got_near
  65.5 1.4 %last.1 = (f32[2,24,8,128]{3,2,1,0:T(8,128)S(1)}, f32[128,128]{1,0:T(8,128)}) custom-call(f32[2,24,8,128]{3,2,1,0:T(8,128)S(1)} %get-tuple-element.84.direct, f32[24,8,128]{2,1,0:T(8,128)S(1)} %get-tuple-element.85.back, f32[24,8,128]{2,1,0:T(8,128)S(1)} %get-tuple-element.86.odd_far, f32[24,8,128]{2,1,0:T(8,128)S(1)} %get-tuple-element.87.odd_near, ...), custom_call_target="tpu_custom_call" | custom-call | tf_op jit(solution)/shard_map/last/pallas_call | solution.py:643
  66.9 7.8 %all-to-all-start = ((f32[128,1,128]{2,1,0:T(1,128)}), f32[128,1,128]{2,1,0:T(1,128)S(1)}, u32[]{:S(2)}, u32[]{:S(2)}) async-start(f32[128,1,128]{2,1,0:T(1,128)} %bitcast.4), calls=%async_computation | async-start | bytes 131072 | tf_op jit(solution)/shard_map/all_to_all | solution.py:772
  74.7 0.1 last_traces.1
  74.8 1.1 %collective-permute-start.15 = (f32[8,2,2,128]{3,2,1,0:T(2,128)S(1)}, f32[8,2,2,128]{3,2,1,0:T(2,128)S(1)}, u32[]{:S(2)}, u32[]{:S(2)}) collective-permute-start(f32[8,2,2,128]{3,2,1,0:T(2,128)S(1)} %get-tuple-element.100), channel_id=1, source_target_pairs={{0,32},{32,0},{64,96},{96,64},{1,33},{33,1},{65,97},{97,65},{2,34}... | collective-permute-start | bytes 49160 | tf_op jit(solution)/shard_map/ppermute | solution.py:674
  75.9 0.7 collective-permute-start.16
  76.6 0.0 collective-permute-done.12.refs_1_
  76.6 1.0 %collective-permute-start.17 = (f32[8,2,2,128]{3,2,1,0:T(2,128)S(1)}, f32[8,2,2,128]{3,2,1,0:T(2,128)S(1)}, u32[]{:S(2)}, u32[]{:S(2)}) collective-permute-start(f32[8,2,2,128]{3,2,1,0:T(2,128)S(1)} %get-tuple-element.102), channel_id=1, source_target_pairs={{0,96},{32,64},{64,32},{96,0},{1,97},{33,65},{65,33},{97,1},{2,98}... | collective-permute-start | bytes 49160 | tf_op jit(solution)/shard_map/ppermute | solution.py:674
  77.7 0.0 collective-permute-done.13.refs_2_
  77.7 0.0 collective-permute-done.14.refs_3_
  77.7 0.0 collective-permute-done.15.refs_5_
  77.7 1.2 %collective-permute-done.16.refs_6_ = f32[8,2,2,128]{3,2,1,0:T(2,128)S(1)} collective-permute-done((f32[8,2,2,128]{3,2,1,0:T(2,128)S(1)}, f32[8,2,2,128]{3,2,1,0:T(2,128)S(1)}, u32[]{:S(2)}, u32[]{:S(2)}) %collective-permute-start.16) | collective-permute-done | bytes 16416 | tf_op jit(solution)/shard_map/ppermute | solution.py:674
  78.9 1.3 %collective-permute-done.17.refs_7_ = f32[8,2,2,128]{3,2,1,0:T(2,128)S(1)} collective-permute-done((f32[8,2,2,128]{3,2,1,0:T(2,128)S(1)}, f32[8,2,2,128]{3,2,1,0:T(2,128)S(1)}, u32[]{:S(2)}, u32[]{:S(2)}) %collective-permute-start.17) | collective-permute-done | bytes 16416 | tf_op jit(solution)/shard_map/ppermute | solution.py:674
  80.1 4.2 %all-to-all-done = f32[128,1,128]{2,1,0:T(1,128)S(1)} async-done(((f32[128,1,128]{2,1,0:T(1,128)}), f32[128,1,128]{2,1,0:T(1,128)S(1)}, u32[]{:S(2)}, u32[]{:S(2)}) %all-to-all-start) | async-done | bytes 65568 | tf_op jit(solution)/shard_map/all_to_all | solution.py:772
  84.4 1.1 %final.1 = f32[16,2,2,128]{3,2,1,0:T(2,128)} custom-call(f32[128,128]{1,0:T(8,128)S(1)} %bitcast.11, f32[32,2,2,128]{3,2,1,0:T(2,128)S(1)} %get-tuple-element.94.refs_0_, f32[32,2,2,128]{3,2,1,0:T(2,128)S(1)} %collective-permute-done.12.refs_1_, f32[32,2,2,128]{3,2,1,0:T(2,128)S(1)} %collective-permute-done.13.refs_2_, ...), custom_call_target="tpu_custom_call" | custom-call | tf_op jit(solution)/shard_map/final/pallas_call | solution.py:643
  (9 shorter events, 0.0 us)
Async XLA Ops:
  0.0 1.0 %copy-start.3 = (f32[2,2,4,3,2,2,128]{6,5,4,3,2,1,0:T(2,128)S(1)}, f32[2,2,4,3,2,2,128]{6,5,4,3,2,1,0:T(2,128)}, u32[]{:S(2)}) copy-start(f32[2,2,4,3,2,2,128]{6,5,4,3,2,1,0:T(2,128)} %param.6) | copy-start | bytes 294916
  0.0 9.7 %copy-start.1 = (bf16[2,2,6,6,2,8,128]{6,5,4,3,2,1,0:T(8,128)(2,1)S(1)}, bf16[2,2,6,6,2,8,128]{6,5,4,3,2,1,0:T(8,128)(2,1)}, u32[]{:S(2)}) copy-start(bf16[2,2,6,6,2,8,128]{6,5,4,3,2,1,0:T(8,128)(2,1)} %odd_inverse.21) | copy-start | bytes 1769476
  1.0 0.7 copy-start.4
  1.7 8.0 %copy-start.5 = (s32[4]{0:T(128)S(1)}, s32[4]{0:T(128)}, u32[]{:S(2)}) copy-start(s32[4]{0:T(128)} %probe_rows.3) | copy-start | bytes 52
  9.7 8.9 %copy-start = (bf16[2,4,2,3,3,2,8,128]{7,6,5,4,3,2,1,0:T(8,128)(2,1)S(1)}, bf16[2,4,2,3,3,2,8,128]{7,6,5,4,3,2,1,0:T(8,128)(2,1)}, u32[]{:S(2)}) copy-start(bf16[2,4,2,3,3,2,8,128]{7,6,5,4,3,2,1,0:T(8,128)(2,1)} %links.21) | copy-start | bytes 1769476
  10.5 10.8 %collective-permute-start = (f32[12,8,128]{2,1,0:T(8,128)S(1)}, f32[12,8,128]{2,1,0:T(8,128)S(1)}, u32[]{:S(2)}, u32[]{:S(2)}) collective-permute-start(f32[12,8,128]{2,1,0:T(8,128)S(1)} %get-tuple-element.56), channel_id=1, source_target_pairs={{0,95},{1,2},{2,1},{3,4},{4,3},{5,6},{6,5},{7,8},{8,7},{9,10},{10,... | collective-permute-start | bytes 147464 | tf_op jit(solution)/shard_map/ppermute | solution.py:668
  18.5 2.9 %collective-permute-start.1 = (f32[12,8,128]{2,1,0:T(8,128)S(1)}, f32[12,8,128]{2,1,0:T(8,128)S(1)}, u32[]{:S(2)}, u32[]{:S(2)}) collective-permute-start(f32[12,8,128]{2,1,0:T(8,128)S(1)} %get-tuple-element.57), channel_id=1, source_target_pairs={{0,1},{1,0},{2,3},{3,2},{4,5},{5,4},{6,7},{7,6},{8,9},{9,8},{10,11... | collective-permute-start | bytes 147464 | tf_op jit(solution)/shard_map/ppermute | solution.py:668
  18.7 10.5 %collective-permute-start.2 = (f32[36,8,128]{2,1,0:T(8,128)S(1)}, f32[36,8,128]{2,1,0:T(8,128)S(1)}, u32[]{:S(2)}, u32[]{:S(2)}) collective-permute-start(f32[36,8,128]{2,1,0:T(8,128)S(1)} %get-tuple-element.61), channel_id=1, source_target_pairs={{0,95},{1,2},{2,1},{3,4},{4,3},{5,6},{6,5},{7,8},{8,7},{9,10},{10,... | collective-permute-start | bytes 442376 | tf_op jit(solution)/shard_map/ppermute | solution.py:668
  19.6 9.6 %collective-permute-start.3 = (f32[36,8,128]{2,1,0:T(8,128)S(1)}, f32[36,8,128]{2,1,0:T(8,128)S(1)}, u32[]{:S(2)}, u32[]{:S(2)}) collective-permute-start(f32[36,8,128]{2,1,0:T(8,128)S(1)} %get-tuple-element.62), channel_id=1, source_target_pairs={{0,1},{1,0},{2,3},{3,2},{4,5},{5,4},{6,7},{7,6},{8,9},{9,8},{10,11... | collective-permute-start | bytes 442376 | tf_op jit(solution)/shard_map/ppermute | solution.py:668
  21.8 9.0 %collective-permute-start.4 = (f32[24,8,128]{2,1,0:T(8,128)S(1)}, f32[24,8,128]{2,1,0:T(8,128)S(1)}, u32[]{:S(2)}, u32[]{:S(2)}) collective-permute-start(f32[24,8,128]{2,1,0:T(8,128)S(1)} %get-tuple-element.59.sent_far), channel_id=1, source_target_pairs={{0,95},{1,2},{2,1},{3,4},{4,3},{5,6},{6,5},{7,8},{8,7},{9,10},{10,... | collective-permute-start | bytes 294920 | tf_op jit(solution)/shard_map/ppermute | solution.py:668
  27.4 1.8 %copy-start.2 = (bf16[2,2,6,6,2,8,128]{6,5,4,3,2,1,0:T(8,128)(2,1)S(1)}, bf16[2,2,6,6,2,8,128]{6,5,4,3,2,1,0:T(8,128)(2,1)}, u32[]{:S(2)}) copy-start(bf16[2,2,6,6,2,8,128]{6,5,4,3,2,1,0:T(8,128)(2,1)} %even.7) | copy-start | bytes 1769476
  27.7 3.8 %collective-permute-start.5 = (f32[24,8,128]{2,1,0:T(8,128)S(1)}, f32[24,8,128]{2,1,0:T(8,128)S(1)}, u32[]{:S(2)}, u32[]{:S(2)}) collective-permute-start(f32[24,8,128]{2,1,0:T(8,128)S(1)} %get-tuple-element.60.sent_near), channel_id=1, source_target_pairs={{0,1},{1,0},{2,3},{3,2},{4,5},{5,4},{6,7},{7,6},{8,9},{9,8},{10,11... | collective-permute-start | bytes 294920 | tf_op jit(solution)/shard_map/ppermute | solution.py:668
  32.5 9.0 %collective-permute-start.6 = (f32[24,8,128]{2,1,0:T(8,128)S(1)}, f32[24,8,128]{2,1,0:T(8,128)S(1)}, u32[]{:S(2)}, u32[]{:S(2)}) collective-permute-start(f32[24,8,128]{2,1,0:T(8,128)S(1)} %get-tuple-element.68.sent_far), channel_id=1, source_target_pairs={{0,95},{1,2},{2,1},{3,4},{4,3},{5,6},{6,5},{7,8},{8,7},{9,10},{10,... | collective-permute-start | bytes 294920 | tf_op jit(solution)/shard_map/ppermute | solution.py:668
  37.7 3.8 %collective-permute-start.7 = (f32[24,8,128]{2,1,0:T(8,128)S(1)}, f32[24,8,128]{2,1,0:T(8,128)S(1)}, u32[]{:S(2)}, u32[]{:S(2)}) collective-permute-start(f32[24,8,128]{2,1,0:T(8,128)S(1)} %get-tuple-element.69.sent_near), channel_id=1, source_target_pairs={{0,1},{1,0},{2,3},{3,2},{4,5},{5,4},{6,7},{7,6},{8,9},{9,8},{10,11... | collective-permute-start | bytes 294920 | tf_op jit(solution)/shard_map/ppermute | solution.py:668
  42.4 9.0 %collective-permute-start.8 = (f32[24,8,128]{2,1,0:T(8,128)S(1)}, f32[24,8,128]{2,1,0:T(8,128)S(1)}, u32[]{:S(2)}, u32[]{:S(2)}) collective-permute-start(f32[24,8,128]{2,1,0:T(8,128)S(1)} %get-tuple-element.75.sent_far), channel_id=1, source_target_pairs={{0,95},{1,2},{2,1},{3,4},{4,3},{5,6},{6,5},{7,8},{8,7},{9,10},{10,... | collective-permute-start | bytes 294920 | tf_op jit(solution)/shard_map/ppermute | solution.py:668
  47.6 3.8 %collective-permute-start.9 = (f32[24,8,128]{2,1,0:T(8,128)S(1)}, f32[24,8,128]{2,1,0:T(8,128)S(1)}, u32[]{:S(2)}, u32[]{:S(2)}) collective-permute-start(f32[24,8,128]{2,1,0:T(8,128)S(1)} %get-tuple-element.76.sent_near), channel_id=1, source_target_pairs={{0,1},{1,0},{2,3},{3,2},{4,5},{5,4},{6,7},{7,6},{8,9},{9,8},{10,11... | collective-permute-start | bytes 294920 | tf_op jit(solution)/shard_map/ppermute | solution.py:668
  52.3 13.2 %collective-permute-start.10 = (f32[24,8,128]{2,1,0:T(8,128)S(1)}, f32[24,8,128]{2,1,0:T(8,128)S(1)}, u32[]{:S(2)}, u32[]{:S(2)}) collective-permute-start(f32[24,8,128]{2,1,0:T(8,128)S(1)} %get-tuple-element.82.sent_far), channel_id=1, source_target_pairs={{0,95},{1,2},{2,1},{3,4},{4,3},{5,6},{6,5},{7,8},{8,7},{9,10},{10,... | collective-permute-start | bytes 294920 | tf_op jit(solution)/shard_map/ppermute | solution.py:668
  57.5 8.0 %collective-permute-start.11 = (f32[24,8,128]{2,1,0:T(8,128)S(1)}, f32[24,8,128]{2,1,0:T(8,128)S(1)}, u32[]{:S(2)}, u32[]{:S(2)}) collective-permute-start(f32[24,8,128]{2,1,0:T(8,128)S(1)} %get-tuple-element.83.sent_near), channel_id=1, source_target_pairs={{0,1},{1,0},{2,3},{3,2},{4,5},{5,4},{6,7},{7,6},{8,9},{9,8},{10,11... | collective-permute-start | bytes 294920 | tf_op jit(solution)/shard_map/ppermute | solution.py:668
  58.0 18.7 %collective-permute-start.12 = (f32[32,2,2,128]{3,2,1,0:T(2,128)S(1)}, f32[32,2,2,128]{3,2,1,0:T(2,128)S(1)}, u32[]{:S(2)}, u32[]{:S(2)}) collective-permute-start(f32[32,2,2,128]{3,2,1,0:T(2,128)S(1)} %get-tuple-element.95), channel_id=1, source_target_pairs={{0,32},{32,0},{64,96},{96,64},{1,33},{33,1},{65,97},{97,65},{2,34}... | collective-permute-start | bytes 196616 | tf_op jit(solution)/shard_map/ppermute | solution.py:674
  63.2 14.4 %collective-permute-start.13 = (f32[32,2,2,128]{3,2,1,0:T(2,128)S(1)}, f32[32,2,2,128]{3,2,1,0:T(2,128)S(1)}, u32[]{:S(2)}, u32[]{:S(2)}) collective-permute-start(f32[32,2,2,128]{3,2,1,0:T(2,128)S(1)} %get-tuple-element.96), channel_id=1, source_target_pairs={{0,64},{32,96},{64,0},{96,32},{1,65},{33,97},{65,1},{97,33},{2,66}... | collective-permute-start | bytes 196616 | tf_op jit(solution)/shard_map/ppermute | solution.py:674
  63.2 14.4 %collective-permute-start.14 = (f32[32,2,2,128]{3,2,1,0:T(2,128)S(1)}, f32[32,2,2,128]{3,2,1,0:T(2,128)S(1)}, u32[]{:S(2)}, u32[]{:S(2)}) collective-permute-start(f32[32,2,2,128]{3,2,1,0:T(2,128)S(1)} %get-tuple-element.97), channel_id=1, source_target_pairs={{0,96},{32,64},{64,32},{96,0},{1,97},{33,65},{65,33},{97,1},{2,98}... | collective-permute-start | bytes 196616 | tf_op jit(solution)/shard_map/ppermute | solution.py:674
  66.9 17.5 %all-to-all-start = ((f32[128,1,128]{2,1,0:T(1,128)}), f32[128,1,128]{2,1,0:T(1,128)S(1)}, u32[]{:S(2)}, u32[]{:S(2)}) async-start(f32[128,1,128]{2,1,0:T(1,128)} %bitcast.4), calls=%async_computation | async-start | bytes 131072 | tf_op jit(solution)/shard_map/all_to_all | solution.py:772
  74.8 2.9 %collective-permute-start.15 = (f32[8,2,2,128]{3,2,1,0:T(2,128)S(1)}, f32[8,2,2,128]{3,2,1,0:T(2,128)S(1)}, u32[]{:S(2)}, u32[]{:S(2)}) collective-permute-start(f32[8,2,2,128]{3,2,1,0:T(2,128)S(1)} %get-tuple-element.100), channel_id=1, source_target_pairs={{0,32},{32,0},{64,96},{96,64},{1,33},{33,1},{65,97},{97,65},{2,34}... | collective-permute-start | bytes 49160 | tf_op jit(solution)/shard_map/ppermute | solution.py:674
  75.9 2.9 %collective-permute-start.16 = (f32[8,2,2,128]{3,2,1,0:T(2,128)S(1)}, f32[8,2,2,128]{3,2,1,0:T(2,128)S(1)}, u32[]{:S(2)}, u32[]{:S(2)}) collective-permute-start(f32[8,2,2,128]{3,2,1,0:T(2,128)S(1)} %get-tuple-element.101), channel_id=1, source_target_pairs={{0,64},{32,96},{64,0},{96,32},{1,65},{33,97},{65,1},{97,33},{2,66}... | collective-permute-start | bytes 49160 | tf_op jit(solution)/shard_map/ppermute | solution.py:674
  76.6 3.5 %collective-permute-start.17 = (f32[8,2,2,128]{3,2,1,0:T(2,128)S(1)}, f32[8,2,2,128]{3,2,1,0:T(2,128)S(1)}, u32[]{:S(2)}, u32[]{:S(2)}) collective-permute-start(f32[8,2,2,128]{3,2,1,0:T(2,128)S(1)} %get-tuple-element.102), channel_id=1, source_target_pairs={{0,96},{32,64},{64,32},{96,0},{1,97},{33,65},{65,33},{97,1},{2,98}... | collective-permute-start | bytes 49160 | tf_op jit(solution)/shard_map/ppermute | solution.py:674

commit v6 on v5

--- a/solution.py
+++ b/solution.py
@@ -574,22 +574,25 @@
 
 
 def factors(table):
-    first_lane = lax.broadcasted_iota(jnp.int32, table.shape, 1) == 0
-    norm, crossed, about, rest, rest_first, image_rest, image_cross, image_norm = [
-        table if n == 0 else pltpu.roll(table, 128 - n, 1) for n in range(8)
-    ]
-    whole = lambda x: jnp.sum(
-        jnp.sum(jnp.where(first_lane, x, 0.0), axis=0, keepdims=True), axis=1, keepdims=True
-    )
-    norm_all, crossed_all = whole(norm), whole(crossed)
+    lane = lax.broadcasted_iota(jnp.int32, table.shape, 1)
+    of_lane = lax.broadcasted_iota(jnp.int32, (1, 128), 1)
+    total = lambda x: jnp.sum(x, axis=1, keepdims=True)
+    columns = jnp.sum(table, axis=0, keepdims=True)
+    norm_all = total(jnp.where(of_lane == 0, columns, 0.0))
+    crossed_all = total(jnp.where(of_lane == 1, columns, 0.0))
+    about = jnp.broadcast_to(table[:, 2:3], table.shape)
+
+    def around_shift(shift_by, square, cross, norm):
+        off = about - shift_by
+        weight = jnp.where(lane == square, 1.0, 0.0)
+        weight = jnp.where(lane == cross, 2.0 * off, weight)
+        weight = jnp.where(lane == norm, off * off, weight)
+        return total(jnp.sum(weight * table, axis=0, keepdims=True))
+
     alpha = norm_all / crossed_all
-    off = about - crossed_all / norm_all
-    norm_next = alpha * alpha * whole(rest + 2.0 * off * rest_first + off * off * norm)
+    norm_next = alpha * alpha * around_shift(crossed_all / norm_all, 3, 4, 0)
     beta = norm_next / norm_all
-    off = about - (1.0 + beta) / alpha
-    curved = alpha * alpha * whole(
-        image_rest + 2.0 * off * image_cross + off * off * image_norm
-    )
+    curved = alpha * alpha * around_shift((1.0 + beta) / alpha, 5, 6, 7)
     alpha_next = norm_next / curved
     return [
         jnp.broadcast_to(value, (2, 128))

time: 85.7 us -> 85.6 us (level)
  no operation moved by 1% of the time
where the time goes in v6:
time: 85.6 us; the launch traced here: 85.4 us
  starting transfers between devices  47.9 us (56%)
  waiting for transfers between devices  17.2 us (20%)
  Pallas kernels  10.4 us (12%)
  blocking collectives  7.97 us (9%)
  local copies, waits for them, and re-layouts  1.66 us (2%)
    ppermute x12, starting transfers between devices, swap(): return lax.ppermute(array, ('sub', 'lat'), pairs)  30.2 us
    ppermute x12, waiting for transfers between devices, swap(): return lax.ppermute(array, ('sub', 'lat'), pairs)  10.5 us
    pallas_call x21, Pallas kernels, call(): pl.pallas_call(kernel, out_shape=tuple((jax.ShapeDtypeStruct(s, F32) for...  10.4 us
    ppermute x6, starting transfers between devices, swap_depths(): lax.ppermute(traces[n], 'sub', [(i, i ^ n) for i in subs])  9.88 us
    all_gather x1, blocking collectives, whole(): gathered = lax.all_gather(own, 'sub')  7.97 us
    all_to_all x1, starting transfers between devices, whole(): sums = lax.all_to_all(sums, ('sub', 'lat'), 0, 0, tiled=True)  7.79 us
    all_to_all x1, waiting for transfers between devices, whole(): sums = lax.all_to_all(sums, ('sub', 'lat'), 0, 0, tiled=True)  4.25 us
    ppermute x6, waiting for transfers between devices, swap_depths(): lax.ppermute(traces[n], 'sub', [(i, i ^ n) for i in subs])  2.46 us
  transfers between devices with their start and end apart: 19, of which 9 were waited for; matrix products, arithmetic and copies ran while one was open for 0% of the time, Pallas kernels for 7%

profile of v6, /device:TPU:1, one launch (start us, length us, event | category | flops | bytes accessed | tf_op | source)
XLA Modules:
  0.0 85.4 jit_solution(15150597905447954127)
XLA Ops:
  0.0 1.0 %slice_bitcast_fusion.time_link = bf16[2,3,3,2,8,128]{5,4,3,2,1,0:T(8,128)(2,1)S(1)} fusion(bf16[2,4,2,3,3,2,8,128]{7,6,5,4,3,2,1,0:T(8,128)(2,1)} %links.21), kind=kLoop, calls=%fused_computation | loop fusion | bytes 147456 | tf_op jit(solution)/shard_map/squeeze | solution.py:695
  1.0 0.7 copy-done.4
  1.7 0.0 copy-start.5
  1.7 8.0 %all-gather = f32[200,2,2,128]{3,2,1,0:T(2,128)S(1)} all-gather(f32[50,2,2,128]{3,2,1,0:T(2,128)S(1)} %pack.1), channel_id=2, replica_groups=mesh['sub'=4,'lat'=32] {'sub'}, dimensions={0}, use_global_device_ids=true | all-gather | bytes 512000 | tf_op jit(solution)/shard_map/all_gather | solution.py:689
  9.7 0.0 copy-done.1
  9.7 0.8 start.1
  10.5 8.0 %collective-permute-start = (f32[12,8,128]{2,1,0:T(8,128)S(1)}, f32[12,8,128]{2,1,0:T(8,128)S(1)}, u32[]{:S(2)}, u32[]{:S(2)}) collective-permute-start(f32[12,8,128]{2,1,0:T(8,128)S(1)} %get-tuple-element.56), channel_id=1, source_target_pairs={{0,95},{1,2},{2,1},{3,4},{4,3},{5,6},{6,5},{7,8},{8,7},{9,10},{10,... | collective-permute-start | bytes 147464 | tf_op jit(solution)/shard_map/ppermute | solution.py:671
  18.5 0.0 collective-permute-start.1
  18.5 0.0 copy-done
  18.5 0.2 around.1
  18.7 0.9 %collective-permute-start.2 = (f32[36,8,128]{2,1,0:T(8,128)S(1)}, f32[36,8,128]{2,1,0:T(8,128)S(1)}, u32[]{:S(2)}, u32[]{:S(2)}) collective-permute-start(f32[36,8,128]{2,1,0:T(8,128)S(1)} %get-tuple-element.61), channel_id=1, source_target_pairs={{0,95},{1,2},{2,1},{3,4},{4,3},{5,6},{6,5},{7,8},{8,7},{9,10},{10,... | collective-permute-start | bytes 442376 | tf_op jit(solution)/shard_map/ppermute | solution.py:671
  19.6 0.8 collective-permute-start.3
  20.4 1.0 %own_rhs.1 = (f32[2,24,8,128]{3,2,1,0:T(8,128)S(1)}, f32[2,24,8,128]{3,2,1,0:T(8,128)S(1)}) custom-call(s32[4]{0:T(128)S(1)} %copy-done.5, f32[4,50,2,2,128]{4,3,2,1,0:T(2,128)S(1)} %bitcast.10, f32[2,24,8,128]{3,2,1,0:T(8,128)S(1)} %get-tuple-element.54.turned._, bf16[2,4,2,3,3,2,8,128]{7,6,5,4,3,2,1,0:T(8,128)(2,1)S(1)} %copy-done), custom_call_target="tpu_custom_call" | custom-call | tf_op jit(solution)/shard_map/own_rhs/pallas_call | solution.py:646
  21.3 0.0 collective-permute-done.got_far
  21.3 0.1 collective-permute-done.1.got_near
  21.5 0.3 rhs.1
  21.8 5.6 %collective-permute-start.4 = (f32[24,8,128]{2,1,0:T(8,128)S(1)}, f32[24,8,128]{2,1,0:T(8,128)S(1)}, u32[]{:S(2)}, u32[]{:S(2)}) collective-permute-start(f32[24,8,128]{2,1,0:T(8,128)S(1)} %get-tuple-element.59.sent_far), channel_id=1, source_target_pairs={{0,95},{1,2},{2,1},{3,4},{4,3},{5,6},{6,5},{7,8},{8,7},{9,10},{10,... | collective-permute-start | bytes 294920 | tf_op jit(solution)/shard_map/ppermute | solution.py:671
  27.4 0.3 near0.1
  27.7 0.1 collective-permute-start.5
  27.8 1.4 %collective-permute-done.2.around_far = f32[36,8,128]{2,1,0:T(8,128)S(1)} collective-permute-done((f32[36,8,128]{2,1,0:T(8,128)S(1)}, f32[36,8,128]{2,1,0:T(8,128)S(1)}, u32[]{:S(2)}, u32[]{:S(2)}) %collective-permute-start.2) | collective-permute-done | bytes 147488 | tf_op jit(solution)/shard_map/ppermute | solution.py:671
  29.2 0.0 collective-permute-done.3.around_near
  29.2 0.2 direct0.1
  29.5 1.4 %collective-permute-done.4.got_far = f32[24,8,128]{2,1,0:T(8,128)S(1)} collective-permute-done((f32[24,8,128]{2,1,0:T(8,128)S(1)}, f32[24,8,128]{2,1,0:T(8,128)S(1)}, u32[]{:S(2)}, u32[]{:S(2)}) %collective-permute-start.4) | collective-permute-done | bytes 98336 | tf_op jit(solution)/shard_map/ppermute | solution.py:671
  30.9 0.7 collective-permute-done.5.got_near
  31.6 0.9 %step0.1 = (f32[2,24,8,128]{3,2,1,0:T(8,128)S(1)}, f32[24,8,128]{2,1,0:T(8,128)S(1)}, f32[24,8,128]{2,1,0:T(8,128)S(1)}) custom-call(f32[2,24,8,128]{3,2,1,0:T(8,128)S(1)} %get-tuple-element.63.direct, f32[24,8,128]{2,1,0:T(8,128)S(1)} %get-tuple-element.64.back, f32[24,8,128]{2,1,0:T(8,128)S(1)} %get-tuple-element.65.odd_far, ...), custom_call_target="tpu_custom_call" | custom-call | tf_op jit(solution)/shard_map/step0/pallas_call | solution.py:646
  32.5 4.8 %collective-permute-start.6 = (f32[24,8,128]{2,1,0:T(8,128)S(1)}, f32[24,8,128]{2,1,0:T(8,128)S(1)}, u32[]{:S(2)}, u32[]{:S(2)}) collective-permute-start(f32[24,8,128]{2,1,0:T(8,128)S(1)} %get-tuple-element.68.sent_far), channel_id=1, source_target_pairs={{0,95},{1,2},{2,1},{3,4},{4,3},{5,6},{6,5},{7,8},{8,7},{9,10},{10,... | collective-permute-start | bytes 294920 | tf_op jit(solution)/shard_map/ppermute | solution.py:671
  37.3 0.3 near1.1
  37.7 0.1 collective-permute-start.7
  37.8 0.2 direct1.1
  38.0 3.4 %collective-permute-done.6.got_far = f32[24,8,128]{2,1,0:T(8,128)S(1)} collective-permute-done((f32[24,8,128]{2,1,0:T(8,128)S(1)}, f32[24,8,128]{2,1,0:T(8,128)S(1)}, u32[]{:S(2)}, u32[]{:S(2)}) %collective-permute-start.6) | collective-permute-done | bytes 98336 | tf_op jit(solution)/shard_map/ppermute | solution.py:671
  41.5 0.0 collective-permute-done.7.got_near
  41.5 0.9 %step1.1 = (f32[2,24,8,128]{3,2,1,0:T(8,128)S(1)}, f32[24,8,128]{2,1,0:T(8,128)S(1)}, f32[24,8,128]{2,1,0:T(8,128)S(1)}, f32[2,24,8,128]{3,2,1,0:T(8,128)S(1)}) custom-call(f32[2,24,8,128]{3,2,1,0:T(8,128)S(1)} %get-tuple-element.70.direct, f32[24,8,128]{2,1,0:T(8,128)S(1)} %get-tuple-element.71.back, f32[24,8,128]{2,1,0:T(8,128)S(1)} %get-tuple-element.72.odd_far, ...), custom_call_target="tpu_custom_call" | custom-call | tf_op jit(solution)/shard_map/step1/pallas_call | solution.py:646
  42.4 4.9 %collective-permute-start.8 = (f32[24,8,128]{2,1,0:T(8,128)S(1)}, f32[24,8,128]{2,1,0:T(8,128)S(1)}, u32[]{:S(2)}, u32[]{:S(2)}) collective-permute-start(f32[24,8,128]{2,1,0:T(8,128)S(1)} %get-tuple-element.75.sent_far), channel_id=1, source_target_pairs={{0,95},{1,2},{2,1},{3,4},{4,3},{5,6},{6,5},{7,8},{8,7},{9,10},{10,... | collective-permute-start | bytes 294920 | tf_op jit(solution)/shard_map/ppermute | solution.py:671
  47.3 0.3 near2.1
  47.6 0.1 collective-permute-start.9
  47.7 0.2 direct2.1
  47.9 3.4 %collective-permute-done.8.got_far = f32[24,8,128]{2,1,0:T(8,128)S(1)} collective-permute-done((f32[24,8,128]{2,1,0:T(8,128)S(1)}, f32[24,8,128]{2,1,0:T(8,128)S(1)}, u32[]{:S(2)}, u32[]{:S(2)}) %collective-permute-start.8) | collective-permute-done | bytes 98336 | tf_op jit(solution)/shard_map/ppermute | solution.py:671
  51.3 0.0 collective-permute-done.9.got_near
  51.4 0.9 %step2.1 = (f32[2,24,8,128]{3,2,1,0:T(8,128)S(1)}, f32[24,8,128]{2,1,0:T(8,128)S(1)}, f32[24,8,128]{2,1,0:T(8,128)S(1)}) custom-call(f32[2,24,8,128]{3,2,1,0:T(8,128)S(1)} %get-tuple-element.77.direct, f32[24,8,128]{2,1,0:T(8,128)S(1)} %get-tuple-element.78.back, f32[24,8,128]{2,1,0:T(8,128)S(1)} %get-tuple-element.79.odd_far, ...), custom_call_target="tpu_custom_call" | custom-call | tf_op jit(solution)/shard_map/step2/pallas_call | solution.py:646
  52.3 4.9 %collective-permute-start.10 = (f32[24,8,128]{2,1,0:T(8,128)S(1)}, f32[24,8,128]{2,1,0:T(8,128)S(1)}, u32[]{:S(2)}, u32[]{:S(2)}) collective-permute-start(f32[24,8,128]{2,1,0:T(8,128)S(1)} %get-tuple-element.82.sent_far), channel_id=1, source_target_pairs={{0,95},{1,2},{2,1},{3,4},{4,3},{5,6},{6,5},{7,8},{8,7},{9,10},{10,... | collective-permute-start | bytes 294920 | tf_op jit(solution)/shard_map/ppermute | solution.py:671
  57.2 0.3 near3.1
  57.5 0.1 collective-permute-start.11
  57.6 0.3 traces.1
  58.0 5.3 %collective-permute-start.12 = (f32[32,2,2,128]{3,2,1,0:T(2,128)S(1)}, f32[32,2,2,128]{3,2,1,0:T(2,128)S(1)}, u32[]{:S(2)}, u32[]{:S(2)}) collective-permute-start(f32[32,2,2,128]{3,2,1,0:T(2,128)S(1)} %get-tuple-element.95), channel_id=1, source_target_pairs={{0,32},{32,0},{64,96},{96,64},{1,33},{33,1},{65,97},{97,65},{2,34}... | collective-permute-start | bytes 196616 | tf_op jit(solution)/shard_map/ppermute | solution.py:677
  63.2 0.0 collective-permute-start.13
  63.2 1.7 %collective-permute-start.14 = (f32[32,2,2,128]{3,2,1,0:T(2,128)S(1)}, f32[32,2,2,128]{3,2,1,0:T(2,128)S(1)}, u32[]{:S(2)}, u32[]{:S(2)}) collective-permute-start(f32[32,2,2,128]{3,2,1,0:T(2,128)S(1)} %get-tuple-element.97), channel_id=1, source_target_pairs={{0,96},{32,64},{64,32},{96,0},{1,97},{33,65},{65,33},{97,1},{2,98}... | collective-permute-start | bytes 196616 | tf_op jit(solution)/shard_map/ppermute | solution.py:677
  65.0 0.3 sums.1
  65.2 0.3 direct3.1
  65.5 0.0 collective-permute-done.10.got_far
  65.5 0.0 collective-permute-done.11.got_near
  65.5 1.4 %last.1 = (f32[2,24,8,128]{3,2,1,0:T(8,128)S(1)}, f32[128,128]{1,0:T(8,128)}) custom-call(f32[2,24,8,128]{3,2,1,0:T(8,128)S(1)} %get-tuple-element.84.direct, f32[24,8,128]{2,1,0:T(8,128)S(1)} %get-tuple-element.85.back, f32[24,8,128]{2,1,0:T(8,128)S(1)} %get-tuple-element.86.odd_far, f32[24,8,128]{2,1,0:T(8,128)S(1)} %get-tuple-element.87.odd_near, ...), custom_call_target="tpu_custom_call" | custom-call | tf_op jit(solution)/shard_map/last/pallas_call | solution.py:646
  66.9 7.8 %all-to-all-start = ((f32[128,1,128]{2,1,0:T(1,128)}), f32[128,1,128]{2,1,0:T(1,128)S(1)}, u32[]{:S(2)}, u32[]{:S(2)}) async-start(f32[128,1,128]{2,1,0:T(1,128)} %bitcast.4), calls=%async_computation | async-start | bytes 131072 | tf_op jit(solution)/shard_map/all_to_all | solution.py:775
  74.7 0.1 last_traces.1
  74.8 1.1 %collective-permute-start.15 = (f32[8,2,2,128]{3,2,1,0:T(2,128)S(1)}, f32[8,2,2,128]{3,2,1,0:T(2,128)S(1)}, u32[]{:S(2)}, u32[]{:S(2)}) collective-permute-start(f32[8,2,2,128]{3,2,1,0:T(2,128)S(1)} %get-tuple-element.100), channel_id=1, source_target_pairs={{0,32},{32,0},{64,96},{96,64},{1,33},{33,1},{65,97},{97,65},{2,34}... | collective-permute-start | bytes 49160 | tf_op jit(solution)/shard_map/ppermute | solution.py:677
  75.9 0.7 collective-permute-start.16
  76.6 0.0 collective-permute-done.12.refs_1_
  76.6 1.0 %collective-permute-start.17 = (f32[8,2,2,128]{3,2,1,0:T(2,128)S(1)}, f32[8,2,2,128]{3,2,1,0:T(2,128)S(1)}, u32[]{:S(2)}, u32[]{:S(2)}) collective-permute-start(f32[8,2,2,128]{3,2,1,0:T(2,128)S(1)} %get-tuple-element.102), channel_id=1, source_target_pairs={{0,96},{32,64},{64,32},{96,0},{1,97},{33,65},{65,33},{97,1},{2,98}... | collective-permute-start | bytes 49160 | tf_op jit(solution)/shard_map/ppermute | solution.py:677
  77.7 0.0 collective-permute-done.13.refs_2_
  77.7 0.0 collective-permute-done.14.refs_3_
  77.7 0.0 collective-permute-done.15.refs_5_
  77.7 1.2 %collective-permute-done.16.refs_6_ = f32[8,2,2,128]{3,2,1,0:T(2,128)S(1)} collective-permute-done((f32[8,2,2,128]{3,2,1,0:T(2,128)S(1)}, f32[8,2,2,128]{3,2,1,0:T(2,128)S(1)}, u32[]{:S(2)}, u32[]{:S(2)}) %collective-permute-start.16) | collective-permute-done | bytes 16416 | tf_op jit(solution)/shard_map/ppermute | solution.py:677
  78.9 1.3 %collective-permute-done.17.refs_7_ = f32[8,2,2,128]{3,2,1,0:T(2,128)S(1)} collective-permute-done((f32[8,2,2,128]{3,2,1,0:T(2,128)S(1)}, f32[8,2,2,128]{3,2,1,0:T(2,128)S(1)}, u32[]{:S(2)}, u32[]{:S(2)}) %collective-permute-start.17) | collective-permute-done | bytes 16416 | tf_op jit(solution)/shard_map/ppermute | solution.py:677
  80.1 4.2 %all-to-all-done = f32[128,1,128]{2,1,0:T(1,128)S(1)} async-done(((f32[128,1,128]{2,1,0:T(1,128)}), f32[128,1,128]{2,1,0:T(1,128)S(1)}, u32[]{:S(2)}, u32[]{:S(2)}) %all-to-all-start) | async-done | bytes 65568 | tf_op jit(solution)/shard_map/all_to_all | solution.py:775
  84.4 1.0 %final.1 = f32[16,2,2,128]{3,2,1,0:T(2,128)} custom-call(f32[128,128]{1,0:T(8,128)S(1)} %bitcast.11, f32[32,2,2,128]{3,2,1,0:T(2,128)S(1)} %get-tuple-element.94.refs_0_, f32[32,2,2,128]{3,2,1,0:T(2,128)S(1)} %collective-permute-done.12.refs_1_, f32[32,2,2,128]{3,2,1,0:T(2,128)S(1)} %collective-permute-done.13.refs_2_, ...), custom_call_target="tpu_custom_call" | custom-call | tf_op jit(solution)/shard_map/final/pallas_call | solution.py:646
  (9 shorter events, 0.0 us)
Async XLA Ops:
  0.0 1.0 %copy-start.3 = (f32[2,2,4,3,2,2,128]{6,5,4,3,2,1,0:T(2,128)S(1)}, f32[2,2,4,3,2,2,128]{6,5,4,3,2,1,0:T(2,128)}, u32[]{:S(2)}) copy-start(f32[2,2,4,3,2,2,128]{6,5,4,3,2,1,0:T(2,128)} %param.6) | copy-start | bytes 294916
  0.0 9.7 %copy-start.1 = (bf16[2,2,6,6,2,8,128]{6,5,4,3,2,1,0:T(8,128)(2,1)S(1)}, bf16[2,2,6,6,2,8,128]{6,5,4,3,2,1,0:T(8,128)(2,1)}, u32[]{:S(2)}) copy-start(bf16[2,2,6,6,2,8,128]{6,5,4,3,2,1,0:T(8,128)(2,1)} %odd_inverse.21) | copy-start | bytes 1769476
  1.0 0.7 copy-start.4
  1.7 8.0 %copy-start.5 = (s32[4]{0:T(128)S(1)}, s32[4]{0:T(128)}, u32[]{:S(2)}) copy-start(s32[4]{0:T(128)} %probe_rows.3) | copy-start | bytes 52
  9.7 8.9 %copy-start = (bf16[2,4,2,3,3,2,8,128]{7,6,5,4,3,2,1,0:T(8,128)(2,1)S(1)}, bf16[2,4,2,3,3,2,8,128]{7,6,5,4,3,2,1,0:T(8,128)(2,1)}, u32[]{:S(2)}) copy-start(bf16[2,4,2,3,3,2,8,128]{7,6,5,4,3,2,1,0:T(8,128)(2,1)} %links.21) | copy-start | bytes 1769476
  10.5 10.8 %collective-permute-start = (f32[12,8,128]{2,1,0:T(8,128)S(1)}, f32[12,8,128]{2,1,0:T(8,128)S(1)}, u32[]{:S(2)}, u32[]{:S(2)}) collective-permute-start(f32[12,8,128]{2,1,0:T(8,128)S(1)} %get-tuple-element.56), channel_id=1, source_target_pairs={{0,95},{1,2},{2,1},{3,4},{4,3},{5,6},{6,5},{7,8},{8,7},{9,10},{10,... | collective-permute-start | bytes 147464 | tf_op jit(solution)/shard_map/ppermute | solution.py:671
  18.5 2.9 %collective-permute-start.1 = (f32[12,8,128]{2,1,0:T(8,128)S(1)}, f32[12,8,128]{2,1,0:T(8,128)S(1)}, u32[]{:S(2)}, u32[]{:S(2)}) collective-permute-start(f32[12,8,128]{2,1,0:T(8,128)S(1)} %get-tuple-element.57), channel_id=1, source_target_pairs={{0,1},{1,0},{2,3},{3,2},{4,5},{5,4},{6,7},{7,6},{8,9},{9,8},{10,11... | collective-permute-start | bytes 147464 | tf_op jit(solution)/shard_map/ppermute | solution.py:671
  18.7 10.5 %collective-permute-start.2 = (f32[36,8,128]{2,1,0:T(8,128)S(1)}, f32[36,8,128]{2,1,0:T(8,128)S(1)}, u32[]{:S(2)}, u32[]{:S(2)}) collective-permute-start(f32[36,8,128]{2,1,0:T(8,128)S(1)} %get-tuple-element.61), channel_id=1, source_target_pairs={{0,95},{1,2},{2,1},{3,4},{4,3},{5,6},{6,5},{7,8},{8,7},{9,10},{10,... | collective-permute-start | bytes 442376 | tf_op jit(solution)/shard_map/ppermute | solution.py:671
  19.6 9.6 %collective-permute-start.3 = (f32[36,8,128]{2,1,0:T(8,128)S(1)}, f32[36,8,128]{2,1,0:T(8,128)S(1)}, u32[]{:S(2)}, u32[]{:S(2)}) collective-permute-start(f32[36,8,128]{2,1,0:T(8,128)S(1)} %get-tuple-element.62), channel_id=1, source_target_pairs={{0,1},{1,0},{2,3},{3,2},{4,5},{5,4},{6,7},{7,6},{8,9},{9,8},{10,11... | collective-permute-start | bytes 442376 | tf_op jit(solution)/shard_map/ppermute | solution.py:671
  21.8 9.0 %collective-permute-start.4 = (f32[24,8,128]{2,1,0:T(8,128)S(1)}, f32[24,8,128]{2,1,0:T(8,128)S(1)}, u32[]{:S(2)}, u32[]{:S(2)}) collective-permute-start(f32[24,8,128]{2,1,0:T(8,128)S(1)} %get-tuple-element.59.sent_far), channel_id=1, source_target_pairs={{0,95},{1,2},{2,1},{3,4},{4,3},{5,6},{6,5},{7,8},{8,7},{9,10},{10,... | collective-permute-start | bytes 294920 | tf_op jit(solution)/shard_map/ppermute | solution.py:671
  27.4 1.8 %copy-start.2 = (bf16[2,2,6,6,2,8,128]{6,5,4,3,2,1,0:T(8,128)(2,1)S(1)}, bf16[2,2,6,6,2,8,128]{6,5,4,3,2,1,0:T(8,128)(2,1)}, u32[]{:S(2)}) copy-start(bf16[2,2,6,6,2,8,128]{6,5,4,3,2,1,0:T(8,128)(2,1)} %even.7) | copy-start | bytes 1769476
  27.7 3.8 %collective-permute-start.5 = (f32[24,8,128]{2,1,0:T(8,128)S(1)}, f32[24,8,128]{2,1,0:T(8,128)S(1)}, u32[]{:S(2)}, u32[]{:S(2)}) collective-permute-start(f32[24,8,128]{2,1,0:T(8,128)S(1)} %get-tuple-element.60.sent_near), channel_id=1, source_target_pairs={{0,1},{1,0},{2,3},{3,2},{4,5},{5,4},{6,7},{7,6},{8,9},{9,8},{10,11... | collective-permute-start | bytes 294920 | tf_op jit(solution)/shard_map/ppermute | solution.py:671
  32.5 9.0 %collective-permute-start.6 = (f32[24,8,128]{2,1,0:T(8,128)S(1)}, f32[24,8,128]{2,1,0:T(8,128)S(1)}, u32[]{:S(2)}, u32[]{:S(2)}) collective-permute-start(f32[24,8,128]{2,1,0:T(8,128)S(1)} %get-tuple-element.68.sent_far), channel_id=1, source_target_pairs={{0,95},{1,2},{2,1},{3,4},{4,3},{5,6},{6,5},{7,8},{8,7},{9,10},{10,... | collective-permute-start | bytes 294920 | tf_op jit(solution)/shard_map/ppermute | solution.py:671
  37.7 3.8 %collective-permute-start.7 = (f32[24,8,128]{2,1,0:T(8,128)S(1)}, f32[24,8,128]{2,1,0:T(8,128)S(1)}, u32[]{:S(2)}, u32[]{:S(2)}) collective-permute-start(f32[24,8,128]{2,1,0:T(8,128)S(1)} %get-tuple-element.69.sent_near), channel_id=1, source_target_pairs={{0,1},{1,0},{2,3},{3,2},{4,5},{5,4},{6,7},{7,6},{8,9},{9,8},{10,11... | collective-permute-start | bytes 294920 | tf_op jit(solution)/shard_map/ppermute | solution.py:671
  42.4 9.0 %collective-permute-start.8 = (f32[24,8,128]{2,1,0:T(8,128)S(1)}, f32[24,8,128]{2,1,0:T(8,128)S(1)}, u32[]{:S(2)}, u32[]{:S(2)}) collective-permute-start(f32[24,8,128]{2,1,0:T(8,128)S(1)} %get-tuple-element.75.sent_far), channel_id=1, source_target_pairs={{0,95},{1,2},{2,1},{3,4},{4,3},{5,6},{6,5},{7,8},{8,7},{9,10},{10,... | collective-permute-start | bytes 294920 | tf_op jit(solution)/shard_map/ppermute | solution.py:671
  47.6 3.8 %collective-permute-start.9 = (f32[24,8,128]{2,1,0:T(8,128)S(1)}, f32[24,8,128]{2,1,0:T(8,128)S(1)}, u32[]{:S(2)}, u32[]{:S(2)}) collective-permute-start(f32[24,8,128]{2,1,0:T(8,128)S(1)} %get-tuple-element.76.sent_near), channel_id=1, source_target_pairs={{0,1},{1,0},{2,3},{3,2},{4,5},{5,4},{6,7},{7,6},{8,9},{9,8},{10,11... | collective-permute-start | bytes 294920 | tf_op jit(solution)/shard_map/ppermute | solution.py:671
  52.3 13.2 %collective-permute-start.10 = (f32[24,8,128]{2,1,0:T(8,128)S(1)}, f32[24,8,128]{2,1,0:T(8,128)S(1)}, u32[]{:S(2)}, u32[]{:S(2)}) collective-permute-start(f32[24,8,128]{2,1,0:T(8,128)S(1)} %get-tuple-element.82.sent_far), channel_id=1, source_target_pairs={{0,95},{1,2},{2,1},{3,4},{4,3},{5,6},{6,5},{7,8},{8,7},{9,10},{10,... | collective-permute-start | bytes 294920 | tf_op jit(solution)/shard_map/ppermute | solution.py:671
  57.5 8.0 %collective-permute-start.11 = (f32[24,8,128]{2,1,0:T(8,128)S(1)}, f32[24,8,128]{2,1,0:T(8,128)S(1)}, u32[]{:S(2)}, u32[]{:S(2)}) collective-permute-start(f32[24,8,128]{2,1,0:T(8,128)S(1)} %get-tuple-element.83.sent_near), channel_id=1, source_target_pairs={{0,1},{1,0},{2,3},{3,2},{4,5},{5,4},{6,7},{7,6},{8,9},{9,8},{10,11... | collective-permute-start | bytes 294920 | tf_op jit(solution)/shard_map/ppermute | solution.py:671
  58.0 18.7 %collective-permute-start.12 = (f32[32,2,2,128]{3,2,1,0:T(2,128)S(1)}, f32[32,2,2,128]{3,2,1,0:T(2,128)S(1)}, u32[]{:S(2)}, u32[]{:S(2)}) collective-permute-start(f32[32,2,2,128]{3,2,1,0:T(2,128)S(1)} %get-tuple-element.95), channel_id=1, source_target_pairs={{0,32},{32,0},{64,96},{96,64},{1,33},{33,1},{65,97},{97,65},{2,34}... | collective-permute-start | bytes 196616 | tf_op jit(solution)/shard_map/ppermute | solution.py:677
  63.2 14.4 %collective-permute-start.13 = (f32[32,2,2,128]{3,2,1,0:T(2,128)S(1)}, f32[32,2,2,128]{3,2,1,0:T(2,128)S(1)}, u32[]{:S(2)}, u32[]{:S(2)}) collective-permute-start(f32[32,2,2,128]{3,2,1,0:T(2,128)S(1)} %get-tuple-element.96), channel_id=1, source_target_pairs={{0,64},{32,96},{64,0},{96,32},{1,65},{33,97},{65,1},{97,33},{2,66}... | collective-permute-start | bytes 196616 | tf_op jit(solution)/shard_map/ppermute | solution.py:677
  63.2 14.4 %collective-permute-start.14 = (f32[32,2,2,128]{3,2,1,0:T(2,128)S(1)}, f32[32,2,2,128]{3,2,1,0:T(2,128)S(1)}, u32[]{:S(2)}, u32[]{:S(2)}) collective-permute-start(f32[32,2,2,128]{3,2,1,0:T(2,128)S(1)} %get-tuple-element.97), channel_id=1, source_target_pairs={{0,96},{32,64},{64,32},{96,0},{1,97},{33,65},{65,33},{97,1},{2,98}... | collective-permute-start | bytes 196616 | tf_op jit(solution)/shard_map/ppermute | solution.py:677
  66.9 17.5 %all-to-all-start = ((f32[128,1,128]{2,1,0:T(1,128)}), f32[128,1,128]{2,1,0:T(1,128)S(1)}, u32[]{:S(2)}, u32[]{:S(2)}) async-start(f32[128,1,128]{2,1,0:T(1,128)} %bitcast.4), calls=%async_computation | async-start | bytes 131072 | tf_op jit(solution)/shard_map/all_to_all | solution.py:775
  74.8 2.9 %collective-permute-start.15 = (f32[8,2,2,128]{3,2,1,0:T(2,128)S(1)}, f32[8,2,2,128]{3,2,1,0:T(2,128)S(1)}, u32[]{:S(2)}, u32[]{:S(2)}) collective-permute-start(f32[8,2,2,128]{3,2,1,0:T(2,128)S(1)} %get-tuple-element.100), channel_id=1, source_target_pairs={{0,32},{32,0},{64,96},{96,64},{1,33},{33,1},{65,97},{97,65},{2,34}... | collective-permute-start | bytes 49160 | tf_op jit(solution)/shard_map/ppermute | solution.py:677
  75.9 2.9 %collective-permute-start.16 = (f32[8,2,2,128]{3,2,1,0:T(2,128)S(1)}, f32[8,2,2,128]{3,2,1,0:T(2,128)S(1)}, u32[]{:S(2)}, u32[]{:S(2)}) collective-permute-start(f32[8,2,2,128]{3,2,1,0:T(2,128)S(1)} %get-tuple-element.101), channel_id=1, source_target_pairs={{0,64},{32,96},{64,0},{96,32},{1,65},{33,97},{65,1},{97,33},{2,66}... | collective-permute-start | bytes 49160 | tf_op jit(solution)/shard_map/ppermute | solution.py:677
  76.6 3.5 %collective-permute-start.17 = (f32[8,2,2,128]{3,2,1,0:T(2,128)S(1)}, f32[8,2,2,128]{3,2,1,0:T(2,128)S(1)}, u32[]{:S(2)}, u32[]{:S(2)}) collective-permute-start(f32[8,2,2,128]{3,2,1,0:T(2,128)S(1)} %get-tuple-element.102), channel_id=1, source_target_pairs={{0,96},{32,64},{64,32},{96,0},{1,97},{33,65},{65,33},{97,1},{2,98}... | collective-permute-start | bytes 49160 | tf_op jit(solution)/shard_map/ppermute | solution.py:677
